TPU v7x, 32 devices: a whole 2x2x4 slice. The times are simulated.
32 devices in a mesh: leaf: 8 (over z, y), vec: 4 (over x, core).
Axes of the slice: x: 2, y: 2, z: 4, core: 2. Of those that a mesh axis runs over, the one named last changes fastest.
Arguments:
- values: bfloat16 [64, 65536], P('vec', 'leaf'), may hold values from -6 to 6
- coords: float32 [3, 65536], P(None, 'leaf'), may hold values from 0 to 16, as said below
- basis: bfloat16 [512, 64, 128], P(('leaf', 'vec')), may hold values from -0.5 to 0.5
- transfer: bfloat16 [1016, 4096], P('leaf'), may hold values from -0.625 to 0.625
- coupling: bfloat16 [24, 4096], replicated, may hold values from -0.15625 to 0.15625
- near_src: int32 [512, 27], P('leaf'), may hold values from -1 to 511, as said below
- far_src: int32 [1016, 24], P('leaf'), may hold values from -1 to 1015, as said below
- far_cls: int32 [1016, 24], P('leaf'), may hold values from 0 to 23
- top_src: int32 [12, 24], replicated, may hold values from -1 to 7, as said below
- top_cls: int32 [12, 24], replicated, may hold values from 0 to 23
Outputs:
- result: bfloat16 [64, 65536], P('vec', 'leaf')
Inputs may be any that keep to these rules, and one draw needn't show every extreme that they name: `coords`: leaf box t owns the unit cube with corner (t % 16, (t % 64) // 16, t // 64), and its points lie in that cube. `near_src`: slot 9 (c + 1) + 3 (b + 1) + (a + 1) of row t names the leaf box whose cube lies at offset (a, b, c) from the cube of t, for a, b, c in -1, 0, 1, or holds -1 where no such box exists or the pair is left out; slot 13 always holds t; the first leaf box of every subtree keeps every neighbour that exists. `far_src`: row p * 127 + s belongs to slot s of subtree p. At most 24 entries of a row are live, the rest are -1, and the row of the first leaf box of every subtree but the first has 24. A live entry p * 127 + s names slot s of subtree p: a node of the row's level, on the row's subtree or one beside it, two to 13 nodes away along that level. The rows of the roots are all -1. `top_src`: rows 0 to 7 belong to the roots and name roots; row 8 + q belongs to top node q and names top nodes. At most 24 entries of a row are live, -1 marks the rest, and a live entry lies two or more places from the row's own node.
All inputs are finite; a program needn't handle non-finite values.
Results may differ from a plain program's by a relative error of at most 0.02125.
Values may be sent and summed in bfloat16 or wider, within the bound.
No kernel may reach another device: no remote copies, remote signals or barrier semaphores. Data moves between devices by JAX's collectives and lax.ppermute only.
A program may use at most 64 MiB of HBM per device.

v0:
```python
import jax
import jax.numpy as jnp
from jax import lax
from jax.sharding import PartitionSpec as P

M = 128
K = 64
REACH = 13
TB = 127


kernel_spread = 0.2
kernel_amplitude = 0.3


def padded(block, sides, width):
    for axis, dim in sides:
        count = lax.axis_size(axis)
        forward = [(i, i + 1) for i in range(count - 1)]
        backward = [(target, source) for source, target in forward]
        low = lax.ppermute(
            lax.slice_in_dim(block, block.shape[dim] - width, None, axis=dim), axis, forward
        )
        high = lax.ppermute(lax.slice_in_dim(block, 0, width, axis=dim), axis, backward)
        block = jnp.concatenate([low, block, high], axis=dim)
    return block


def couple_terms(gathered, classes, live_mask, coupling, columns):
    class_count = coupling.shape[0]
    class_picks = (
        classes[:, :, None] == jnp.arange(class_count, dtype=jnp.int32)[None, None, :]
    ) & live_mask[:, :, None]
    grouped = jnp.einsum(
        "rsc,rsx->rcx",
        class_picks.astype(jnp.bfloat16),
        gathered,
        preferred_element_type=jnp.float32,
    ).astype(jnp.bfloat16)
    row_total = grouped.shape[0]
    grouped = grouped.reshape(row_total, class_count, columns, K)
    matrices = coupling.reshape(class_count, K, K)
    return jnp.einsum("ckl,rcnl->rnk", matrices, grouped, preferred_element_type=jnp.float32)


def per_device(
    values, coords, basis, transfer, coupling, near_src, far_src, far_cls, top_src, top_cls
):
    columns = values.shape[0]
    box_count = values.shape[1] // M
    width_coef = columns * K
    position = lax.axis_index("leaf")
    subtrees = lax.axis_size("leaf")
    stacked = jnp.concatenate([values.astype(jnp.float32), coords], axis=0)
    widened = padded(stacked, (("leaf", 1),), box_count * M)
    row_length = min(16, box_count)
    margin = row_length + 1
    widened = widened.reshape(columns + 3, 3 * box_count, M)
    widened = jnp.pad(widened, ((0, 0), (margin, margin), (0, 0)))
    near_flags = (near_src >= 0).astype(jnp.float32)
    target_points = coords.reshape(3, box_count, M)
    near_values = jnp.zeros((columns, box_count, M), jnp.float32)
    for slot in range(27):
        step_a = slot % 3 - 1
        step_b = slot // 3 % 3 - 1
        step_c = slot // 9 - 1
        start = margin + box_count + step_a + step_b * row_length + step_c * box_count
        pulled = widened[:, start : start + box_count]
        distance = jnp.zeros((box_count, M, M), jnp.float32)
        for axis_index in range(3):
            offset = (
                target_points[axis_index][:, :, None] - pulled[columns + axis_index][:, None, :]
            )
            distance = distance + offset * offset
        kernel = (
            kernel_amplitude
            * jnp.exp(-distance / kernel_spread)
            * near_flags[:, slot][:, None, None]
        ).astype(jnp.bfloat16)
        source_values = pulled[:columns].astype(jnp.bfloat16)
        near_values = near_values + jnp.einsum(
            "bij,nbj->nbi", kernel, source_values, preferred_element_type=jnp.float32
        )
    near_values = near_values.reshape(columns, box_count * M)
    value_boxes = values.reshape(columns, box_count, M)
    whole_basis = lax.all_gather(basis, "vec", axis=0, tiled=True)
    leaf_coef = jnp.einsum(
        "bkm,nbm->bnk", whole_basis, value_boxes, preferred_element_type=jnp.float32
    ).astype(jnp.bfloat16)
    levels = [leaf_coef]
    node_count = box_count
    while node_count > 1:
        matrices = transfer[node_count - 1 : 2 * node_count - 1].reshape(node_count, K, K)
        lifted = jnp.einsum(
            "ckl,cnl->cnk", matrices, levels[-1], preferred_element_type=jnp.float32
        )
        levels.append(
            lifted.reshape(node_count // 2, 2, columns, K).sum(axis=1).astype(jnp.bfloat16)
        )
        node_count = node_count // 2
    level_total = len(levels) - 1
    rim_widths = [min(box_count >> level_depth, REACH) for level_depth in range(level_total)]
    fields = []
    for level_depth in range(level_total):
        node_count = box_count >> level_depth
        flat_coef = levels[level_depth].reshape(node_count, width_coef)
        extended = padded(flat_coef, (("leaf", 0),), rim_widths[level_depth])
        gather_source_rows = far_src[node_count - 1 : 2 * node_count - 1]
        gather_live_mask = gather_source_rows >= 0
        safe_rows = jnp.where(gather_live_mask, gather_source_rows, 0)
        owner_index = safe_rows // TB
        slot_index = safe_rows % TB
        place_index = jnp.where(
            gather_live_mask,
            (owner_index - position) * node_count
            + slot_index
            - (node_count - 1)
            + rim_widths[level_depth],
            0,
        )
        gather_pulled = jnp.take(extended, place_index, axis=0)
        fields.append(
            couple_terms(
                gather_pulled,
                far_cls[node_count - 1 : 2 * node_count - 1],
                gather_live_mask,
                coupling,
                columns,
            )
        )
    root_coef = levels[-1]
    root_matrix = transfer[0].reshape(K, K)
    root_lift = jnp.einsum(
        "kl,nl->nk", root_matrix, root_coef[0], preferred_element_type=jnp.float32
    )
    roots_all, lifts_all = (
        lax.all_gather(root_coef.astype(jnp.float32), "leaf", axis=0, tiled=True),
        lax.all_gather(root_lift[None], "leaf", axis=0, tiled=True),
    )
    root_table = roots_all.reshape(subtrees, width_coef).astype(jnp.bfloat16)
    top_table = lifts_all.reshape(subtrees // 2, 2, width_coef).sum(axis=1).astype(jnp.bfloat16)

    def top_terms(row_index, coef_table):
        source_rows = lax.dynamic_slice_in_dim(top_src, row_index, 1, 0)
        classes = lax.dynamic_slice_in_dim(top_cls, row_index, 1, 0)
        live_mask = source_rows >= 0
        pulled = jnp.take(coef_table, jnp.where(live_mask, source_rows, 0), axis=0)
        return couple_terms(pulled, classes, live_mask, coupling, columns)

    top_down = top_terms(subtrees + position // 2, top_table).astype(jnp.bfloat16)
    root_field = top_terms(position, root_table)
    pushed_root = jnp.einsum(
        "kl,nk->nl", root_matrix, top_down[0], preferred_element_type=jnp.float32
    )
    down_coef = (root_field + pushed_root[None]).astype(jnp.bfloat16)
    for level_depth in reversed(range(level_total)):
        node_count = box_count >> level_depth
        matrices = transfer[node_count - 1 : 2 * node_count - 1].reshape(node_count, K, K)
        pushed = jnp.einsum(
            "ckl,cnk->cnl",
            matrices,
            jnp.repeat(down_coef, 2, axis=0),
            preferred_element_type=jnp.float32,
        )
        down_coef = (fields[level_depth] + pushed).astype(jnp.bfloat16)
    far_values = jnp.einsum(
        "bkm,bnk->nbm", whole_basis, down_coef, preferred_element_type=jnp.float32
    ).reshape(columns, box_count * M)
    return (near_values + far_values).astype(jnp.bfloat16)


def solution(mesh):
    in_specs = (
        P("vec", "leaf"),
        P(None, "leaf"),
        P(("leaf", "vec"), None, None),
        P("leaf", None),
        P(),
        P("leaf", None),
        P("leaf", None),
        P("leaf", None),
        P(),
        P(),
    )
    out_specs = P("vec", "leaf")
    return jax.shard_map(
        per_device, mesh=mesh, in_specs=in_specs, out_specs=out_specs, check_vma=False
    )
```

profile of v0, /device:TPU:10, one launch (start us, length us, event | category | flops | bytes accessed | tf_op | source)
XLA Modules:
  0.0 429.5 jit_solution(11535582435205824122)
XLA Ops:
  7.6 1.9 pad_maximum_fusion.1
  9.5 3.4 collective-permute-start
  12.9 3.3 collective-permute-start.1
  22.2 1.5 slice_reduce_fusion
  39.6 1.3 copy.93
  46.1 1.4 copy.90
  47.4 1.4 copy.89
  53.2 1.4 copy.86
  59.8 1.4 copy.82
  61.2 1.4 copy.81
  68.1 1.3 copy.75
  74.3 1.4 copy.70
  75.7 1.4 copy.68
  77.9 1.5 pad_maximum_fusion
  83.1 6.7 %fusion.46 = f32[16,64,128]{2,0,1:T(8,128)S(1)} fusion(f32[64]{0:T(128)S(1)} %get-tuple-element.126, f32[64,128]{1,0:T(8,128)S(1)} %get-tuple-element.63, f32[64,128]{1,0:T(8,128)S(1)} %get-tuple-element.64, f32[64,128]{1,0:T(8,128)S(1)} %get-tuple-element.65, f32[64,128]{1,0:T(8,128)S(1)} %bitcast.458, f32[64,128]{1,0:T(8,128)S(1)} %bitcast.485, ...), kind=kOutput, calls=%fused_computation.108 | convolution fusion | flops 46137344 | bytes 983552 | tf_op jit(solution)/shard_map/bij,nbj->nbi/dot_general | solution.py:81
  89.8 6.6 %fusion.45 = f32[16,64,128]{2,0,1:T(8,128)S(1)} fusion(f32[64]{0:T(128)S(1)} %get-tuple-element.125, f32[64,128]{1,0:T(8,128)S(1)} %get-tuple-element.60, f32[64,128]{1,0:T(8,128)S(1)} %get-tuple-element.61, f32[64,128]{1,0:T(8,128)S(1)} %get-tuple-element.62, f32[64,128]{1,0:T(8,128)S(1)} %bitcast.459, f32[64,128]{1,0:T(8,128)S(1)} %bitcast.486, ...), kind=kOutput, calls=%fused_computation.107 | convolution fusion | flops 46137344 | bytes 983552 | tf_op jit(solution)/shard_map/bij,nbj->nbi/dot_general | solution.py:81
  96.4 6.6 %fusion.44 = f32[16,64,128]{2,0,1:T(8,128)S(1)} fusion(f32[64]{0:T(128)S(1)} %get-tuple-element.124, f32[64,128]{1,0:T(8,128)S(1)} %get-tuple-element.57, f32[64,128]{1,0:T(8,128)S(1)} %get-tuple-element.58, f32[64,128]{1,0:T(8,128)S(1)} %get-tuple-element.59, f32[64,128]{1,0:T(8,128)S(1)} %bitcast.460, f32[64,128]{1,0:T(8,128)S(1)} %bitcast.487, ...), kind=kOutput, calls=%fused_computation.106 | convolution fusion | flops 46137344 | bytes 983552 | tf_op jit(solution)/shard_map/bij,nbj->nbi/dot_general | solution.py:81
  103.0 6.6 %fusion.43 = f32[16,64,128]{2,0,1:T(8,128)S(1)} fusion(f32[64]{0:T(128)S(1)} %get-tuple-element.123, f32[64,128]{1,0:T(8,128)S(1)} %get-tuple-element.54, f32[64,128]{1,0:T(8,128)S(1)} %get-tuple-element.55, f32[64,128]{1,0:T(8,128)S(1)} %get-tuple-element.56, f32[64,128]{1,0:T(8,128)S(1)} %bitcast.461, f32[64,128]{1,0:T(8,128)S(1)} %bitcast.488, ...), kind=kOutput, calls=%fused_computation.105 | convolution fusion | flops 46137344 | bytes 983552 | tf_op jit(solution)/shard_map/bij,nbj->nbi/dot_general | solution.py:81
  109.5 6.6 %fusion.42 = f32[16,64,128]{2,0,1:T(8,128)S(1)} fusion(f32[64]{0:T(128)S(1)} %get-tuple-element.122, f32[64,128]{1,0:T(8,128)S(1)} %get-tuple-element.107, f32[64,128]{1,0:T(8,128)S(1)} %get-tuple-element.52, f32[64,128]{1,0:T(8,128)S(1)} %get-tuple-element.53, f32[64,128]{1,0:T(8,128)S(1)} %bitcast.462, f32[64,128]{1,0:T(8,128)S(1)} %bitcast.489, ...), kind=kOutput, calls=%fused_computation.104 | convolution fusion | flops 46137344 | bytes 983552 | tf_op jit(solution)/shard_map/bij,nbj->nbi/dot_general | solution.py:81
  116.1 6.6 %fusion.8 = f32[64,16,128]{2,1,0:T(8,128)S(1)} fusion(f32[64]{0:T(128)S(1)} %get-tuple-element.143, f32[64,128]{1,0:T(8,128)S(1)} %bitcast.428, f32[64,128]{1,0:T(8,128)S(1)} %bitcast.463, f32[64,128]{1,0:T(8,128)S(1)} %bitcast.427, f32[64,128]{1,0:T(8,128)S(1)} %bitcast.490, f32[64,128]{1,0:T(8,128)S(1)} %bitcast.430, f32[64,128]{1,0:T(8,128)S(1)} %bitcast.436, ...), kind=kOutput, calls=%fused_computation.67 | convolution fusion | flops 46137344 | bytes 983552 | tf_op jit(solution)/shard_map/bij,nbj->nbi/dot_general | solution.py:81
  122.6 6.6 %fusion.41 = f32[16,64,128]{2,0,1:T(8,128)S(1)} fusion(f32[64]{0:T(128)S(1)} %get-tuple-element.121, f32[64,128]{1,0:T(8,128)S(1)} %bitcast.426, f32[64,128]{1,0:T(8,128)S(1)} %bitcast.425, f32[64,128]{1,0:T(8,128)S(1)} %bitcast.424, f32[64,128]{1,0:T(8,128)S(1)} %bitcast.464, f32[64,128]{1,0:T(8,128)S(1)} %bitcast.491, f32[64,128]{1,0:T(8,128)S(1)} %bitcast.437, ...), kind=kOutput, calls=%fused_computation.103 | convolution fusion | flops 46137344 | bytes 983552 | tf_op jit(solution)/shard_map/bij,nbj->nbi/dot_general | solution.py:81
  129.2 6.6 %fusion.40 = f32[16,64,128]{2,0,1:T(8,128)S(1)} fusion(f32[64]{0:T(128)S(1)} %get-tuple-element.120, f32[64,128]{1,0:T(8,128)S(1)} %bitcast.423, f32[64,128]{1,0:T(8,128)S(1)} %bitcast.422, f32[64,128]{1,0:T(8,128)S(1)} %bitcast.421, f32[64,128]{1,0:T(8,128)S(1)} %bitcast.465, f32[64,128]{1,0:T(8,128)S(1)} %bitcast.492, f32[64,128]{1,0:T(8,128)S(1)} %bitcast.438, ...), kind=kOutput, calls=%fused_computation.102 | convolution fusion | flops 46137344 | bytes 983552 | tf_op jit(solution)/shard_map/bij,nbj->nbi/dot_general | solution.py:81
  135.8 6.6 %fusion.39 = f32[16,64,128]{2,0,1:T(8,128)S(1)} fusion(f32[64]{0:T(128)S(1)} %get-tuple-element.119, f32[64,128]{1,0:T(8,128)S(1)} %bitcast.429, f32[64,128]{1,0:T(8,128)S(1)} %bitcast.420, f32[64,128]{1,0:T(8,128)S(1)} %bitcast.419, f32[64,128]{1,0:T(8,128)S(1)} %bitcast.466, f32[64,128]{1,0:T(8,128)S(1)} %bitcast.493, f32[64,128]{1,0:T(8,128)S(1)} %bitcast.439, ...), kind=kOutput, calls=%fused_computation.101 | convolution fusion | flops 46137344 | bytes 983552 | tf_op jit(solution)/shard_map/bij,nbj->nbi/dot_general | solution.py:81
  142.3 6.6 %fusion.81 = f32[64,16,128]{2,1,0:T(8,128)S(1)} fusion(f32[64,16,128]{2,1,0:T(8,128)S(1)} %fusion.8, f32[64]{0:T(128)S(1)} %get-tuple-element.142, f32[64,128]{1,0:T(8,128)S(1)} %bitcast.418, f32[64,128]{1,0:T(8,128)S(1)} %bitcast.417, f32[64,128]{1,0:T(8,128)S(1)} %bitcast.416, f32[64,128]{1,0:T(8,128)S(1)} %bitcast.467, f32[64,128]{1,0:T(8,128)S(1)} %bitcast.494, ...), kind=kOutput, calls=%fused_computation.140 | convolution fusion | flops 46268416 | bytes 1507840 | tf_op jit(solution)/shard_map/bij,nbj->nbi/dot_general | solution.py:81
  148.9 6.6 %fusion.80 = f32[64,16,128]{2,1,0:T(8,128)S(1)} fusion(f32[64,16,128]{2,1,0:T(8,128)S(1)} %fusion.81, f32[64]{0:T(128)S(1)} %get-tuple-element.141, f32[64,128]{1,0:T(8,128)S(1)} %bitcast.415, f32[64,128]{1,0:T(8,128)S(1)} %bitcast.414, f32[64,128]{1,0:T(8,128)S(1)} %bitcast.413, f32[64,128]{1,0:T(8,128)S(1)} %bitcast.468, f32[64,128]{1,0:T(8,128)S(1)} %bitcast.495, ...), kind=kOutput, calls=%fused_computation.139 | convolution fusion | flops 46268416 | bytes 1507840 | tf_op jit(solution)/shard_map/bij,nbj->nbi/dot_general | solution.py:81
  155.5 6.6 %fusion.79 = f32[64,16,128]{2,1,0:T(8,128)S(1)} fusion(f32[64,16,128]{2,1,0:T(8,128)S(1)} %fusion.80, f32[64]{0:T(128)S(1)} %get-tuple-element.140, f32[64,128]{1,0:T(8,128)S(1)} %bitcast.412, f32[64,128]{1,0:T(8,128)S(1)} %bitcast.411, f32[64,128]{1,0:T(8,128)S(1)} %bitcast.410, f32[64,128]{1,0:T(8,128)S(1)} %bitcast.469, f32[64,128]{1,0:T(8,128)S(1)} %bitcast.496, ...), kind=kOutput, calls=%fused_computation.138 | convolution fusion | flops 46268416 | bytes 1507840 | tf_op jit(solution)/shard_map/bij,nbj->nbi/dot_general | solution.py:81
  162.1 6.6 %fusion.78 = f32[64,16,128]{2,1,0:T(8,128)S(1)} fusion(f32[64,16,128]{2,1,0:T(8,128)S(1)} %fusion.79, f32[64]{0:T(128)S(1)} %get-tuple-element.139, f32[64,128]{1,0:T(8,128)S(1)} %get-tuple-element.104, f32[64,128]{1,0:T(8,128)S(1)} %get-tuple-element.105, f32[64,128]{1,0:T(8,128)S(1)} %get-tuple-element.106, f32[64,128]{1,0:T(8,128)S(1)} %bitcast.470, ...), kind=kOutput, calls=%fused_computation.137 | convolution fusion | flops 46268416 | bytes 1507840 | tf_op jit(solution)/shard_map/bij,nbj->nbi/dot_general | solution.py:81
  168.7 6.6 %fusion.77 = f32[64,16,128]{2,1,0:T(8,128)S(1)} fusion(f32[64,16,128]{2,1,0:T(8,128)S(1)} %fusion.78, f32[64]{0:T(128)S(1)} %get-tuple-element.138, f32[64,128]{1,0:T(8,128)S(1)} %get-tuple-element.101, f32[64,128]{1,0:T(8,128)S(1)} %get-tuple-element.102, f32[64,128]{1,0:T(8,128)S(1)} %get-tuple-element.103, f32[64,128]{1,0:T(8,128)S(1)} %bitcast.471, ...), kind=kOutput, calls=%fused_computation.136 | convolution fusion | flops 46268416 | bytes 1507840 | tf_op jit(solution)/shard_map/bij,nbj->nbi/dot_general | solution.py:81
  175.3 6.6 %fusion.76 = f32[64,16,128]{2,1,0:T(8,128)S(1)} fusion(f32[64,16,128]{2,1,0:T(8,128)S(1)} %fusion.77, f32[64]{0:T(128)S(1)} %get-tuple-element.137, f32[64,128]{1,0:T(8,128)S(1)} %get-tuple-element.98, f32[64,128]{1,0:T(8,128)S(1)} %get-tuple-element.99, f32[64,128]{1,0:T(8,128)S(1)} %get-tuple-element.100, f32[64,128]{1,0:T(8,128)S(1)} %bitcast.472, ...), kind=kOutput, calls=%fused_computation.135 | convolution fusion | flops 46268416 | bytes 1507840 | tf_op jit(solution)/shard_map/bij,nbj->nbi/dot_general | solution.py:81
  181.9 6.6 %fusion.75 = f32[64,16,128]{2,1,0:T(8,128)S(1)} fusion(f32[64,16,128]{2,1,0:T(8,128)S(1)} %fusion.76, f32[64]{0:T(128)S(1)} %get-tuple-element.136, f32[64,128]{1,0:T(8,128)S(1)} %get-tuple-element.95, f32[64,128]{1,0:T(8,128)S(1)} %get-tuple-element.96, f32[64,128]{1,0:T(8,128)S(1)} %get-tuple-element.97, f32[64,128]{1,0:T(8,128)S(1)} %bitcast.473, ...), kind=kOutput, calls=%fused_computation.134 | convolution fusion | flops 46268416 | bytes 1507840 | tf_op jit(solution)/shard_map/bij,nbj->nbi/dot_general | solution.py:81
  188.5 6.6 %fusion.74 = f32[64,16,128]{2,1,0:T(8,128)S(1)} fusion(f32[64,16,128]{2,1,0:T(8,128)S(1)} %fusion.75, f32[64]{0:T(128)S(1)} %get-tuple-element.135, f32[64,128]{1,0:T(8,128)S(1)} %get-tuple-element.92, f32[64,128]{1,0:T(8,128)S(1)} %get-tuple-element.93, f32[64,128]{1,0:T(8,128)S(1)} %get-tuple-element.94, f32[64,128]{1,0:T(8,128)S(1)} %bitcast.474, ...), kind=kOutput, calls=%fused_computation.133 | convolution fusion | flops 46268416 | bytes 1507840 | tf_op jit(solution)/shard_map/bij,nbj->nbi/dot_general | solution.py:81
  195.0 6.6 %fusion.73 = f32[64,16,128]{2,1,0:T(8,128)S(1)} fusion(f32[64,16,128]{2,1,0:T(8,128)S(1)} %fusion.74, f32[64]{0:T(128)S(1)} %get-tuple-element.134, f32[64,128]{1,0:T(8,128)S(1)} %get-tuple-element.90, f32[64,128]{1,0:T(8,128)S(1)} %get-tuple-element.91, f32[64,128]{1,0:T(8,128)S(1)} %get-tuple-element.89, f32[64,128]{1,0:T(8,128)S(1)} %bitcast.475, ...), kind=kOutput, calls=%fused_computation.132 | convolution fusion | flops 46268416 | bytes 1507840 | tf_op jit(solution)/shard_map/bij,nbj->nbi/dot_general | solution.py:81
  201.6 6.6 %fusion.72 = f32[64,16,128]{2,1,0:T(8,128)S(1)} fusion(f32[64,16,128]{2,1,0:T(8,128)S(1)} %fusion.73, f32[64]{0:T(128)S(1)} %get-tuple-element.133, f32[64,128]{1,0:T(8,128)S(1)} %get-tuple-element.86, f32[64,128]{1,0:T(8,128)S(1)} %get-tuple-element.87, f32[64,128]{1,0:T(8,128)S(1)} %get-tuple-element.88, f32[64,128]{1,0:T(8,128)S(1)} %bitcast.476, ...), kind=kOutput, calls=%fused_computation.131 | convolution fusion | flops 46268416 | bytes 1507840 | tf_op jit(solution)/shard_map/bij,nbj->nbi/dot_general | solution.py:81
  208.2 6.6 %fusion.71 = f32[64,16,128]{2,1,0:T(8,128)S(1)} fusion(f32[64,16,128]{2,1,0:T(8,128)S(1)} %fusion.72, f32[64]{0:T(128)S(1)} %get-tuple-element.132, f32[64,128]{1,0:T(8,128)S(1)} %get-tuple-element.83, f32[64,128]{1,0:T(8,128)S(1)} %get-tuple-element.84, f32[64,128]{1,0:T(8,128)S(1)} %get-tuple-element.85, f32[64,128]{1,0:T(8,128)S(1)} %bitcast.477, ...), kind=kOutput, calls=%fused_computation.130 | convolution fusion | flops 46268416 | bytes 1507840 | tf_op jit(solution)/shard_map/bij,nbj->nbi/dot_general | solution.py:81
  214.8 6.6 %fusion.70 = f32[64,16,128]{2,1,0:T(8,128)S(1)} fusion(f32[64,16,128]{2,1,0:T(8,128)S(1)} %fusion.71, f32[64]{0:T(128)S(1)} %get-tuple-element.131, f32[64,128]{1,0:T(8,128)S(1)} %get-tuple-element.80, f32[64,128]{1,0:T(8,128)S(1)} %get-tuple-element.81, f32[64,128]{1,0:T(8,128)S(1)} %get-tuple-element.82, f32[64,128]{1,0:T(8,128)S(1)} %bitcast.478, ...), kind=kOutput, calls=%fused_computation.129 | convolution fusion | flops 46268416 | bytes 1507840 | tf_op jit(solution)/shard_map/bij,nbj->nbi/dot_general | solution.py:81
  221.4 6.6 %fusion.69 = f32[64,16,128]{2,1,0:T(8,128)S(1)} fusion(f32[64,16,128]{2,1,0:T(8,128)S(1)} %fusion.70, f32[64]{0:T(128)S(1)} %get-tuple-element.130, f32[64,128]{1,0:T(8,128)S(1)} %get-tuple-element.77, f32[64,128]{1,0:T(8,128)S(1)} %get-tuple-element.78, f32[64,128]{1,0:T(8,128)S(1)} %get-tuple-element.79, f32[64,128]{1,0:T(8,128)S(1)} %bitcast.479, ...), kind=kOutput, calls=%fused_computation.128 | convolution fusion | flops 46268416 | bytes 1507840 | tf_op jit(solution)/shard_map/bij,nbj->nbi/dot_general | solution.py:81
  228.0 6.6 %fusion.68 = f32[64,16,128]{2,1,0:T(8,128)S(1)} fusion(f32[64,16,128]{2,1,0:T(8,128)S(1)} %fusion.69, f32[64]{0:T(128)S(1)} %get-tuple-element.129, f32[64,128]{1,0:T(8,128)S(1)} %get-tuple-element.74, f32[64,128]{1,0:T(8,128)S(1)} %get-tuple-element.75, f32[64,128]{1,0:T(8,128)S(1)} %get-tuple-element.76, f32[64,128]{1,0:T(8,128)S(1)} %bitcast.480, ...), kind=kOutput, calls=%fused_computation.127 | convolution fusion | flops 46268416 | bytes 1507840 | tf_op jit(solution)/shard_map/bij,nbj->nbi/dot_general | solution.py:81
  234.6 6.6 %fusion.38 = f32[16,64,128]{2,0,1:T(8,128)S(1)} fusion(f32[64]{0:T(128)S(1)} %get-tuple-element.118, f32[64,128]{1,0:T(8,128)S(1)} %bitcast.409, f32[64,128]{1,0:T(8,128)S(1)} %bitcast.408, f32[64,128]{1,0:T(8,128)S(1)} %bitcast.407, f32[64,128]{1,0:T(8,128)S(1)} %bitcast.481, f32[64,128]{1,0:T(8,128)S(1)} %bitcast.508, f32[64,128]{1,0:T(8,128)S(1)} %bitcast.454, ...), kind=kOutput, calls=%fused_computation.100 | convolution fusion | flops 46137344 | bytes 983552 | tf_op jit(solution)/shard_map/bij,nbj->nbi/dot_general | solution.py:81
  241.1 6.6 %fusion.67 = f32[64,16,128]{2,1,0:T(8,128)S(1)} fusion(f32[64,16,128]{2,1,0:T(8,128)S(1)} %fusion.68, f32[64]{0:T(128)S(1)} %get-tuple-element.128, f32[64,128]{1,0:T(8,128)S(1)} %get-tuple-element.71, f32[64,128]{1,0:T(8,128)S(1)} %get-tuple-element.72, f32[64,128]{1,0:T(8,128)S(1)} %get-tuple-element.73, f32[64,128]{1,0:T(8,128)S(1)} %bitcast.482, ...), kind=kOutput, calls=%fused_computation.126 | convolution fusion | flops 46268416 | bytes 1507840 | tf_op jit(solution)/shard_map/bij,nbj->nbi/dot_general | solution.py:81
  247.7 6.6 %fusion.66 = f32[16,64,128]{2,0,1:T(8,128)S(1)} fusion(f32[64,16,128]{2,1,0:T(8,128)S(1)} %fusion.67, f32[64]{0:T(128)S(1)} %get-tuple-element.127, f32[64,128]{1,0:T(8,128)S(1)} %get-tuple-element.68, f32[64,128]{1,0:T(8,128)S(1)} %get-tuple-element.69, f32[64,128]{1,0:T(8,128)S(1)} %get-tuple-element.70, f32[64,128]{1,0:T(8,128)S(1)} %bitcast.483, ...), kind=kOutput, calls=%fused_computation.125 | convolution fusion | flops 46268416 | bytes 1507840 | tf_op jit(solution)/shard_map/bij,nbj->nbi/dot_general | solution.py:81
  254.3 5.7 %fusion.64 = f32[16,64,128]{2,0,1:T(8,128)} fusion(f32[16,64,128]{2,0,1:T(8,128)S(1)} %fusion.38, f32[16,64,128]{2,0,1:T(8,128)S(1)} %fusion.39, f32[16,64,128]{2,0,1:T(8,128)S(1)} %fusion.40, f32[16,64,128]{2,0,1:T(8,128)S(1)} %fusion.41, f32[16,64,128]{2,0,1:T(8,128)S(1)} %fusion.42, f32[16,64,128]{2,0,1:T(8,128)S(1)} %fusion.43, ...), kind=kOutput, calls=%fused_computation.123 | convolution fusion | flops 47448064 | bytes 6226432 | tf_op jit(solution)/shard_map/bij,nbj->nbi/dot_general | solution.py:81
  260.0 1.9 convolution_convert_fusion.3
  263.7 2.5 collective-permute-start.12
  266.2 4.2 collective-permute-start.13
  270.5 2.0 collective-permute-start.10
  272.6 4.7 %collective-permute-start.11 = (bf16[4,1024]{1,0:T(4,128)(2,1)S(1)}, bf16[4,1024]{1,0:T(4,128)(2,1)S(1)}, u32[]{:S(2)}, u32[]{:S(2)}) collective-permute-start(bf16[4,1024]{1,0:T(4,128)(2,1)S(1)} %convert_element_type.287), channel_id=1, source_target_pairs={{4,0},{8,4},{12,8},{16,12},{20,16},{24,20},{28,24},{5,1},{9,5},{13... | collective-permute-start | bytes 24584 | tf_op jit(solution)/shard_map/ppermute | solution.py:24
  278.7 27.9 %all-gather = bf16[128,64]{1,0:T(8,128)(2,1)S(1)} all-gather(bf16[16,64]{1,0:T(8,128)(2,1)S(1)} %fusion.93), channel_id=2, replica_groups=mesh['leaf'=8,'vec'=4] {'leaf'}, dimensions={0}, use_global_device_ids=true | all-gather | bytes 18432 | tf_op jit(solution)/shard_map/all_gather | solution.py:137
  308.0 30.5 %all-gather.1 = f32[128,64]{1,0:T(8,128)S(1)} all-gather(f32[16,64]{1,0:T(8,128)S(1)} %fusion.283), channel_id=3, replica_groups=mesh['leaf'=8,'vec'=4] {'leaf'}, dimensions={0}, use_global_device_ids=true | all-gather | bytes 36864 | tf_op jit(solution)/shard_map/all_gather | solution.py:138
  340.5 1.9 collective-permute-start.8
  344.9 4.8 %collective-permute-start.9 = (bf16[8,1024]{1,0:T(8,128)(2,1)S(1)}, bf16[8,1024]{1,0:T(8,128)(2,1)S(1)}, u32[]{:S(2)}, u32[]{:S(2)}) collective-permute-start(bf16[8,1024]{1,0:T(8,128)(2,1)S(1)} %convert_element_type.284), channel_id=1, source_target_pairs={{4,0},{8,4},{12,8},{16,12},{20,16},{24,20},{28,24},{5,1},{9,5},{13... | collective-permute-start | bytes 49160 | tf_op jit(solution)/shard_map/ppermute | solution.py:24
  349.7 2.1 collective-permute-start.6
  353.5 4.8 %collective-permute-start.7 = (bf16[13,1024]{1,0:T(8,128)(2,1)S(1)}, bf16[13,1024]{1,0:T(8,128)(2,1)S(1)}, u32[]{:S(2)}, u32[]{:S(2)}) collective-permute-start(bf16[13,1024]{1,0:T(8,128)(2,1)S(1)} %slice.932), channel_id=1, source_target_pairs={{4,0},{8,4},{12,8},{16,12},{20,16},{24,20},{28,24},{5,1},{9,5},{13... | collective-permute-start | bytes 79880 | tf_op jit(solution)/shard_map/ppermute | solution.py:24
  358.3 1.9 collective-permute-start.4
  362.1 4.8 %collective-permute-start.5 = (bf16[13,1024]{1,0:T(8,128)(2,1)S(1)}, bf16[13,1024]{1,0:T(8,128)(2,1)S(1)}, u32[]{:S(2)}, u32[]{:S(2)}) collective-permute-start(bf16[13,1024]{1,0:T(8,128)(2,1)S(1)} %slice.925), channel_id=1, source_target_pairs={{4,0},{8,4},{12,8},{16,12},{20,16},{24,20},{28,24},{5,1},{9,5},{13... | collective-permute-start | bytes 79880 | tf_op jit(solution)/shard_map/ppermute | solution.py:24
  366.9 1.9 collective-permute-start.2
  371.9 4.8 %collective-permute-start.3 = (bf16[13,1024]{1,0:T(8,128)(2,1)}, bf16[13,1024]{1,0:T(8,128)(2,1)}, u32[]{:S(2)}, u32[]{:S(2)}) collective-permute-start(bf16[13,1024]{1,0:T(8,128)(2,1)} %slice.918), channel_id=1, source_target_pairs={{4,0},{8,4},{12,8},{16,12},{20,16},{24,20},{28,24},{5,1},{9,5},{13... | collective-permute-start | bytes 79880 | tf_op jit(solution)/shard_map/ppermute | solution.py:24
  376.8 2.1 gather_fusion.2
  381.7 2.8 gather_fusion.1
  384.5 1.8 convolution_convert_fusion
  386.3 4.1 reshape.652
  395.9 5.8 %gather_fusion = bf16[1536,1024]{1,0:T(8,128)(2,1)} fusion(bf16[90,1024]{1,0:T(8,128)(2,1)S(1)} %pad_maximum_fusion.2, s32[2048]{0:T(1024)S(1)} %pad_clamp_fusion), kind=kCustom, calls=%fused_computation | custom fusion | bytes 6297600 | tf_op jit(solution)/shard_map/jit(_take)/gather | solution.py:121
  401.7 3.0 fusion.5
  404.7 6.3 %reshape.648 = bf16[64,24,16,64]{3,2,1,0:T(8,128)(2,1)} reshape(bf16[64,24,1024]{2,1,0:T(8,128)(2,1)S(1)} %fusion.5) | data formatting | bytes 6291456 | tf_op jit(solution)/shard_map/reshape | solution.py:41
  411.0 10.2 %fusion.83 = bf16[64,16,64]{2,0,1:T(8,128)(2,1)S(1)} fusion(bf16[24,64,64,1]{2,1,0,3:T(8,128)(2,1)S(1)} %reshape.761, bf16[64,24,16,64]{3,2,1,0:T(8,128)(2,1)} %reshape.648, f32[64,16,64]{2,1,0:T(8,128)} %fusion.284), kind=kOutput, calls=%fused_computation.142 | convolution fusion | flops 201457664 | bytes 3735552 | tf_op jit(solution)/shard_map/ckl,rcnl->rnk/dot_general | solution.py:43
  (234 shorter events, 76.8 us)
Async XLA Ops:
  6.5 24.9 %copy-start.7 = (f32[3,8192]{1,0:T(4,128)S(1)}, f32[3,8192]{1,0:T(4,128)}, u32[]{:S(2)}) copy-start(f32[3,8192]{1,0:T(4,128)} %param.11) | copy-start | bytes 294916
  6.5 17.1 %copy-start.8 = (bf16[24,4096]{1,0:T(8,128)(2,1)S(1)}, bf16[24,4096]{1,0:T(8,128)(2,1)}, u32[]{:S(2)}) copy-start(bf16[24,4096]{1,0:T(8,128)(2,1)} %param.14) | copy-start | bytes 589828
  6.5 17.9 %copy-start.12 = (s32[127,24]{0,1:T(8,128)S(1)}, s32[127,24]{0,1:T(8,128)}, u32[]{:S(2)}) copy-start(s32[127,24]{0,1:T(8,128)} %param.16) | copy-start | bytes 36580
  6.5 19.3 %copy-start.11 = (s32[127,24]{0,1:T(8,128)S(1)}, s32[127,24]{0,1:T(8,128)}, u32[]{:S(2)}) copy-start(s32[127,24]{0,1:T(8,128)} %param.17) | copy-start | bytes 36580
  6.5 253.5 %all-gather.4.cloned.1.call-start = ((), (), s32[]{:S(2)}) async-start(), calls=%async_computation | async-start | bytes 1310720 | tf_op jit(solution)/shard_map/all_gather | solution.py:86
  9.5 68.3 %collective-permute-start = (f32[19,8192]{1,0:T(8,128)}, f32[19,8192]{1,0:T(8,128)}, u32[]{:S(2)}, u32[]{:S(2)}) collective-permute-start(f32[19,8192]{1,0:T(8,128)} %pad_maximum_fusion.1), channel_id=1, source_target_pairs={{0,4},{4,8},{8,12},{12,16},{16,20},{20,24},{24,28},{1,5},{5,9},{9,... | collective-permute-start | bytes 1867784 | tf_op jit(solution)/shard_map/ppermute | solution.py:21
  12.9 64.9 %collective-permute-start.1 = (f32[19,8192]{1,0:T(8,128)}, f32[19,8192]{1,0:T(8,128)}, u32[]{:S(2)}, u32[]{:S(2)}) collective-permute-start(f32[19,8192]{1,0:T(8,128)} %pad_maximum_fusion.1), channel_id=1, source_target_pairs={{4,0},{8,4},{12,8},{16,12},{20,16},{24,20},{28,24},{5,1},{9,5},{13... | collective-permute-start | bytes 1867784 | tf_op jit(solution)/shard_map/ppermute | solution.py:24
  35.1 226.8 %copy-start = (bf16[64,64,64]{2,1,0:T(8,128)(2,1)}, bf16[64,64,64]{2,1,0:T(8,128)(2,1)S(1)}, u32[]{:S(2)}) copy-start(bf16[64,64,64]{2,1,0:T(8,128)(2,1)S(1)} %reshape.650) | copy-start | bytes 1572868
  35.7 226.9 %copy-start.2 = (bf16[32,64,64]{2,1,0:T(8,128)(2,1)}, bf16[32,64,64]{2,1,0:T(8,128)(2,1)S(1)}, u32[]{:S(2)}) copy-start(bf16[32,64,64]{2,1,0:T(8,128)(2,1)S(1)} %reshape.653) | copy-start | bytes 786436
  35.9 227.1 %copy-start.5 = (bf16[16,64,64]{2,1,0:T(8,128)(2,1)}, bf16[16,64,64]{2,1,0:T(8,128)(2,1)S(1)}, u32[]{:S(2)}) copy-start(bf16[16,64,64]{2,1,0:T(8,128)(2,1)S(1)} %reshape.656) | copy-start | bytes 393220
  81.6 1.4 copy-start.17
  81.7 1.4 copy-start.18
  81.7 1.4 copy-start.19
  254.3 5.7 %copy-start.6 = (bf16[16,8192]{1,0:T(8,128)(2,1)S(1)}, bf16[16,8192]{1,0:T(8,128)(2,1)}, u32[]{:S(2)}) copy-start(bf16[16,8192]{1,0:T(8,128)(2,1)} %param.10) | copy-start | bytes 786436
  260.0 47.5 %copy-start.35 = (pred[24]{0:T(512)(128)(4,1)S(1)}, pred[24]{0:T(512)(128)(4,1)}, u32[]{:S(2)}) copy-start(pred[24]{0:T(512)(128)(4,1)} %get-tuple-element.147) | copy-start | bytes 76
  260.0 47.5 %copy-start.36 = (pred[24]{0:T(512)(128)(4,1)S(1)}, pred[24]{0:T(512)(128)(4,1)}, u32[]{:S(2)}) copy-start(pred[24]{0:T(512)(128)(4,1)} %get-tuple-element.149) | copy-start | bytes 76
  260.0 47.5 %copy-start.37 = (s32[24]{0:T(128)S(1)}, s32[24]{0:T(128)}, u32[]{:S(2)}) copy-start(s32[24]{0:T(128)} %get-tuple-element.146) | copy-start | bytes 292
  262.6 90.1 %copy-start.30 = (s32[2,24]{1,0:T(2,128)S(1)}, s32[2,24]{1,0:T(2,128)}, u32[]{:S(2)}) copy-start(s32[2,24]{1,0:T(2,128)} %copy.90) | copy-start | bytes 580
  262.6 90.1 %copy-start.33 = (pred[2,24]{1,0:T(4,128)(4,1)S(1)}, pred[2,24]{1,0:T(4,128)(4,1)}, u32[]{:S(2)}) copy-start(pred[2,24]{1,0:T(4,128)(4,1)} %copy.91) | copy-start | bytes 148
  262.6 90.1 %copy-start.34 = (pred[2,24]{1,0:T(4,128)(4,1)S(1)}, pred[2,24]{1,0:T(4,128)(4,1)}, u32[]{:S(2)}) copy-start(pred[2,24]{1,0:T(4,128)(4,1)} %copy.92) | copy-start | bytes 148
  262.6 97.7 %copy-start.24 = (s32[1024]{0:T(1024)S(1)}, s32[1024]{0:T(1024)}, u32[]{:S(2)}) copy-start(s32[1024]{0:T(1024)} %pad_clamp_fusion.4) | copy-start | bytes 12292
  263.7 81.2 %collective-permute-start.12 = (bf16[2,1024]{1,0:T(2,128)(2,1)S(1)}, bf16[2,1024]{1,0:T(2,128)(2,1)S(1)}, u32[]{:S(2)}, u32[]{:S(2)}) collective-permute-start(bf16[2,1024]{1,0:T(2,128)(2,1)S(1)} %convert_element_type.290), channel_id=1, source_target_pairs={{0,4},{4,8},{8,12},{12,16},{16,20},{20,24},{24,28},{1,5},{5,9},{9,... | collective-permute-start | bytes 12296 | tf_op jit(solution)/shard_map/ppermute | solution.py:21
  266.2 83.5 %collective-permute-start.13 = (bf16[2,1024]{1,0:T(2,128)(2,1)S(1)}, bf16[2,1024]{1,0:T(2,128)(2,1)S(1)}, u32[]{:S(2)}, u32[]{:S(2)}) collective-permute-start(bf16[2,1024]{1,0:T(2,128)(2,1)S(1)} %convert_element_type.290), channel_id=1, source_target_pairs={{4,0},{8,4},{12,8},{16,12},{20,16},{24,20},{28,24},{5,1},{9,5},{13... | collective-permute-start | bytes 12296 | tf_op jit(solution)/shard_map/ppermute | solution.py:24
  270.5 82.9 %collective-permute-start.10 = (bf16[4,1024]{1,0:T(4,128)(2,1)S(1)}, bf16[4,1024]{1,0:T(4,128)(2,1)S(1)}, u32[]{:S(2)}, u32[]{:S(2)}) collective-permute-start(bf16[4,1024]{1,0:T(4,128)(2,1)S(1)} %convert_element_type.287), channel_id=1, source_target_pairs={{0,4},{4,8},{8,12},{12,16},{16,20},{20,24},{24,28},{1,5},{5,9},{9,... | collective-permute-start | bytes 24584 | tf_op jit(solution)/shard_map/ppermute | solution.py:21
  272.6 85.7 %collective-permute-start.11 = (bf16[4,1024]{1,0:T(4,128)(2,1)S(1)}, bf16[4,1024]{1,0:T(4,128)(2,1)S(1)}, u32[]{:S(2)}, u32[]{:S(2)}) collective-permute-start(bf16[4,1024]{1,0:T(4,128)(2,1)S(1)} %convert_element_type.287), channel_id=1, source_target_pairs={{4,0},{8,4},{12,8},{16,12},{20,16},{24,20},{28,24},{5,1},{9,5},{13... | collective-permute-start | bytes 24584 | tf_op jit(solution)/shard_map/ppermute | solution.py:24
  277.5 83.6 %copy-start.25 = (s32[4,24]{1,0:T(4,128)S(1)}, s32[4,24]{1,0:T(4,128)}, u32[]{:S(2)}) copy-start(s32[4,24]{1,0:T(4,128)} %copy.86) | copy-start | bytes 1156
  277.5 83.6 %copy-start.31 = (pred[4,24]{1,0:T(4,128)(4,1)S(1)}, pred[4,24]{1,0:T(4,128)(4,1)}, u32[]{:S(2)}) copy-start(pred[4,24]{1,0:T(4,128)(4,1)} %copy.87) | copy-start | bytes 292
  277.5 83.6 %copy-start.32 = (pred[4,24]{1,0:T(4,128)(4,1)S(1)}, pred[4,24]{1,0:T(4,128)(4,1)}, u32[]{:S(2)}) copy-start(pred[4,24]{1,0:T(4,128)(4,1)} %copy.88) | copy-start | bytes 292
  338.7 30.2 %copy-start.23 = (s32[1024]{0:T(1024)S(1)}, s32[1024]{0:T(1024)}, u32[]{:S(2)}) copy-start(s32[1024]{0:T(1024)} %pad_clamp_fusion.5) | copy-start | bytes 12292
  340.5 21.6 %collective-permute-start.8 = (bf16[8,1024]{1,0:T(8,128)(2,1)S(1)}, bf16[8,1024]{1,0:T(8,128)(2,1)S(1)}, u32[]{:S(2)}, u32[]{:S(2)}) collective-permute-start(bf16[8,1024]{1,0:T(8,128)(2,1)S(1)} %convert_element_type.284), channel_id=1, source_target_pairs={{0,4},{4,8},{8,12},{12,16},{16,20},{20,24},{24,28},{1,5},{5,9},{9,... | collective-permute-start | bytes 49160 | tf_op jit(solution)/shard_map/ppermute | solution.py:21
  344.9 22.1 %collective-permute-start.9 = (bf16[8,1024]{1,0:T(8,128)(2,1)S(1)}, bf16[8,1024]{1,0:T(8,128)(2,1)S(1)}, u32[]{:S(2)}, u32[]{:S(2)}) collective-permute-start(bf16[8,1024]{1,0:T(8,128)(2,1)S(1)} %convert_element_type.284), channel_id=1, source_target_pairs={{4,0},{8,4},{12,8},{16,12},{20,16},{24,20},{28,24},{5,1},{9,5},{13... | collective-permute-start | bytes 49160 | tf_op jit(solution)/shard_map/ppermute | solution.py:24
  349.7 22.2 %collective-permute-start.6 = (bf16[13,1024]{1,0:T(8,128)(2,1)S(1)}, bf16[13,1024]{1,0:T(8,128)(2,1)S(1)}, u32[]{:S(2)}, u32[]{:S(2)}) collective-permute-start(bf16[13,1024]{1,0:T(8,128)(2,1)S(1)} %slice.930), channel_id=1, source_target_pairs={{0,4},{4,8},{8,12},{12,16},{16,20},{20,24},{24,28},{1,5},{5,9},{9,... | collective-permute-start | bytes 79880 | tf_op jit(solution)/shard_map/ppermute | solution.py:21
  352.9 17.0 %copy-start.22 = (s32[8,24]{1,0:T(8,128)S(1)}, s32[8,24]{1,0:T(8,128)}, u32[]{:S(2)}) copy-start(s32[8,24]{1,0:T(8,128)} %copy.82) | copy-start | bytes 2308
  352.9 17.0 %copy-start.28 = (pred[8,24]{1,0:T(8,128)(4,1)S(1)}, pred[8,24]{1,0:T(8,128)(4,1)}, u32[]{:S(2)}) copy-start(pred[8,24]{1,0:T(8,128)(4,1)} %copy.83) | copy-start | bytes 580
  352.9 17.0 %copy-start.29 = (pred[8,24]{1,0:T(8,128)(4,1)S(1)}, pred[8,24]{1,0:T(8,128)(4,1)}, u32[]{:S(2)}) copy-start(pred[8,24]{1,0:T(8,128)(4,1)} %copy.84) | copy-start | bytes 580
  353.5 23.3 %collective-permute-start.7 = (bf16[13,1024]{1,0:T(8,128)(2,1)S(1)}, bf16[13,1024]{1,0:T(8,128)(2,1)S(1)}, u32[]{:S(2)}, u32[]{:S(2)}) collective-permute-start(bf16[13,1024]{1,0:T(8,128)(2,1)S(1)} %slice.932), channel_id=1, source_target_pairs={{4,0},{8,4},{12,8},{16,12},{20,16},{24,20},{28,24},{5,1},{9,5},{13... | collective-permute-start | bytes 79880 | tf_op jit(solution)/shard_map/ppermute | solution.py:24
  358.3 23.3 %collective-permute-start.4 = (bf16[13,1024]{1,0:T(8,128)(2,1)S(1)}, bf16[13,1024]{1,0:T(8,128)(2,1)S(1)}, u32[]{:S(2)}, u32[]{:S(2)}) collective-permute-start(bf16[13,1024]{1,0:T(8,128)(2,1)S(1)} %slice.923), channel_id=1, source_target_pairs={{0,4},{4,8},{8,12},{12,16},{16,20},{20,24},{24,28},{1,5},{5,9},{9,... | collective-permute-start | bytes 79880 | tf_op jit(solution)/shard_map/ppermute | solution.py:21
  361.7 15.1 %copy-start.15 = (s32[1024]{0:T(1024)S(1)}, s32[1024]{0:T(1024)}, u32[]{:S(2)}) copy-start(s32[1024]{0:T(1024)} %pad_clamp_fusion.6) | copy-start | bytes 12292
  362.1 19.5 %collective-permute-start.5 = (bf16[13,1024]{1,0:T(8,128)(2,1)S(1)}, bf16[13,1024]{1,0:T(8,128)(2,1)S(1)}, u32[]{:S(2)}, u32[]{:S(2)}) collective-permute-start(bf16[13,1024]{1,0:T(8,128)(2,1)S(1)} %slice.925), channel_id=1, source_target_pairs={{4,0},{8,4},{12,8},{16,12},{20,16},{24,20},{28,24},{5,1},{9,5},{13... | collective-permute-start | bytes 79880 | tf_op jit(solution)/shard_map/ppermute | solution.py:24
  366.9 28.1 %collective-permute-start.2 = (bf16[13,1024]{1,0:T(8,128)(2,1)}, bf16[13,1024]{1,0:T(8,128)(2,1)}, u32[]{:S(2)}, u32[]{:S(2)}) collective-permute-start(bf16[13,1024]{1,0:T(8,128)(2,1)} %slice.916), channel_id=1, source_target_pairs={{0,4},{4,8},{8,12},{12,16},{16,20},{20,24},{24,28},{1,5},{5,9},{9,... | collective-permute-start | bytes 79880 | tf_op jit(solution)/shard_map/ppermute | solution.py:21
  370.8 8.1 %copy-start.16 = (s32[16,24]{1,0:T(8,128)S(1)}, s32[16,24]{1,0:T(8,128)}, u32[]{:S(2)}) copy-start(s32[16,24]{1,0:T(8,128)} %copy.78) | copy-start | bytes 4612
  370.8 8.1 %copy-start.26 = (pred[16,24]{1,0:T(8,128)(4,1)S(1)}, pred[16,24]{1,0:T(8,128)(4,1)}, u32[]{:S(2)}) copy-start(pred[16,24]{1,0:T(8,128)(4,1)} %copy.79) | copy-start | bytes 1156
  370.8 8.1 %copy-start.27 = (pred[16,24]{1,0:T(8,128)(4,1)S(1)}, pred[16,24]{1,0:T(8,128)(4,1)}, u32[]{:S(2)}) copy-start(pred[16,24]{1,0:T(8,128)(4,1)} %copy.80) | copy-start | bytes 1156
  371.9 23.1 %collective-permute-start.3 = (bf16[13,1024]{1,0:T(8,128)(2,1)}, bf16[13,1024]{1,0:T(8,128)(2,1)}, u32[]{:S(2)}, u32[]{:S(2)}) collective-permute-start(bf16[13,1024]{1,0:T(8,128)(2,1)} %slice.918), channel_id=1, source_target_pairs={{4,0},{8,4},{12,8},{16,12},{20,16},{24,20},{28,24},{5,1},{9,5},{13... | collective-permute-start | bytes 79880 | tf_op jit(solution)/shard_map/ppermute | solution.py:24
  378.9 2.7 copy-start.13
  381.6 2.9 copy-start.14
  381.6 2.9 copy-start.20
  381.7 2.9 copy-start.21
  390.5 3.0 copy-start.3
  390.5 3.3 copy-start.1
  390.5 4.5 %copy-start.9 = (bf16[64,1024]{1,0:T(8,128)(2,1)S(1)}, bf16[64,1024]{1,0:T(8,128)(2,1)}, u32[]{:S(2)}) copy-start(bf16[64,1024]{1,0:T(8,128)(2,1)} %reshape.647) | copy-start | bytes 393220
  410.9 10.2 %copy-start.4 = (bf16[64,64,128]{2,1,0:T(8,128)(2,1)S(1)}, bf16[64,64,128]{2,1,0:T(8,128)(2,1)}, u32[]{:S(2)}) copy-start(bf16[64,64,128]{2,1,0:T(8,128)(2,1)} %all-gather.4.cloned.1.call-done) | copy-start | bytes 3145732
  410.9 10.2 %copy-start.10 = (f32[16,64,128]{2,0,1:T(8,128)S(1)}, f32[16,64,128]{2,0,1:T(8,128)}, u32[]{:S(2)}) copy-start(f32[16,64,128]{2,0,1:T(8,128)} %fusion.64) | copy-start | bytes 1572868
Sparse Core Ops, SparseCore 0:
  16.4 16.9 all-gather.3
where the time goes:
time: 438 us; the launch traced here: 430 us
  matrix products  206 us (47%)
  local copies, waits for them, and re-layouts  84 us (19%)
  blocking collectives  58.5 us (13%)
  starting transfers between devices  47.4 us (11%)
  other arithmetic  19 us (4%)
  between operations  15 us (3%)
    dot_general x27, matrix products, per_device(): jnp.einsum('bij,nbj->nbi', kernel, source_values, preferred_element_type=...  177 us
    ppermute x7, starting transfers between devices, padded(): lax.ppermute(lax.slice_in_dim(block, 0, width, axis=dim), axis, backward)  31.5 us
    all_gather x1, blocking collectives, per_device(): lax.all_gather(root_lift[None], 'leaf', axis=0, tiled=True)  30.5 us
    all_gather x1, blocking collectives, per_device(): lax.all_gather(root_coef.astype(jnp.float32), 'leaf', axis=0, tiled=True)  27.9 us
    ppermute x7, starting transfers between devices, padded(): lax.ppermute(lax.slice_in_dim(block, block.shape[dim] - width, None, axis...  15.9 us
    dot_general x7, matrix products, couple_terms(): jnp.einsum('ckl,rcnl->rnk', matrices, grouped, preferred_element_type=jnp...  13.4 us
    gather x6, local copies, waits for them, and re-layouts, per_device(): gather_pulled = jnp.take(extended, place_index, axis=0)  13.3 us
    reshape x6, local copies, waits for them, and re-layouts, couple_terms(): grouped = grouped.reshape(row_total, class_count, columns, K)  12.3 us
  transfers between devices with their start and end apart: 15, of which 0 were waited for; matrix products, arithmetic and copies ran while one was open for 64% of the time, Pallas kernels for 0%

commit v1 on v0

v1 whole, which is shorter than its diff:
```python
import math

import jax
import jax.numpy as jnp
import numpy as np
from jax import lax
from jax.experimental import pallas as pl
from jax.experimental.pallas import tpu as pltpu
from jax.sharding import PartitionSpec as P

M = 128
K = 64
REACH = 13
TB = 127
ROW = 16
N = 16
B = 64
PAIRS = 64
RIM = 28

SCALE = math.log2(math.e) / 0.2
SHIFT = math.log2(0.3)
DEAD = -1000.0

NN = (((1,), (0,)), ((), ()))
NT = (((1,), (1,)), ((), ()))
TN = (((0,), (0,)), ((), ()))


def dot(a, b, dims=NN):
    return lax.dot_general(a, b, dims, preferred_element_type=jnp.float32)


def vmem():
    return pl.BlockSpec(memory_space=pltpu.VMEM)


def rounded(x):
    return lax.reduce_precision(x, 8, 7)


def near_kernel(near_ref, x_ref, low_ref, own_ref, high_ref, sel_ref, mask_ref, out_ref, yp_ref):
    layers = (low_ref, own_ref, high_ref)
    for l, src in enumerate(layers):

        def features(u, carry, l=l, src=src):
            first = pl.multiple_of(jnp.maximum(u - 1, 0) * M, M)
            second = pl.multiple_of(jnp.minimum(u, B - 1) * M, M)
            both = jnp.concatenate(
                [src[16:32, pl.ds(first, M)], src[16:32, pl.ds(second, M)]], axis=0
            )
            yp_ref[l, u] = dot(both, sel_ref[...], TN).astype(jnp.bfloat16)
            return carry

        lax.fori_loop(0, B + 1, features, 0, unroll=5)

    zero = jnp.zeros((64, M), jnp.bfloat16)

    def weights(t, a, b, c, slot):
        live = jnp.where(near_ref[t, slot] >= 0, 1, 0)
        return jnp.concatenate(
            [x_ref[t, a], x_ref[t, 3 + b], x_ref[t, 6 + c], mask_ref[live]], axis=0
        )

    for row in range(B // ROW):
        steps = [b for b in range(3) if 0 <= row + b - 1 < B // ROW]

        def pair(q, carry, row=row, steps=steps):
            t = row * ROW + 2 * q
            kernels, vectors = [], []
            for c in range(3):
                for b in steps:
                    for a in range(3):
                        slot = 9 * c + 3 * b + a
                        u = t + (b - 1) * ROW + a - 1
                        w = jnp.concatenate(
                            [
                                jnp.concatenate([weights(t, a, b, c, slot), zero], axis=1),
                                jnp.concatenate([zero, weights(t + 1, a, b, c, slot)], axis=1),
                            ],
                            axis=0,
                        )
                        e = dot(yp_ref[c, u + 1], w)
                        kernels.append(jnp.exp2(e).astype(jnp.bfloat16))
                        first = pl.multiple_of(jnp.maximum(u, 0) * M, M)
                        second = pl.multiple_of(jnp.minimum(u + 1, B - 1) * M, M)
                        src = layers[c]
                        vectors.append(
                            jnp.concatenate(
                                [src[0:16, pl.ds(first, M)], src[0:16, pl.ds(second, M)]], axis=0
                            )
                        )
            total = dot(jnp.concatenate(vectors, axis=1), jnp.concatenate(kernels, axis=0))
            here = pl.multiple_of(t * M, M)
            out_ref[:, pl.ds(here, M)] = total[0:16, 0:M]
            out_ref[:, pl.ds(here + M, M)] = total[16:32, M : 2 * M]
            return carry

        lax.fori_loop(0, ROW // 2, pair, 0)


def near_field(near_src, x_tiles, low, own, high):
    sel = np.zeros((32, 128), np.float32)
    for half in range(2):
        for k in range(3):
            for r, source in enumerate((2 * k, 2 * k + 1, 2 * k, 2 * k + 1, 9, 9, 9)):
                sel[16 * half + source, 64 * half + 16 * k + r] = 1
        for r, source in enumerate((9, 6, 7, 8)):
            sel[16 * half + source, 64 * half + 48 + r] = 1
    mask = np.zeros((2, 16, 128), np.float32)
    mask[:, 1:4] = 1
    mask[0, 0] = DEAD
    return pl.pallas_call(
        near_kernel,
        name="near_field",
        out_shape=jax.ShapeDtypeStruct((N, B * M), jnp.float32),
        in_specs=[pl.BlockSpec(memory_space=pltpu.SMEM)] + [vmem()] * 6,
        out_specs=vmem(),
        scratch_shapes=[pltpu.VMEM((3, B + 1, M, M), jnp.bfloat16)],
        compiler_params=pltpu.CompilerParams(vmem_limit_bytes=40 << 20),
        cost_estimate=pl.CostEstimate(
            flops=20_000_000_000, bytes_accessed=5_000_000, transcendentals=28_000_000
        ),
    )(
        near_src,
        x_tiles,
        low,
        own,
        high,
        jnp.asarray(sel, jnp.bfloat16),
        jnp.asarray(mask, jnp.bfloat16),
    )


def counts_kernel(col_ref, cls_ref, a_ref):
    classes = a_ref.shape[0]
    width = a_ref.shape[2]
    slots = col_ref.shape[1]
    spread = slots * 8
    lane = lax.broadcasted_iota(jnp.int32, (slots, spread), 1)
    copies = (lane // 8 == lax.broadcasted_iota(jnp.int32, (slots, spread), 0)).astype(jnp.float32)
    columns = lax.broadcasted_iota(jnp.int32, (8, width), 1)
    match = (
        lax.broadcasted_iota(jnp.int32, (8, spread), 1) % 8
        == lax.broadcasted_iota(jnp.int32, (8, spread), 0)
    )

    def block(g, carry):
        halves = []
        for h in range(2):
            rows = pl.ds(pl.multiple_of(g * 16 + h * 8, 8), 8)
            col = col_ref[rows, :]
            wide = dot(cls_ref[rows, :].astype(jnp.float32), copies).astype(jnp.int32)
            wide = jnp.where(match, wide, -1)
            left = jnp.concatenate(
                [jnp.where(wide == c, 1.0, 0.0) for c in range(classes)], axis=0
            ).astype(jnp.bfloat16)
            right = jnp.concatenate(
                [jnp.where(col[:, e : e + 1] == columns, 1.0, 0.0) for e in range(slots)], axis=0
            ).astype(jnp.bfloat16)
            halves.append(dot(left, right))
        for c in range(classes):
            both = jnp.concatenate([half[8 * c : 8 * c + 8] for half in halves], axis=0)
            a_ref[c, pl.ds(pl.multiple_of(g * 16, 16), 16), :] = both.astype(jnp.bfloat16)
        return carry

    lax.fori_loop(0, 2 * PAIRS // 16, block, 0)


def class_counts(columns, classes, class_count, width):
    return pl.pallas_call(
        counts_kernel,
        name="class_counts",
        out_shape=jax.ShapeDtypeStruct((class_count, 2 * PAIRS, width), jnp.bfloat16),
        in_specs=[vmem()] * 2,
        out_specs=vmem(),
        compiler_params=pltpu.CompilerParams(vmem_limit_bytes=20 << 20),
        cost_estimate=pl.CostEstimate(
            flops=2_000_000_000, bytes_accessed=1_600_000, transcendentals=0
        ),
    )(columns, classes)


def up_kernel(values_ref, basis_ref, links_ref, first_ref, root_ref, out_ref, cs_ref):
    lower = lax.broadcasted_iota(jnp.int32, (N, 2 * K), 1) < K

    def keep(pair_index, tile):
        cs_ref[pl.ds(pair_index, N, stride=PAIRS), :] = tile
        return tile

    def lift(stacked, matrix):
        both = dot(stacked, matrix, NT)
        return jnp.where(lower, both[:N], both[N:]).astype(jnp.bfloat16)

    tiles = {}
    for i in range(B // 2):
        stacked = jnp.concatenate(
            [values_ref[:, 2 * i * M : (2 * i + 1) * M], values_ref[:, (2 * i + 1) * M : (2 * i + 2) * M]],
            axis=0,
        )
        tiles[B // 2 - 1 + i] = lift(stacked, basis_ref[i])
        keep(B // 2 - 1 + i, tiles[B // 2 - 1 + i].astype(jnp.float32))
    for j in reversed(range(B // 2 - 1)):
        stacked = jnp.concatenate([tiles[2 * j + 1], tiles[2 * j + 2]], axis=0)
        tiles[j] = lift(stacked, links_ref[j])
        keep(j, tiles[j].astype(jnp.float32))
    root = dot(tiles[0], first_ref[...], NT).astype(jnp.bfloat16)
    up = dot(root, root_ref[...], NT)
    last = jnp.concatenate([root.astype(jnp.float32), up], axis=1)
    keep(PAIRS - 1, last)
    for n in range(N):
        out_ref[n] = cs_ref[n * PAIRS : (n + 1) * PAIRS, :].astype(jnp.bfloat16)
    out_ref[N, 0:N, :] = last.astype(jnp.bfloat16)
    out_ref[N, N:PAIRS, :] = jnp.zeros((PAIRS - N, 2 * K), jnp.bfloat16)


def upward(values, basis, links, first, root):
    return pl.pallas_call(
        up_kernel,
        name="upward",
        out_shape=jax.ShapeDtypeStruct((N + 1, PAIRS, 2 * K), jnp.bfloat16),
        in_specs=[vmem()] * 5,
        out_specs=vmem(),
        scratch_shapes=[pltpu.VMEM((N * PAIRS, 2 * K), jnp.float32)],
        compiler_params=pltpu.CompilerParams(vmem_limit_bytes=20 << 20),
        cost_estimate=pl.CostEstimate(
            flops=300_000_000, bytes_accessed=3_000_000, transcendentals=0
        ),
    )(values, basis, links, first, root)


def down_kernel(
    place_ref,
    low_ref,
    own_ref,
    high_ref,
    tops_ref,
    a_ref,
    coupling_ref,
    links_ref,
    first_ref,
    root_ref,
    basis_ref,
    near_ref,
    out_ref,
    cf_ref,
    side_ref,
    call_ref,
    bd_ref,
    lhs_ref,
    fs_ref,
):
    classes = a_ref.shape[0]
    height = a_ref.shape[2] // 2
    subtrees = tops_ref.shape[0]
    lower = lax.broadcasted_iota(jnp.int32, (N, 2 * K), 1) < K

    used = PAIRS + 2 * RIM + subtrees
    for n in range(N):
        base = n * height
        cf_ref[base : base + PAIRS, :] = own_ref[0, n].astype(jnp.float32)
        side_ref[...] = low_ref[0, n].astype(jnp.float32)
        at = base + PAIRS
        for start, size in ((0, 7), (8, 7), (24, 7), (56, 7)):
            cf_ref[at : at + size, :] = side_ref[start : start + size, :]
            at += size
        side_ref[...] = high_ref[0, n].astype(jnp.float32)
        for start, size in ((0, 14), (15, 7), (31, 7)):
            cf_ref[at : at + size, :] = side_ref[start : start + size, :]
            at += size
        if used < height:
            cf_ref[base + used : base + height, :] = jnp.zeros((height - used, 2 * K), jnp.float32)
    for q in range(subtrees // 2):
        even = tops_ref[2 * q, 0].astype(jnp.float32)
        odd = tops_ref[2 * q + 1, 0].astype(jnp.float32)
        at = PAIRS + 2 * RIM + 2 * q
        cf_ref[pl.ds(at, N, stride=height), :] = jnp.where(lower, even, even + odd)
        cf_ref[pl.ds(at + 1, N, stride=height), :] = odd
    wide_lower = lax.broadcasted_iota(jnp.int32, (height, 2 * K), 1) < K
    for m in range(N // 2):
        one = cf_ref[2 * m * height : (2 * m + 1) * height, :]
        two = cf_ref[(2 * m + 1) * height : (2 * m + 2) * height, :]
        lanes = slice(m * 2 * K, (m + 1) * 2 * K)
        call_ref[0:height, lanes] = jnp.where(
            wide_lower, one, pltpu.roll(two, K, 1)
        ).astype(jnp.bfloat16)
        call_ref[height : 2 * height, lanes] = jnp.where(
            wide_lower, pltpu.roll(one, K, 1), two
        ).astype(jnp.bfloat16)

    def spread(c, carry):
        s = coupling_ref[c]
        z = jnp.zeros((K, K), jnp.bfloat16)
        at = pl.multiple_of(c * 4 * K, 4 * K)
        for block in range(4):
            place = (0, 2, 1, 3)[block]
            bd_ref[pl.ds(at + block * K, K), :] = jnp.concatenate(
                [s if place == i else z for i in range(4)], axis=1
            )
        return carry

    lax.fori_loop(0, classes, spread, 0)

    for c in range(classes):
        grouped = dot(a_ref[c], call_ref[...]).astype(jnp.bfloat16)
        for m in range(N // 2):
            for parity in range(2):
                lhs_ref[
                    m * PAIRS : (m + 1) * PAIRS,
                    (2 * c + parity) * 2 * K : (2 * c + parity + 1) * 2 * K,
                ] = grouped[parity * PAIRS : (parity + 1) * PAIRS, m * 2 * K : (m + 1) * 2 * K]
    for m in range(N // 2):
        field = dot(lhs_ref[m * PAIRS : (m + 1) * PAIRS, :], bd_ref[...])
        fs_ref[2 * m * PAIRS : (2 * m + 1) * PAIRS, :] = field[:, 0 : 2 * K]
        fs_ref[(2 * m + 1) * PAIRS : (2 * m + 2) * PAIRS, :] = field[:, 2 * K : 4 * K]

    def field_of(pair_index):
        return fs_ref[pl.ds(pair_index, N, stride=PAIRS), :]

    def push(tile, matrix):
        none = jnp.zeros_like(tile)
        stacked = jnp.concatenate(
            [jnp.where(lower, tile, none), jnp.where(lower, none, tile)], axis=0
        ).astype(jnp.bfloat16)
        return dot(stacked, matrix)

    last = field_of(PAIRS - 1)
    top = last[:, K : 2 * K].astype(jnp.bfloat16)
    root = (last[:, 0:K] + dot(top, root_ref[...])).astype(jnp.bfloat16)
    tiles = {0: field_of(0) + dot(root, first_ref[...])}
    for j in range(B // 2 - 1):
        both = push(tiles[j], links_ref[j])
        tiles[2 * j + 1] = field_of(2 * j + 1) + both[:N]
        tiles[2 * j + 2] = field_of(2 * j + 2) + both[N:]
    for i in range(B // 2):
        both = push(tiles[B // 2 - 1 + i], basis_ref[i])
        for h in range(2):
            lanes = slice((2 * i + h) * M, (2 * i + h + 1) * M)
            out_ref[:, lanes] = (near_ref[:, lanes] + both[h * N : (h + 1) * N]).astype(jnp.bfloat16)


def downward(place, gathered, counts, coupling, links, first, root, basis, near):
    subtrees = gathered.shape[0]
    classes = counts.shape[0]
    height = counts.shape[2] // 2
    block = (1, N + 1, PAIRS, 2 * K)

    def whole(x):
        return pl.BlockSpec(x.shape, lambda i, p: (0,) * x.ndim)

    grid_spec = pltpu.PrefetchScalarGridSpec(
        num_scalar_prefetch=1,
        grid=(1,),
        in_specs=[
            pl.BlockSpec(block, lambda i, p: (jnp.maximum(p[0] - 1, 0), 0, 0, 0)),
            pl.BlockSpec(block, lambda i, p: (p[0], 0, 0, 0)),
            pl.BlockSpec(block, lambda i, p: (jnp.minimum(p[0] + 1, subtrees - 1), 0, 0, 0)),
            pl.BlockSpec((subtrees, 1, N, 2 * K), lambda i, p: (0, N, 0, 0)),
        ]
        + [whole(x) for x in (counts, coupling, links, first, root, basis, near)],
        out_specs=pl.BlockSpec((N, B * M), lambda i, p: (0, 0)),
        scratch_shapes=[
            pltpu.VMEM((N * height, 2 * K), jnp.float32),
            pltpu.VMEM((PAIRS, 2 * K), jnp.float32),
            pltpu.VMEM((2 * height, N * K), jnp.bfloat16),
            pltpu.VMEM((classes * 4 * K, 4 * K), jnp.bfloat16),
            pltpu.VMEM((N // 2 * PAIRS, classes * 4 * K), jnp.bfloat16),
            pltpu.VMEM((N * PAIRS, 2 * K), jnp.float32),
        ],
    )
    return pl.pallas_call(
        down_kernel,
        name="downward",
        out_shape=jax.ShapeDtypeStruct((N, B * M), jnp.bfloat16),
        grid_spec=grid_spec,
        compiler_params=pltpu.CompilerParams(vmem_limit_bytes=48 << 20),
        cost_estimate=pl.CostEstimate(
            flops=4_000_000_000, bytes_accessed=6_000_000, transcendentals=0
        ),
    )(place, gathered, gathered, gathered, gathered, counts, coupling, links, first, root, basis, near)


def source_columns(far_src, top_src, position, subtrees, height):
    owner = far_src // TB
    slot = far_src % TB
    count = jnp.ones_like(slot)
    for bit in range(1, 7):
        count = jnp.where(slot + 1 >= 2**bit, 2**bit, count)
    first = (count - 2) // 2
    inside = (slot - (count - 1)) // 2
    pairs = count // 2
    width = jnp.minimum(pairs, 7)
    rim_first = jnp.where(count <= 16, first, jnp.where(count == 32, 14, 21))
    side = owner - position
    row = jnp.where(
        side == 0,
        first + inside,
        jnp.where(
            side < 0,
            PAIRS + rim_first + inside - (pairs - width),
            PAIRS + RIM + rim_first + inside,
        ),
    )
    column = jnp.where(far_src >= 0, row + ((slot - 1) % 2) * height, -1)
    base = PAIRS + 2 * RIM
    roots = lax.dynamic_slice_in_dim(top_src, position, 1, 0)
    tops = lax.dynamic_slice_in_dim(top_src, subtrees + position // 2, 1, 0)
    roots = jnp.where(roots >= 0, base + roots, -1)
    tops = jnp.where(tops >= 0, height + base + 2 * tops, -1)
    return by_parity(column, roots, tops)


def by_parity(rows, root, top):
    paired = rows[1:].reshape(PAIRS - 1, 2, rows.shape[1])
    return jnp.concatenate([paired[:, 0], root, paired[:, 1], top], axis=0)


def per_device(
    values, coords, basis, transfer, coupling, near_src, far_src, far_cls, top_src, top_cls
):
    position = lax.axis_index("leaf")
    subtrees = lax.axis_size("leaf")
    class_count = coupling.shape[0]
    height = -(-(PAIRS + 2 * RIM + subtrees) // 64) * 64

    whole_basis = lax.all_gather(basis, "vec", axis=0, tiled=True)

    box = jnp.arange(B, dtype=jnp.int32)
    centre = jnp.stack(
        [box % ROW, box // ROW, jnp.full((B,), 0, jnp.int32) + position]
    ).astype(jnp.float32) + 0.5
    local = coords.reshape(3, B, M) - centre[:, :, None]
    flat = coords - jnp.repeat(centre, M, axis=1)
    high = rounded(flat)
    rest = rounded(flat - high)
    held = high + rest
    size = -SCALE * (held[0] ** 2 + held[1] ** 2 + held[2] ** 2)
    size_a = rounded(size)
    size_b = rounded(size - size_a)
    size_c = size - size_a - size_b
    rows = []
    for k in range(3):
        rows += [high[k], rest[k]]
    rows += [size_a, size_b, size_c, jnp.ones_like(size)]
    rows += [jnp.zeros_like(size)] * 6
    packed = jnp.concatenate([values, jnp.stack(rows).astype(jnp.bfloat16)], axis=0)
    forward = [(i, i + 1) for i in range(subtrees - 1)]
    backward = [(i + 1, i) for i in range(subtrees - 1)]
    from_low = lax.ppermute(packed, "leaf", forward)
    from_high = lax.ppermute(packed, "leaf", backward)

    moved = (
        jnp.transpose(local, (1, 0, 2))[:, :, None, None, :]
        - jnp.arange(-1, 2, dtype=jnp.float32)[None, None, :, None, None]
    )
    row = jnp.arange(16, dtype=jnp.int32)[None, None, None, :, None]
    axis = jnp.arange(3, dtype=jnp.int32)[None, :, None, None, None]
    term = jnp.where(
        row < 4,
        2 * SCALE * moved,
        -SCALE * moved * moved + jnp.where(axis == 0, SHIFT, 0.0),
    )
    term_a = rounded(term)
    term_b = rounded(term - term_a)
    term_c = term - term_a - term_b
    x_tiles = jnp.where(
        (row < 2) | (row == 4),
        term_a,
        jnp.where((row < 4) | (row == 5), term_b, jnp.where(row == 6, term_c, 0.0)),
    )
    x_tiles = x_tiles.astype(jnp.bfloat16).reshape(B, 9, 16, M)

    matrices = transfer.reshape(TB, K, K)
    siblings = matrices[1:].reshape(TB // 2, 2, K, K).transpose(0, 2, 1, 3).reshape(TB // 2, K, 2 * K)
    first = siblings[0]
    links = siblings[1:].reshape(B // 2 - 1, 2 * K, 2 * K)
    root = matrices[0]
    coupling_t = jnp.transpose(coupling.reshape(class_count, K, K), (0, 2, 1))

    columns = source_columns(far_src, top_src, position, subtrees, height)
    classes = by_parity(
        far_cls,
        lax.dynamic_slice_in_dim(top_cls, position, 1, 0),
        lax.dynamic_slice_in_dim(top_cls, subtrees + position // 2, 1, 0),
    )
    counts = class_counts(columns, classes, class_count, 2 * height)

    basis_pairs = whole_basis.reshape(B // 2, 2 * K, M)
    coefs = upward(values, basis_pairs, links, first, root)
    gathered = lax.all_gather(coefs, "leaf", axis=0)
    near = near_field(near_src, x_tiles, from_low, packed, from_high)
    place = jnp.full((1,), 0, jnp.int32) + position
    return downward(
        place, gathered, counts, coupling_t, links, first, root, basis_pairs, near
    )


def solution(mesh):
    in_specs = (
        P("vec", "leaf"),
        P(None, "leaf"),
        P(("leaf", "vec"), None, None),
        P("leaf", None),
        P(),
        P("leaf", None),
        P("leaf", None),
        P("leaf", None),
        P(),
        P(),
    )
    out_specs = P("vec", "leaf")
    return jax.shard_map(
        per_device, mesh=mesh, in_specs=in_specs, out_specs=out_specs, check_vma=False
    )
```

time: 438 us -> 113 us (0.26)
  the two profiles are of different devices: /device:TPU:10 before, /device:TPU:0 now
where the time goes in v1:
time: 113 us
  Pallas kernels  54 us (48%)
  local copies, waits for them, and re-layouts  26.5 us (23%)
  between operations  13.8 us (12%)
  starting transfers between devices  7.03 us (6%)
  waiting for transfers between devices  6.98 us (6%)
  other arithmetic  4.23 us (4%)
    pallas_call x1, Pallas kernels, near_field(): pl.pallas_call(near_kernel, name='near_field', out_shape=jax.ShapeDtypeSt...  37.2 us
    pallas_call x1, Pallas kernels, downward(): pl.pallas_call(down_kernel, name='downward', out_shape=jax.ShapeDtypeStru...  11.6 us
    all_gather x1, waiting for transfers between devices, per_device(): gathered = lax.all_gather(coefs, 'leaf', axis=0)  6.24 us
    unnamed x31, local copies, waits for them, and re-layouts  6.18 us
    ppermute x1, starting transfers between devices, per_device(): from_low = lax.ppermute(packed, 'leaf', forward)  5.71 us
    reshape x2, local copies, waits for them, and re-layouts, per_device(): matrices[1:].reshape(TB // 2, 2, K, K).transpose(0, 2, 1, 3)  5.35 us
    reshape x1, local copies, waits for them, and re-layouts, per_device(): links = siblings[1:].reshape(B // 2 - 1, 2 * K, 2 * K)  3.8 us
    slice x1, local copies, waits for them, and re-layouts, per_device(): links = siblings[1:].reshape(B // 2 - 1, 2 * K, 2 * K)  3.1 us
  transfers between devices with their start and end apart: 4, of which 1 were waited for; matrix products, arithmetic and copies ran while one was open for 22% of the time, Pallas kernels for 38%

profile of v1, /device:TPU:0, one launch (start us, length us, event | category | flops | bytes accessed | tf_op | source)
XLA Modules:
  0.0 112.6 jit_solution(10785055070647786477)
XLA Ops:
  6.5 0.7 all-gather.4.cloned.1.call-update
  7.3 0.0 all-gather.6.cloned.1.call-start
  7.3 0.1 pad.2.clone
  7.4 0.1 fusion.25
  7.5 1.0 broadcast_bitcast_fusion
  8.5 1.0 reduce-precision_add_fusion
  9.5 0.1 fusion.7
  9.6 0.1 fusion.27
  9.7 0.1 fusion.28
  9.9 1.6 %concatenate.16.own_ref = bf16[32,8192]{1,0:T(8,128)(2,1)S(1)} concatenate(bf16[16,8192]{1,0:T(8,128)(2,1)} %values_ref.1, bf16[1,8192]{1,0:T(2,128)(2,1)S(1)} %get-tuple-element.19, bf16[1,8192]{1,0:T(2,128)(2,1)S(1)} %get-tuple-element.16, bf16[1,8192]{1,0:T(2,128)(2,1)S(1)} %get-tuple-element.18, bf16[1,8192]{1,0:T(2,128)(2,1)S(1)} %get-tuple-element.15, ...), dimensions={0} | concatenate | bytes 1048576 | tf_op jit(solution)/shard_map/concatenate | solution.py:446
  11.5 5.7 %collective-permute-start = (bf16[32,8192]{1,0:T(8,128)(2,1)S(1)}, bf16[32,8192]{1,0:T(8,128)(2,1)}, u32[]{:S(2)}, u32[]{:S(2)}) collective-permute-start(bf16[32,8192]{1,0:T(8,128)(2,1)S(1)} %concatenate.16.own_ref), channel_id=1, source_target_pairs={{0,4},{4,8},{8,12},{12,16},{16,20},{20,24},{24,28},{1,5},{5,9},{9,... | collective-permute-start | bytes 1572872 | tf_op jit(solution)/shard_map/ppermute | solution.py:449
  17.2 1.3 %collective-permute-start.1 = (bf16[32,8192]{1,0:T(8,128)(2,1)S(1)}, bf16[32,8192]{1,0:T(8,128)(2,1)}, u32[]{:S(2)}, u32[]{:S(2)}) collective-permute-start(bf16[32,8192]{1,0:T(8,128)(2,1)S(1)} %concatenate.16.own_ref), channel_id=1, source_target_pairs={{4,0},{8,4},{12,8},{16,12},{20,16},{24,20},{28,24},{5,1},{9,5},{13... | collective-permute-start | bytes 1572872 | tf_op jit(solution)/shard_map/ppermute | solution.py:450
  18.5 1.2 %slice.67 = bf16[126,4096]{1,0:T(8,128)(2,1)} slice(bf16[127,4096]{1,0:T(8,128)(2,1)S(1)} %copy-done.9), slice={[1:127], [0:4096]} | slice | bytes 2064384 | tf_op jit(solution)/shard_map/slice | solution.py:474
  19.7 3.2 %reshape.170 = bf16[63,2,64,64]{3,2,1,0:T(8,128)(2,1)S(1)} reshape(bf16[126,4096]{1,0:T(8,128)(2,1)} %slice.67) | data formatting | bytes 2064384 | tf_op jit(solution)/shard_map/reshape | solution.py:474
  23.0 2.1 %copy.76 = bf16[63,2,64,64]{3,1,2,0:T(2,128)(2,1)S(1)} copy(bf16[63,2,64,64]{3,2,1,0:T(8,128)(2,1)S(1)} %reshape.170) | data formatting | bytes 2064384 | tf_op jit(solution)/shard_map/reshape | solution.py:474
  25.1 0.0 copy-start.10
  25.1 3.1 %slice.86 = bf16[62,64,2,64]{3,2,1,0:T(2,128)(2,1)} slice(bf16[63,64,2,64]{3,2,1,0:T(2,128)(2,1)S(1)} %bitcast.38), slice={[1:63], [0:64], [0:2], [0:64]} | slice | bytes 2031616 | tf_op jit(solution)/shard_map/slice | solution.py:476
  28.3 0.8 constant_dynamic-slice_fusion.1
  29.1 0.1 copy.62
  29.1 0.1 copy.61
  29.2 0.1 add_select_fusion.5
  29.3 0.1 fusion.16
  29.4 0.1 copy.45
  29.5 0.1 fusion.30
  29.6 0.1 copy.46
  29.7 0.1 copy.48
  29.8 3.8 %reshape.171.links_ref = bf16[31,128,128]{2,1,0:T(8,128)(2,1)S(1)} reshape(bf16[62,64,2,64]{3,2,1,0:T(2,128)(2,1)} %slice.86) | data formatting | bytes 2031616 | tf_op jit(solution)/shard_map/reshape | solution.py:476
  33.6 0.0 copy-start.12
  33.6 0.1 squeeze.21.first_ref
  33.7 0.9 slice_reduce_fusion
  34.5 0.1 squeeze.22.root_ref
  34.7 1.2 %copy-done.1 = bf16[64,64,128]{2,1,0:T(8,128)(2,1)S(1)} copy-done((bf16[64,64,128]{2,1,0:T(8,128)(2,1)S(1)}, bf16[64,64,128]{2,1,0:T(8,128)(2,1)}, u32[]{:S(2)}) %copy-start.1) | copy-done | bytes 1048600
  35.9 2.6 %upward.1 = bf16[17,64,128]{2,1,0:T(8,128)(2,1)} custom-call(bf16[16,8192]{1,0:T(8,128)(2,1)S(1)} %copy-done, bf16[32,128,128]{2,1,0:T(8,128)(2,1)S(1)} %bitcast.35, bf16[31,128,128]{2,1,0:T(8,128)(2,1)S(1)} %reshape.171.links_ref, bf16[64,128]{1,0:T(8,128)(2,1)S(1)} %squeeze.21.first_ref, bf16[64,64]{1,0:T(8,128)(2,1)S(1)} %squeeze.22.root_ref), custom_call_target="tpu_custom_call" | custom-call | flops 300000000 | bytes 3000000 | tf_op jit(solution)/shard_map/upward/pallas_call | solution.py:218
  38.5 0.0 all-gather.6.cloned.1.call-update
  38.5 0.1 pad_add_fusion
  38.6 0.1 copy.55.col_ref
  38.7 0.1 copy.63
  38.8 0.1 copy.64
  38.9 0.1 slice.74
  39.0 0.1 copy.50
  39.1 0.1 fusion.29
  39.2 0.1 copy.51
  39.3 0.1 copy.53
  39.3 0.1 pad_add_fusion.1
  39.4 0.1 copy.56.cls_ref
  39.6 0.0 copy-start.11
  39.6 2.6 %class_counts.1.a_ref = bf16[24,128,256]{2,1,0:T(8,128)(2,1)S(1)} custom-call(s32[128,24]{1,0:T(8,128)S(1)} %copy.55.col_ref, s32[128,24]{1,0:T(8,128)S(1)} %copy.56.cls_ref), custom_call_target="tpu_custom_call" | custom-call | flops 2000000000 | bytes 1600000 | tf_op jit(solution)/shard_map/class_counts/pallas_call | solution.py:171
  42.2 1.1 %copy-done.5 = bf16[24,128,256]{2,1,0:T(8,128)(2,1)} copy-done((bf16[24,128,256]{2,1,0:T(8,128)(2,1)}, bf16[24,128,256]{2,1,0:T(8,128)(2,1)S(1)}, u32[]{:S(2)}) %copy-start.5) | copy-done | bytes 1572888
  43.4 0.1 add.165
  43.5 0.1 add.166
  43.5 0.1 sub.132
  43.6 0.1 fusion.3
  43.8 0.2 copy.58
  44.0 0.2 copy.59
  44.2 0.1 copy.60.near_ref
  44.3 1.3 %reshape.174 = bf16[24,64,64]{2,1,0:T(8,128)(2,1)S(1)} reshape(bf16[24,4096]{1,0:T(8,128)(2,1)} %param.16) | data formatting | bytes 393216 | tf_op jit(solution)/shard_map/reshape | solution.py:478
  45.6 0.2 copy.57
  45.8 1.5 %fusion.x_ref = bf16[64,9,16,128]{3,2,1,0:T(8,128)(2,1)S(1)} fusion(f32[64,9,128]{2,1,0:T(8,128)S(1)} %copy.59, f32[64,9,128]{2,1,0:T(8,128)S(1)} %copy.58, pred[16]{0:T(512)(128)(4,1)S(1)} %get-tuple-element.46, pred[16]{0:T(512)(128)(4,1)S(1)} %get-tuple-element.44, pred[16]{0:T(512)(128)(4,1)S(1)} %get-tuple-element.47, pred[16]{0:T(512)(128)(4,1)S(1)} %get-tuple-element.45), kind=kLoop, calls=%fused_computation.4 | loop fusion | flops 10616832 | bytes 2949184 | tf_op jit(solution)/shard_map/convert_element_type | solution.py:471
  47.4 37.2 %near_field.1.near_ref = f32[16,8192]{1,0:T(8,128)S(1)} custom-call(s32[64,27]{1,0:T(8,128)S(1)} %copy.60.near_ref, bf16[64,9,16,128]{3,2,1,0:T(8,128)(2,1)S(1)} %fusion.x_ref, bf16[32,8192]{1,0:T(8,128)(2,1)} %collective-permute-done.low_ref, bf16[32,8192]{1,0:T(8,128)(2,1)S(1)} %concatenate.16.own_ref, bf16[32,8192]{1,0:T(8,128)(2,1)} %collective-permute-done.1.high_ref, ...), custom_call_target="tpu_custom_call" | custom-call | flops 20000000000 | bytes 5000000 | tf_op jit(solution)/shard_map/near_field/pallas_call | solution.py:113
  84.5 0.9 copy-done.7
  85.5 6.2 %all-gather.6.cloned.1.call-done = bf16[136,64,128]{2,1,0:T(8,128)(2,1)} async-done(((bf16[17,64,128]{2,1,0:T(8,128)(2,1)}), bf16[136,64,128]{2,1,0:T(8,128)(2,1)}) %all-gather.6.cloned.1.call-update) | async-done | bytes 2228240 | tf_op jit(solution)/shard_map/all_gather | solution.py:490
  91.7 1.4 %copy-done.6 = bf16[24,128,256]{2,1,0:T(8,128)(2,1)S(1)} copy-done((bf16[24,128,256]{2,1,0:T(8,128)(2,1)S(1)}, bf16[24,128,256]{2,1,0:T(8,128)(2,1)}, u32[]{:S(2)}) %copy-start.6) | copy-done | bytes 1572888
  93.1 1.0 copy-done.8
  94.2 11.6 %downward.1 = bf16[16,8192]{1,0:T(8,128)(2,1)} custom-call(s32[1]{0:T(128)} %bitcast.place_ref, bf16[8,17,64,128]{3,2,1,0:T(8,128)(2,1)} %bitcast.45, bf16[8,17,64,128]{3,2,1,0:T(8,128)(2,1)} %bitcast.46, bf16[8,17,64,128]{3,2,1,0:T(8,128)(2,1)} %bitcast.47, bf16[8,17,64,128]{3,2,1,0:T(8,128)(2,1)} %bitcast.48, bf16[24,128,256]{2,1,0:T(8,128)(2,1)S(1)} %copy-done.6, ...), custom_call_target="tpu_custom_call" | custom-call | flops 4000000000 | bytes 6000000 | tf_op jit(solution)/shard_map/downward/pallas_call | solution.py:371
  (37 shorter events, 0.3 us)
Async XLA Ops:
  6.5 12.0 %copy-start.9 = (bf16[127,4096]{1,0:T(8,128)(2,1)S(1)}, bf16[127,4096]{1,0:T(8,128)(2,1)}, u32[]{:S(2)}) copy-start(bf16[127,4096]{1,0:T(8,128)(2,1)} %param.15) | copy-start | bytes 3121156
  6.5 28.1 %all-gather.4.cloned.1.call-start = ((), (), s32[]{:S(2)}) async-start(), calls=%async_computation | async-start | bytes 1310720 | tf_op jit(solution)/shard_map/all_gather | solution.py:426
  7.3 84.4 %all-gather.6.cloned.1.call-start = ((), (), s32[]{:S(2)}) async-start(), calls=%async_computation.1 | async-start | bytes 2506752 | tf_op jit(solution)/shard_map/all_gather | solution.py:490
  11.5 35.8 %collective-permute-start = (bf16[32,8192]{1,0:T(8,128)(2,1)S(1)}, bf16[32,8192]{1,0:T(8,128)(2,1)}, u32[]{:S(2)}, u32[]{:S(2)}) collective-permute-start(bf16[32,8192]{1,0:T(8,128)(2,1)S(1)} %concatenate.16.own_ref), channel_id=1, source_target_pairs={{0,4},{4,8},{8,12},{12,16},{16,20},{20,24},{24,28},{1,5},{5,9},{9,... | collective-permute-start | bytes 1572872 | tf_op jit(solution)/shard_map/ppermute | solution.py:449
  17.2 30.2 %collective-permute-start.1 = (bf16[32,8192]{1,0:T(8,128)(2,1)S(1)}, bf16[32,8192]{1,0:T(8,128)(2,1)}, u32[]{:S(2)}, u32[]{:S(2)}) collective-permute-start(bf16[32,8192]{1,0:T(8,128)(2,1)S(1)} %concatenate.16.own_ref), channel_id=1, source_target_pairs={{4,0},{8,4},{12,8},{16,12},{20,16},{24,20},{28,24},{5,1},{9,5},{13... | collective-permute-start | bytes 1572872 | tf_op jit(solution)/shard_map/ppermute | solution.py:450
  25.1 4.1 %copy-start.10 = (s32[127,24]{0,1:T(8,128)S(1)}, s32[127,24]{0,1:T(8,128)}, u32[]{:S(2)}) copy-start(s32[127,24]{0,1:T(8,128)} %param.18) | copy-start | bytes 36580
  28.2 6.4 %copy-start = (bf16[16,8192]{1,0:T(8,128)(2,1)S(1)}, bf16[16,8192]{1,0:T(8,128)(2,1)}, u32[]{:S(2)}) copy-start(bf16[16,8192]{1,0:T(8,128)(2,1)} %values_ref.1) | copy-start | bytes 786436
  33.6 5.3 %copy-start.12 = (s32[127,24]{0,1:T(8,128)S(1)}, s32[127,24]{0,1:T(8,128)}, u32[]{:S(2)}) copy-start(s32[127,24]{0,1:T(8,128)} %param.19) | copy-start | bytes 36580
  34.6 1.2 %copy-start.1 = (bf16[64,64,128]{2,1,0:T(8,128)(2,1)S(1)}, bf16[64,64,128]{2,1,0:T(8,128)(2,1)}, u32[]{:S(2)}) copy-start(bf16[64,64,128]{2,1,0:T(8,128)(2,1)} %all-gather.4.cloned.1.call-done) | copy-start | bytes 3145732
  39.6 4.6 %copy-start.11 = (s32[64,27]{0,1:T(8,128)S(1)}, s32[64,27]{0,1:T(8,128)}, u32[]{:S(2)}) copy-start(s32[64,27]{0,1:T(8,128)} %param.17) | copy-start | bytes 20740
  42.2 1.1 %copy-start.5 = (bf16[24,128,256]{2,1,0:T(8,128)(2,1)}, bf16[24,128,256]{2,1,0:T(8,128)(2,1)S(1)}, u32[]{:S(2)}) copy-start(bf16[24,128,256]{2,1,0:T(8,128)(2,1)S(1)} %class_counts.1.a_ref) | copy-start | bytes 4718596
  44.2 3.1 %copy-start.3 = (bf16[32,128]{1,0:T(8,128)(2,1)S(1)}, bf16[32,128]{1,0:T(8,128)(2,1)}, u32[]{:S(2)}) copy-start(bf16[32,128]{1,0:T(8,128)(2,1)} %constant.171.clone.sel_ref) | copy-start | bytes 24580
  44.2 3.1 %copy-start.4 = (bf16[2,16,128]{2,1,0:T(8,128)(2,1)S(1)}, bf16[2,16,128]{2,1,0:T(8,128)(2,1)}, u32[]{:S(2)}) copy-start(bf16[2,16,128]{2,1,0:T(8,128)(2,1)} %constant.172.clone.mask_ref) | copy-start | bytes 24580
  47.3 44.4 %copy-start.2 = (bf16[64,64,128]{2,1,0:T(8,128)(2,1)S(1)}, bf16[64,64,128]{2,1,0:T(8,128)(2,1)}, u32[]{:S(2)}) copy-start(bf16[64,64,128]{2,1,0:T(8,128)(2,1)} %all-gather.4.cloned.1.call-done) | copy-start | bytes 3145732
  84.5 0.9 copy-start.7
  91.7 1.4 %copy-start.6 = (bf16[24,128,256]{2,1,0:T(8,128)(2,1)S(1)}, bf16[24,128,256]{2,1,0:T(8,128)(2,1)}, u32[]{:S(2)}) copy-start(bf16[24,128,256]{2,1,0:T(8,128)(2,1)} %copy-done.5) | copy-start | bytes 4718596
  93.1 1.0 copy-start.8
Sparse Core Ops, SparseCore 0:
  8.9 19.4 all-gather.3
  38.6 53.0 all-gather.5

commit v2 on v1

--- a/solution.py
+++ b/solution.py
@@ -19,7 +19,7 @@
 RIM = 28
 
 SCALE = math.log2(math.e) / 0.2
-SHIFT = math.log2(0.3)
+AMPLITUDE = 0.3
 DEAD = -1000.0
 
 NN = (((1,), (0,)), ((), ()))
@@ -81,7 +81,7 @@
                             axis=0,
                         )
                         e = dot(yp_ref[c, u + 1], w)
-                        kernels.append(jnp.exp2(e).astype(jnp.bfloat16))
+                        kernels.append(jnp.exp2(e.astype(jnp.bfloat16)))
                         first = pl.multiple_of(jnp.maximum(u, 0) * M, M)
                         second = pl.multiple_of(jnp.minimum(u + 1, B - 1) * M, M)
                         src = layers[c]
@@ -92,8 +92,8 @@
                         )
             total = dot(jnp.concatenate(vectors, axis=1), jnp.concatenate(kernels, axis=0))
             here = pl.multiple_of(t * M, M)
-            out_ref[:, pl.ds(here, M)] = total[0:16, 0:M]
-            out_ref[:, pl.ds(here + M, M)] = total[16:32, M : 2 * M]
+            out_ref[:, pl.ds(here, M)] = AMPLITUDE * total[0:16, 0:M]
+            out_ref[:, pl.ds(here + M, M)] = AMPLITUDE * total[16:32, M : 2 * M]
             return carry
 
         lax.fori_loop(0, ROW // 2, pair, 0)
@@ -181,12 +181,32 @@
     )(columns, classes)
 
 
-def up_kernel(values_ref, basis_ref, links_ref, first_ref, root_ref, out_ref, cs_ref):
+FIRST_ROWS = tuple(range(14)) + tuple(range(15, 22)) + tuple(range(31, 38))
+LAST_ROWS = tuple(range(7)) + tuple(range(8, 15)) + tuple(range(24, 31)) + tuple(range(56, 63))
+RIM_ROWS = 32
+
+
+def children_of(matrix_ref, slot):
+    return jnp.concatenate([matrix_ref[2 * slot + 1], matrix_ref[2 * slot + 2]], axis=1)
+
+
+def links_of(matrix_ref, pair_index):
+    return jnp.concatenate(
+        [children_of(matrix_ref, 2 * pair_index + 1), children_of(matrix_ref, 2 * pair_index + 2)],
+        axis=0,
+    )
+
+
+def up_kernel(
+    values_ref, basis_ref, matrix_ref, out_ref, first_ref, last_ref, root_ref, cs_ref, fs_ref, ls_ref
+):
     lower = lax.broadcasted_iota(jnp.int32, (N, 2 * K), 1) < K
 
     def keep(pair_index, tile):
         cs_ref[pl.ds(pair_index, N, stride=PAIRS), :] = tile
-        return tile
+        for rows, ref in ((FIRST_ROWS, fs_ref), (LAST_ROWS, ls_ref)):
+            if pair_index in rows:
+                ref[pl.ds(rows.index(pair_index), N, stride=RIM_ROWS), :] = tile
 
     def lift(stacked, matrix):
         both = dot(stacked, matrix, NT)
@@ -202,49 +222,57 @@
         keep(B // 2 - 1 + i, tiles[B // 2 - 1 + i].astype(jnp.float32))
     for j in reversed(range(B // 2 - 1)):
         stacked = jnp.concatenate([tiles[2 * j + 1], tiles[2 * j + 2]], axis=0)
-        tiles[j] = lift(stacked, links_ref[j])
+        tiles[j] = lift(stacked, links_of(matrix_ref, j))
         keep(j, tiles[j].astype(jnp.float32))
-    root = dot(tiles[0], first_ref[...], NT).astype(jnp.bfloat16)
-    up = dot(root, root_ref[...], NT)
+    root = dot(tiles[0], children_of(matrix_ref, 0), NT).astype(jnp.bfloat16)
+    up = dot(root, matrix_ref[0], NT)
     last = jnp.concatenate([root.astype(jnp.float32), up], axis=1)
     keep(PAIRS - 1, last)
+    root_ref[...] = last.astype(jnp.bfloat16)
     for n in range(N):
         out_ref[n] = cs_ref[n * PAIRS : (n + 1) * PAIRS, :].astype(jnp.bfloat16)
-    out_ref[N, 0:N, :] = last.astype(jnp.bfloat16)
-    out_ref[N, N:PAIRS, :] = jnp.zeros((PAIRS - N, 2 * K), jnp.bfloat16)
-
-
-def upward(values, basis, links, first, root):
+        for source, target in ((fs_ref, first_ref), (ls_ref, last_ref)):
+            base = n * RIM_ROWS
+            source[base + RIM : base + RIM_ROWS, :] = jnp.zeros((RIM_ROWS - RIM, 2 * K), jnp.float32)
+            target[n] = source[base : base + RIM_ROWS, :].astype(jnp.bfloat16)
+
+
+def upward(values, basis, matrices):
     return pl.pallas_call(
         up_kernel,
         name="upward",
-        out_shape=jax.ShapeDtypeStruct((N + 1, PAIRS, 2 * K), jnp.bfloat16),
-        in_specs=[vmem()] * 5,
-        out_specs=vmem(),
-        scratch_shapes=[pltpu.VMEM((N * PAIRS, 2 * K), jnp.float32)],
+        out_shape=[
+            jax.ShapeDtypeStruct((N, PAIRS, 2 * K), jnp.bfloat16),
+            jax.ShapeDtypeStruct((N, RIM_ROWS, 2 * K), jnp.bfloat16),
+            jax.ShapeDtypeStruct((N, RIM_ROWS, 2 * K), jnp.bfloat16),
+            jax.ShapeDtypeStruct((N, 2 * K), jnp.bfloat16),
+        ],
+        in_specs=[vmem()] * 3,
+        out_specs=[vmem()] * 4,
+        scratch_shapes=[
+            pltpu.VMEM((N * PAIRS, 2 * K), jnp.float32),
+            pltpu.VMEM((N * RIM_ROWS, 2 * K), jnp.float32),
+            pltpu.VMEM((N * RIM_ROWS, 2 * K), jnp.float32),
+        ],
         compiler_params=pltpu.CompilerParams(vmem_limit_bytes=20 << 20),
         cost_estimate=pl.CostEstimate(
             flops=300_000_000, bytes_accessed=3_000_000, transcendentals=0
         ),
-    )(values, basis, links, first, root)
+    )(values, basis, matrices)
 
 
 def down_kernel(
-    place_ref,
     low_ref,
     own_ref,
     high_ref,
     tops_ref,
     a_ref,
     coupling_ref,
-    links_ref,
-    first_ref,
-    root_ref,
+    matrix_ref,
     basis_ref,
     near_ref,
     out_ref,
     cf_ref,
-    side_ref,
     call_ref,
     bd_ref,
     lhs_ref,
@@ -258,21 +286,16 @@
     used = PAIRS + 2 * RIM + subtrees
     for n in range(N):
         base = n * height
-        cf_ref[base : base + PAIRS, :] = own_ref[0, n].astype(jnp.float32)
-        side_ref[...] = low_ref[0, n].astype(jnp.float32)
+        cf_ref[base : base + PAIRS, :] = own_ref[n].astype(jnp.float32)
         at = base + PAIRS
-        for start, size in ((0, 7), (8, 7), (24, 7), (56, 7)):
-            cf_ref[at : at + size, :] = side_ref[start : start + size, :]
-            at += size
-        side_ref[...] = high_ref[0, n].astype(jnp.float32)
-        for start, size in ((0, 14), (15, 7), (31, 7)):
-            cf_ref[at : at + size, :] = side_ref[start : start + size, :]
-            at += size
+        cf_ref[at : at + RIM, :] = low_ref[n].astype(jnp.float32)[:RIM]
+        at += RIM
+        cf_ref[at : at + RIM, :] = high_ref[n].astype(jnp.float32)[:RIM]
         if used < height:
             cf_ref[base + used : base + height, :] = jnp.zeros((height - used, 2 * K), jnp.float32)
     for q in range(subtrees // 2):
-        even = tops_ref[2 * q, 0].astype(jnp.float32)
-        odd = tops_ref[2 * q + 1, 0].astype(jnp.float32)
+        even = tops_ref[2 * q].astype(jnp.float32)
+        odd = tops_ref[2 * q + 1].astype(jnp.float32)
         at = PAIRS + 2 * RIM + 2 * q
         cf_ref[pl.ds(at, N, stride=height), :] = jnp.where(lower, even, even + odd)
         cf_ref[pl.ds(at + 1, N, stride=height), :] = odd
@@ -326,10 +349,10 @@
 
     last = field_of(PAIRS - 1)
     top = last[:, K : 2 * K].astype(jnp.bfloat16)
-    root = (last[:, 0:K] + dot(top, root_ref[...])).astype(jnp.bfloat16)
-    tiles = {0: field_of(0) + dot(root, first_ref[...])}
+    root = (last[:, 0:K] + dot(top, matrix_ref[0])).astype(jnp.bfloat16)
+    tiles = {0: field_of(0) + dot(root, children_of(matrix_ref, 0))}
     for j in range(B // 2 - 1):
-        both = push(tiles[j], links_ref[j])
+        both = push(tiles[j], links_of(matrix_ref, j))
         tiles[2 * j + 1] = field_of(2 * j + 1) + both[:N]
         tiles[2 * j + 2] = field_of(2 * j + 2) + both[N:]
     for i in range(B // 2):
@@ -339,45 +362,27 @@
             out_ref[:, lanes] = (near_ref[:, lanes] + both[h * N : (h + 1) * N]).astype(jnp.bfloat16)
 
 
-def downward(place, gathered, counts, coupling, links, first, root, basis, near):
-    subtrees = gathered.shape[0]
+def downward(low, own, high, tops, counts, coupling, matrices, basis, near):
     classes = counts.shape[0]
     height = counts.shape[2] // 2
-    block = (1, N + 1, PAIRS, 2 * K)
-
-    def whole(x):
-        return pl.BlockSpec(x.shape, lambda i, p: (0,) * x.ndim)
-
-    grid_spec = pltpu.PrefetchScalarGridSpec(
-        num_scalar_prefetch=1,
-        grid=(1,),
-        in_specs=[
-            pl.BlockSpec(block, lambda i, p: (jnp.maximum(p[0] - 1, 0), 0, 0, 0)),
-            pl.BlockSpec(block, lambda i, p: (p[0], 0, 0, 0)),
-            pl.BlockSpec(block, lambda i, p: (jnp.minimum(p[0] + 1, subtrees - 1), 0, 0, 0)),
-            pl.BlockSpec((subtrees, 1, N, 2 * K), lambda i, p: (0, N, 0, 0)),
-        ]
-        + [whole(x) for x in (counts, coupling, links, first, root, basis, near)],
-        out_specs=pl.BlockSpec((N, B * M), lambda i, p: (0, 0)),
+    return pl.pallas_call(
+        down_kernel,
+        name="downward",
+        out_shape=jax.ShapeDtypeStruct((N, B * M), jnp.bfloat16),
+        in_specs=[vmem()] * 9,
+        out_specs=vmem(),
         scratch_shapes=[
             pltpu.VMEM((N * height, 2 * K), jnp.float32),
-            pltpu.VMEM((PAIRS, 2 * K), jnp.float32),
             pltpu.VMEM((2 * height, N * K), jnp.bfloat16),
             pltpu.VMEM((classes * 4 * K, 4 * K), jnp.bfloat16),
             pltpu.VMEM((N // 2 * PAIRS, classes * 4 * K), jnp.bfloat16),
             pltpu.VMEM((N * PAIRS, 2 * K), jnp.float32),
         ],
-    )
-    return pl.pallas_call(
-        down_kernel,
-        name="downward",
-        out_shape=jax.ShapeDtypeStruct((N, B * M), jnp.bfloat16),
-        grid_spec=grid_spec,
-        compiler_params=pltpu.CompilerParams(vmem_limit_bytes=48 << 20),
+        compiler_params=pltpu.CompilerParams(vmem_limit_bytes=40 << 20),
         cost_estimate=pl.CostEstimate(
             flops=4_000_000_000, bytes_accessed=6_000_000, transcendentals=0
         ),
-    )(place, gathered, gathered, gathered, gathered, counts, coupling, links, first, root, basis, near)
+    )(low, own, high, tops, counts, coupling, matrices, basis, near)
 
 
 def source_columns(far_src, top_src, position, subtrees, height):
@@ -431,16 +436,16 @@
     ).astype(jnp.float32) + 0.5
     local = coords.reshape(3, B, M) - centre[:, :, None]
     flat = coords - jnp.repeat(centre, M, axis=1)
-    high = rounded(flat)
-    rest = rounded(flat - high)
-    held = high + rest
+    coarse = rounded(flat)
+    rest = rounded(flat - coarse)
+    held = coarse + rest
     size = -SCALE * (held[0] ** 2 + held[1] ** 2 + held[2] ** 2)
     size_a = rounded(size)
     size_b = rounded(size - size_a)
     size_c = size - size_a - size_b
     rows = []
     for k in range(3):
-        rows += [high[k], rest[k]]
+        rows += [coarse[k], rest[k]]
     rows += [size_a, size_b, size_c, jnp.ones_like(size)]
     rows += [jnp.zeros_like(size)] * 6
     packed = jnp.concatenate([values, jnp.stack(rows).astype(jnp.bfloat16)], axis=0)
@@ -454,11 +459,10 @@
         - jnp.arange(-1, 2, dtype=jnp.float32)[None, None, :, None, None]
     )
     row = jnp.arange(16, dtype=jnp.int32)[None, None, None, :, None]
-    axis = jnp.arange(3, dtype=jnp.int32)[None, :, None, None, None]
     term = jnp.where(
         row < 4,
         2 * SCALE * moved,
-        -SCALE * moved * moved + jnp.where(axis == 0, SHIFT, 0.0),
+        -SCALE * moved * moved,
     )
     term_a = rounded(term)
     term_b = rounded(term - term_a)
@@ -471,10 +475,6 @@
     x_tiles = x_tiles.astype(jnp.bfloat16).reshape(B, 9, 16, M)
 
     matrices = transfer.reshape(TB, K, K)
-    siblings = matrices[1:].reshape(TB // 2, 2, K, K).transpose(0, 2, 1, 3).reshape(TB // 2, K, 2 * K)
-    first = siblings[0]
-    links = siblings[1:].reshape(B // 2 - 1, 2 * K, 2 * K)
-    root = matrices[0]
     coupling_t = jnp.transpose(coupling.reshape(class_count, K, K), (0, 2, 1))
 
     columns = source_columns(far_src, top_src, position, subtrees, height)
@@ -485,14 +485,14 @@
     )
     counts = class_counts(columns, classes, class_count, 2 * height)
 
+    whole_basis, counts, x_tiles = lax.optimization_barrier((whole_basis, counts, x_tiles))
     basis_pairs = whole_basis.reshape(B // 2, 2 * K, M)
-    coefs = upward(values, basis_pairs, links, first, root)
-    gathered = lax.all_gather(coefs, "leaf", axis=0)
+    coefs, first, last, root = upward(values, basis_pairs, matrices)
+    tops = lax.all_gather(root, "leaf", axis=0)
+    low = lax.ppermute(last, "leaf", forward)
+    high = lax.ppermute(first, "leaf", backward)
     near = near_field(near_src, x_tiles, from_low, packed, from_high)
-    place = jnp.full((1,), 0, jnp.int32) + position
-    return downward(
-        place, gathered, counts, coupling_t, links, first, root, basis_pairs, near
-    )
+    return downward(low, coefs, high, tops, counts, coupling_t, matrices, basis_pairs, near)
 
 
 def solution(mesh):

time: 113 us -> 136 us (1.20)
  blocking collectives: 0 us -> 33 us
  local copies, waits for them, and re-layouts: 26.5 us -> 16.5 us
  waiting for transfers between devices: 6.98 us -> 0.03 us
  starting transfers between devices: 7.03 us -> 13 us
  other arithmetic: 4.23 us -> 6.83 us
    all_gather x0 -> x1, blocking collectives: none -> 33 us  [per_device(): tops = lax.all_gather(root, 'leaf', axis=0)]
    all_gather x1 -> x0, waiting for transfers between devices: 6.24 us -> none  [per_device(): gathered = lax.all_gather(coefs, 'leaf', axis=0)]
    ppermute x0 -> x2, starting transfers between devices: none -> 5.99 us  [the longest x1 4.56 us: per_device(): low = lax.ppermute(last, 'leaf', forward)]
    slice x6 -> x2, local copies, waits for them, and re-layouts: 5.4 us -> 0.15 us  [per_device(): rows += [coarse[k], rest[k]]]
    reshape x3 -> x1, local copies, waits for them, and re-layouts: 9.15 us -> 4.24 us  [per_device(): matrices = transfer.reshape(TB, K, K)]
    convert_element_type x1, other arithmetic: 1.49 us -> 4.1 us  [per_device(): x_tiles = x_tiles.astype(jnp.bfloat16).reshape(B, 9, 16, M)]
    unnamed x31 -> x30, local copies, waits for them, and re-layouts: 6.18 us -> 4.24 us
    mul x1 -> x2, local copies, waits for them, and re-layouts: 0.19 us -> 2.06 us  [per_device(): term = jnp.where(row < 4, 2 * SCALE * moved, -SCALE * moved * moved)]
  transfers between devices with their start and end apart: 4 -> 5, of which waited for: 1 -> 0; matrix products, arithmetic and copies ran while one was open for 22% -> 13% of each run, Pallas kernels for 38% -> 31%
where the time goes in v2:
time: 136 us
  Pallas kernels  52.9 us (39%)
  blocking collectives  33 us (24%)
  local copies, waits for them, and re-layouts  16.5 us (12%)
  between operations  13.8 us (10%)
  starting transfers between devices  13 us (10%)
  other arithmetic  6.83 us (5%)
    pallas_call x1, Pallas kernels, near_field(): pl.pallas_call(near_kernel, name='near_field', out_shape=jax.ShapeDtypeSt...  37.8 us
    all_gather x1, blocking collectives, per_device(): tops = lax.all_gather(root, 'leaf', axis=0)  33 us
    pallas_call x1, Pallas kernels, downward(): pl.pallas_call(down_kernel, name='downward', out_shape=jax.ShapeDtypeStru...  10.4 us
    ppermute x1, starting transfers between devices, per_device(): from_low = lax.ppermute(packed, 'leaf', forward)  5.71 us
    ppermute x1, starting transfers between devices, per_device(): low = lax.ppermute(last, 'leaf', forward)  4.56 us
    reshape x1, local copies, waits for them, and re-layouts, per_device(): matrices = transfer.reshape(TB, K, K)  4.24 us
    unnamed x30, local copies, waits for them, and re-layouts  4.24 us
    convert_element_type x1, other arithmetic, per_device(): x_tiles = x_tiles.astype(jnp.bfloat16).reshape(B, 9, 16, M)  4.1 us
  transfers between devices with their start and end apart: 5, of which 0 were waited for; matrix products, arithmetic and copies ran while one was open for 13% of the time, Pallas kernels for 31%

profile of v2, /device:TPU:0, one launch (start us, length us, event | category | flops | bytes accessed | tf_op | source)
XLA Modules:
  0.0 136.1 jit_solution(10597451179418006413)
XLA Ops:
  6.5 0.0 all-gather.3.cloned.1.call-start
  6.6 0.1 pad.2.clone
  6.6 0.1 fusion.24
  6.7 1.0 broadcast_bitcast_fusion
  7.7 1.0 reduce-precision_add_fusion
  8.7 0.1 fusion.6
  8.9 0.1 fusion.26
  9.0 0.1 fusion.27
  9.2 1.6 %concatenate.16.own_ref = bf16[32,8192]{1,0:T(8,128)(2,1)S(1)} concatenate(bf16[16,8192]{1,0:T(8,128)(2,1)} %values_ref.1, bf16[1,8192]{1,0:T(2,128)(2,1)S(1)} %get-tuple-element.33, bf16[1,8192]{1,0:T(2,128)(2,1)S(1)} %get-tuple-element.30, bf16[1,8192]{1,0:T(2,128)(2,1)S(1)} %get-tuple-element.32, bf16[1,8192]{1,0:T(2,128)(2,1)S(1)} %get-tuple-element.29, ...), dimensions={0} | concatenate | bytes 1048576 | tf_op jit(solution)/shard_map/concatenate | solution.py:451
  10.7 5.7 %collective-permute-start.2 = (bf16[32,8192]{1,0:T(8,128)(2,1)S(1)}, bf16[32,8192]{1,0:T(8,128)(2,1)}, u32[]{:S(2)}, u32[]{:S(2)}) collective-permute-start(bf16[32,8192]{1,0:T(8,128)(2,1)S(1)} %concatenate.16.own_ref), channel_id=1, source_target_pairs={{0,4},{4,8},{8,12},{12,16},{16,20},{20,24},{24,28},{1,5},{5,9},{9,... | collective-permute-start | bytes 1572872 | tf_op jit(solution)/shard_map/ppermute | solution.py:454
  16.4 1.3 collective-permute-start.3
  17.7 0.0 all-gather.3.cloned.1.call-update
  17.8 0.8 constant_dynamic-slice_fusion.1
  18.5 0.1 copy.68
  18.6 0.1 copy.69
  18.7 0.0 copy-done.11
  18.7 0.1 slice.54
  18.8 0.1 copy.52
  18.9 0.1 fusion.28
  19.0 0.1 copy.53
  19.1 0.1 copy.55
  19.1 0.1 pad_add_fusion.1
  19.2 0.1 copy.58.cls_ref
  19.3 0.1 copy.67
  19.4 0.1 copy.66
  19.5 0.0 copy-done.9
  19.5 0.1 add_select_fusion.5
  19.6 0.1 fusion.15
  19.7 0.1 copy.47
  19.8 0.1 fusion.29
  19.9 0.1 copy.48
  20.0 0.1 copy.50
  20.0 0.1 pad_add_fusion
  20.1 0.1 copy.57.col_ref
  20.3 0.0 copy-start.10
  20.3 2.6 %class_counts.1.a_ref = bf16[24,128,256]{2,1,0:T(8,128)(2,1)S(1)} custom-call(s32[128,24]{1,0:T(8,128)S(1)} %copy.57.col_ref, s32[128,24]{1,0:T(8,128)S(1)} %copy.58.cls_ref), custom_call_target="tpu_custom_call" | custom-call | flops 2000000000 | bytes 1600000 | tf_op jit(solution)/shard_map/class_counts/pallas_call | solution.py:171
  22.9 0.0 copy-start.6
  23.0 0.1 sub.132
  23.0 0.1 fusion.2
  23.2 1.1 copy.59
  24.2 1.0 copy.60
  25.2 0.0 copy-done.10
  25.2 0.1 copy.64.near_ref
  25.3 2.4 %copy.61 = bf16[127,4096]{0,1:T(8,128)(2,1)} copy(bf16[127,4096]{1,0:T(8,128)(2,1)} %param.15) | data formatting | bytes 2080768 | tf_op args[3]
  27.7 0.0 copy-done.6
  27.7 4.2 %copy.62.matrix_ref = bf16[127,64,64]{2,1,0:T(8,128)(2,1)S(1)} copy(bf16[127,64,64]{0,2,1:T(8,128)(2,1)} %bitcast.36) | data formatting | bytes 2080768 | tf_op jit(solution)/shard_map/reshape | solution.py:477
  32.0 0.0 copy-start.3
  32.0 1.1 reshape.149
  33.1 1.2 copy.63
  34.3 0.0 copy-start.4
  34.3 0.0 copy-start.5
  34.3 4.1 %fusion.x_ref = bf16[64,9,16,128]{3,2,1,0:T(8,128)(2,1)} fusion(f32[64,9,128]{2,1,0:T(8,128)} %copy.60, f32[64,9,128]{2,1,0:T(8,128)} %copy.59, pred[16]{0:T(512)(128)(4,1)S(1)} %get-tuple-element.60, pred[16]{0:T(512)(128)(4,1)S(1)} %get-tuple-element.58, pred[16]{0:T(512)(128)(4,1)S(1)} %get-tuple-element.61, pred[16]{0:T(512)(128)(4,1)S(1)} %get-tuple-element.59), kind=kLoop, calls=%fused_computation.4 | loop fusion | flops 10616832 | bytes 2949184 | tf_op jit(solution)/shard_map/convert_element_type | solution.py:475
  38.4 0.0 copy-done.3
  38.4 1.4 %copy-done.1 = bf16[64,64,128]{2,1,0:T(8,128)(2,1)S(1)} copy-done((bf16[64,64,128]{2,1,0:T(8,128)(2,1)S(1)}, bf16[64,64,128]{2,1,0:T(8,128)(2,1)}, u32[]{:S(2)}) %copy-start.1) | copy-done | bytes 1048600
  39.8 2.1 %upward.1 = (bf16[16,64,128]{2,1,0:T(8,128)(2,1)S(1)}, bf16[16,32,128]{2,1,0:T(8,128)(2,1)S(1)}, bf16[16,32,128]{2,1,0:T(8,128)(2,1)S(1)}, bf16[16,128]{1,0:T(8,128)(2,1)S(1)}) custom-call(bf16[16,8192]{1,0:T(8,128)(2,1)S(1)} %copy-done.3, bf16[32,128,128]{2,1,0:T(8,128)(2,1)S(1)} %bitcast.32, bf16[127,64,64]{2,1,0:T(8,128)(2,1)S(1)} %copy.62.matrix_ref), custom_call_target="tpu_custom_call" | custom-call | flops 300000000 | bytes 3000000 | tf_op jit(solution)/shard_map/upward/pallas_call | solution.py:241
  41.9 4.6 %collective-permute-start = (bf16[16,32,128]{2,1,0:T(8,128)(2,1)S(1)}, bf16[16,32,128]{2,1,0:T(8,128)(2,1)S(1)}, u32[]{:S(2)}, u32[]{:S(2)}) collective-permute-start(bf16[16,32,128]{2,1,0:T(8,128)(2,1)S(1)} %get-tuple-element.13), channel_id=1, source_target_pairs={{0,4},{4,8},{8,12},{12,16},{16,20},{20,24},{24,28},{1,5},{5,9},{9,... | collective-permute-start | bytes 393224 | tf_op jit(solution)/shard_map/ppermute | solution.py:492
  46.5 1.4 %collective-permute-start.1 = (bf16[16,32,128]{2,1,0:T(8,128)(2,1)S(1)}, bf16[16,32,128]{2,1,0:T(8,128)(2,1)S(1)}, u32[]{:S(2)}, u32[]{:S(2)}) collective-permute-start(bf16[16,32,128]{2,1,0:T(8,128)(2,1)S(1)} %get-tuple-element.15), channel_id=1, source_target_pairs={{4,0},{8,4},{12,8},{16,12},{20,16},{24,20},{28,24},{5,1},{9,5},{13... | collective-permute-start | bytes 393224 | tf_op jit(solution)/shard_map/ppermute | solution.py:493
  47.9 0.0 collective-permute-done.2.low_ref
  47.9 0.0 collective-permute-done.3.high_ref
  48.0 37.8 %near_field.1.near_ref = f32[16,8192]{1,0:T(8,128)S(1)} custom-call(s32[64,27]{1,0:T(8,128)S(1)} %copy.64.near_ref, bf16[64,9,16,128]{3,2,1,0:T(8,128)(2,1)S(1)} %copy-done, bf16[32,8192]{1,0:T(8,128)(2,1)} %collective-permute-done.2.low_ref, bf16[32,8192]{1,0:T(8,128)(2,1)S(1)} %concatenate.16.own_ref, bf16[32,8192]{1,0:T(8,128)(2,1)} %collective-permute-done.3.high_ref, ...), custom_call_target="tpu_custom_call" | custom-call | flops 20000000000 | bytes 5000000 | tf_op jit(solution)/shard_map/near_field/pallas_call | solution.py:113
  85.8 33.0 %all-gather = bf16[128,128]{1,0:T(8,128)(2,1)S(1)} all-gather(bf16[16,128]{1,0:T(8,128)(2,1)S(1)} %get-tuple-element.16), channel_id=2, replica_groups=mesh['leaf'=8,'vec'=4] {'leaf'}, dimensions={0}, use_global_device_ids=true | all-gather | bytes 36864 | tf_op jit(solution)/shard_map/all_gather | solution.py:491
  118.8 0.0 collective-permute-done.low_ref
  118.8 0.0 collective-permute-done.1.high_ref
  118.8 10.4 %downward.1 = bf16[16,8192]{1,0:T(8,128)(2,1)} custom-call(bf16[16,32,128]{2,1,0:T(8,128)(2,1)S(1)} %collective-permute-done.low_ref, bf16[16,64,128]{2,1,0:T(8,128)(2,1)S(1)} %get-tuple-element.14.own_ref, bf16[16,32,128]{2,1,0:T(8,128)(2,1)S(1)} %collective-permute-done.1.high_ref, bf16[8,16,128]{2,1,0:T(8,128)(2,1)S(1)} %bitcast.35, ...), custom_call_target="tpu_custom_call" | custom-call | flops 4000000000 | bytes 6000000 | tf_op jit(solution)/shard_map/downward/pallas_call | solution.py:368
  (27 shorter events, 0.2 us)
Async XLA Ops:
  6.5 12.2 %copy-start.11 = (s32[127,24]{0,1:T(8,128)S(1)}, s32[127,24]{0,1:T(8,128)}, u32[]{:S(2)}) copy-start(s32[127,24]{0,1:T(8,128)} %param.19) | copy-start | bytes 36580
  6.5 13.0 %copy-start.9 = (s32[127,24]{0,1:T(8,128)S(1)}, s32[127,24]{0,1:T(8,128)}, u32[]{:S(2)}) copy-start(s32[127,24]{0,1:T(8,128)} %param.18) | copy-start | bytes 36580
  6.5 31.9 %all-gather.3.cloned.1.call-start = ((), (), s32[]{:S(2)}) async-start(), calls=%async_computation | async-start | bytes 1310720 | tf_op jit(solution)/shard_map/all_gather | solution.py:431
  10.7 37.2 %collective-permute-start.2 = (bf16[32,8192]{1,0:T(8,128)(2,1)S(1)}, bf16[32,8192]{1,0:T(8,128)(2,1)}, u32[]{:S(2)}, u32[]{:S(2)}) collective-permute-start(bf16[32,8192]{1,0:T(8,128)(2,1)S(1)} %concatenate.16.own_ref), channel_id=1, source_target_pairs={{0,4},{4,8},{8,12},{12,16},{16,20},{20,24},{24,28},{1,5},{5,9},{9,... | collective-permute-start | bytes 1572872 | tf_op jit(solution)/shard_map/ppermute | solution.py:454
  16.4 31.5 %collective-permute-start.3 = (bf16[32,8192]{1,0:T(8,128)(2,1)S(1)}, bf16[32,8192]{1,0:T(8,128)(2,1)}, u32[]{:S(2)}, u32[]{:S(2)}) collective-permute-start(bf16[32,8192]{1,0:T(8,128)(2,1)S(1)} %concatenate.16.own_ref), channel_id=1, source_target_pairs={{4,0},{8,4},{12,8},{16,12},{20,16},{24,20},{28,24},{5,1},{9,5},{13... | collective-permute-start | bytes 1572872 | tf_op jit(solution)/shard_map/ppermute | solution.py:455
  20.3 5.0 %copy-start.10 = (s32[64,27]{0,1:T(8,128)S(1)}, s32[64,27]{0,1:T(8,128)}, u32[]{:S(2)}) copy-start(s32[64,27]{0,1:T(8,128)} %param.17) | copy-start | bytes 20740
  22.9 4.8 %copy-start.6 = (bf16[24,128,256]{2,1,0:T(8,128)(2,1)}, bf16[24,128,256]{2,1,0:T(8,128)(2,1)S(1)}, u32[]{:S(2)}) copy-start(bf16[24,128,256]{2,1,0:T(8,128)(2,1)S(1)} %class_counts.1.a_ref) | copy-start | bytes 4718596
  25.3 6.6 %copy-start.8 = (bf16[24,4096]{1,0:T(8,128)(2,1)S(1)}, bf16[24,4096]{1,0:T(8,128)(2,1)}, u32[]{:S(2)}) copy-start(bf16[24,4096]{1,0:T(8,128)(2,1)} %param.16) | copy-start | bytes 589828
  32.0 6.5 %copy-start.3 = (bf16[16,8192]{1,0:T(8,128)(2,1)S(1)}, bf16[16,8192]{1,0:T(8,128)(2,1)}, u32[]{:S(2)}) copy-start(bf16[16,8192]{1,0:T(8,128)(2,1)} %values_ref.1) | copy-start | bytes 786436
  34.3 13.6 %copy-start.4 = (bf16[32,128]{1,0:T(8,128)(2,1)S(1)}, bf16[32,128]{1,0:T(8,128)(2,1)}, u32[]{:S(2)}) copy-start(bf16[32,128]{1,0:T(8,128)(2,1)} %constant.168.clone.sel_ref) | copy-start | bytes 24580
  34.3 13.6 %copy-start.5 = (bf16[2,16,128]{2,1,0:T(8,128)(2,1)S(1)}, bf16[2,16,128]{2,1,0:T(8,128)(2,1)}, u32[]{:S(2)}) copy-start(bf16[2,16,128]{2,1,0:T(8,128)(2,1)} %constant.169.clone.mask_ref) | copy-start | bytes 24580
  38.4 9.5 %copy-start = (bf16[64,9,16,128]{3,2,1,0:T(8,128)(2,1)S(1)}, bf16[64,9,16,128]{3,2,1,0:T(8,128)(2,1)}, u32[]{:S(2)}) copy-start(bf16[64,9,16,128]{3,2,1,0:T(8,128)(2,1)} %fusion.x_ref) | copy-start | bytes 7077892
  38.4 1.4 %copy-start.1 = (bf16[64,64,128]{2,1,0:T(8,128)(2,1)S(1)}, bf16[64,64,128]{2,1,0:T(8,128)(2,1)}, u32[]{:S(2)}) copy-start(bf16[64,64,128]{2,1,0:T(8,128)(2,1)} %all-gather.3.cloned.1.call-done) | copy-start | bytes 3145732
  41.9 76.9 %collective-permute-start = (bf16[16,32,128]{2,1,0:T(8,128)(2,1)S(1)}, bf16[16,32,128]{2,1,0:T(8,128)(2,1)S(1)}, u32[]{:S(2)}, u32[]{:S(2)}) collective-permute-start(bf16[16,32,128]{2,1,0:T(8,128)(2,1)S(1)} %get-tuple-element.13), channel_id=1, source_target_pairs={{0,4},{4,8},{8,12},{12,16},{16,20},{20,24},{24,28},{1,5},{5,9},{9,... | collective-permute-start | bytes 393224 | tf_op jit(solution)/shard_map/ppermute | solution.py:492
  46.5 72.4 %copy-start.2 = (bf16[64,64,128]{2,1,0:T(8,128)(2,1)S(1)}, bf16[64,64,128]{2,1,0:T(8,128)(2,1)}, u32[]{:S(2)}) copy-start(bf16[64,64,128]{2,1,0:T(8,128)(2,1)} %all-gather.3.cloned.1.call-done) | copy-start | bytes 3145732
  46.5 72.4 %copy-start.7 = (bf16[24,128,256]{2,1,0:T(8,128)(2,1)S(1)}, bf16[24,128,256]{2,1,0:T(8,128)(2,1)}, u32[]{:S(2)}) copy-start(bf16[24,128,256]{2,1,0:T(8,128)(2,1)} %copy-done.6) | copy-start | bytes 4718596
  46.5 72.3 %collective-permute-start.1 = (bf16[16,32,128]{2,1,0:T(8,128)(2,1)S(1)}, bf16[16,32,128]{2,1,0:T(8,128)(2,1)S(1)}, u32[]{:S(2)}, u32[]{:S(2)}) collective-permute-start(bf16[16,32,128]{2,1,0:T(8,128)(2,1)S(1)} %get-tuple-element.15), channel_id=1, source_target_pairs={{4,0},{8,4},{12,8},{16,12},{20,16},{24,20},{28,24},{5,1},{9,5},{13... | collective-permute-start | bytes 393224 | tf_op jit(solution)/shard_map/ppermute | solution.py:493
Sparse Core Ops, SparseCore 0:
  17.9 19.0 all-gather.2

commit v3 on v2

--- a/solution.py
+++ b/solution.py
@@ -39,97 +39,175 @@
     return lax.reduce_precision(x, 8, 7)
 
 
-def near_kernel(near_ref, x_ref, low_ref, own_ref, high_ref, sel_ref, mask_ref, out_ref, yp_ref):
+def near_tables():
+    def split(value, parts):
+        out = []
+        for _ in range(parts):
+            part = float(np.float32(np.asarray(value).astype(jnp.bfloat16)))
+            out.append(part)
+            value -= part
+        return out
+
+    one = 9
+    lanes = []
+    for k in range(3):
+        high, rest = 2 * k, 2 * k + 1
+        x_high, x_rest = 10 + 2 * k, 11 + 2 * k
+        for y in (high, rest):
+            for x in (x_high, x_rest):
+                lanes.append((y, None, x, 1.0))
+            for part in split(-2 * SCALE, 2):
+                lanes.append((y, k, one, part))
+        for x in (x_high, x_rest):
+            lanes.append((one, k, x, 1.0))
+    for row in (6, 7, 8):
+        lanes.append((one, None, row, 1.0))
+        lanes.append((row, None, one, 1.0))
+    for part in split(-SCALE, 3):
+        lanes.append((one, 3, one, part))
+    lanes.append((one, 4, one, DEAD))
+    source = np.zeros((32, 128), np.float32)
+    target = np.zeros((64, 16), np.float32)
+    factor = np.zeros((27, 16, 128), np.float32)
+    dead = np.zeros((4, 16, 128), np.float32)
+    for lane, (y, kind, x, part) in enumerate(lanes):
+        target[lane, x] = part
+        for half in range(2):
+            at = 64 * half + lane
+            source[16 * half + y, at] = 1
+            for slot in range(27):
+                step = (slot % 3 - 1, slot // 3 % 3 - 1, slot // 9 - 1)
+                if kind is None:
+                    factor[slot, :, at] = 1
+                elif kind < 3:
+                    factor[slot, :, at] = step[kind]
+                elif kind == 3:
+                    factor[slot, :, at] = sum(d * d for d in step)
+            if kind == 4:
+                for flags in range(4):
+                    dead[flags, :, at] = flags >> half & 1
+    return [jnp.asarray(x, jnp.bfloat16) for x in (source, target, factor, dead)]
+
+
+def near_kernel(
+    near_ref, low_ref, own_ref, high_ref, source_ref, target_ref, factor_ref, dead_ref, out_ref, yp_ref
+):
     layers = (low_ref, own_ref, high_ref)
+
+    def at(u):
+        return pl.ds(pl.multiple_of(jnp.clip(u, 0, B - 1) * M, M), M)
+
     for l, src in enumerate(layers):
 
         def features(u, carry, l=l, src=src):
-            first = pl.multiple_of(jnp.maximum(u - 1, 0) * M, M)
-            second = pl.multiple_of(jnp.minimum(u, B - 1) * M, M)
-            both = jnp.concatenate(
-                [src[16:32, pl.ds(first, M)], src[16:32, pl.ds(second, M)]], axis=0
-            )
-            yp_ref[l, u] = dot(both, sel_ref[...], TN).astype(jnp.bfloat16)
+            both = jnp.concatenate([src[16:32, at(u - 1)], src[16:32, at(u)]], axis=0)
+            yp_ref[l, u] = dot(both, source_ref[...], TN).astype(jnp.bfloat16)
             return carry
 
         lax.fori_loop(0, B + 1, features, 0, unroll=5)
 
     zero = jnp.zeros((64, M), jnp.bfloat16)
 
-    def weights(t, a, b, c, slot):
-        live = jnp.where(near_ref[t, slot] >= 0, 1, 0)
-        return jnp.concatenate(
-            [x_ref[t, a], x_ref[t, 3 + b], x_ref[t, 6 + c], mask_ref[live]], axis=0
+    def target(t):
+        return dot(target_ref[...], own_ref[16:32, at(t)]).astype(jnp.bfloat16)
+
+    def pair(t, steps):
+        w = jnp.concatenate(
+            [
+                jnp.concatenate([target(t), zero], axis=1),
+                jnp.concatenate([zero, target(t + 1)], axis=1),
+            ],
+            axis=0,
         )
-
-    for row in range(B // ROW):
-        steps = [b for b in range(3) if 0 <= row + b - 1 < B // ROW]
-
-        def pair(q, carry, row=row, steps=steps):
-            t = row * ROW + 2 * q
-            kernels, vectors = [], []
-            for c in range(3):
-                for b in steps:
-                    for a in range(3):
-                        slot = 9 * c + 3 * b + a
-                        u = t + (b - 1) * ROW + a - 1
-                        w = jnp.concatenate(
-                            [
-                                jnp.concatenate([weights(t, a, b, c, slot), zero], axis=1),
-                                jnp.concatenate([zero, weights(t + 1, a, b, c, slot)], axis=1),
-                            ],
-                            axis=0,
-                        )
-                        e = dot(yp_ref[c, u + 1], w)
-                        kernels.append(jnp.exp2(e.astype(jnp.bfloat16)))
-                        first = pl.multiple_of(jnp.maximum(u, 0) * M, M)
-                        second = pl.multiple_of(jnp.minimum(u + 1, B - 1) * M, M)
-                        src = layers[c]
-                        vectors.append(
-                            jnp.concatenate(
-                                [src[0:16, pl.ds(first, M)], src[0:16, pl.ds(second, M)]], axis=0
-                            )
-                        )
-            total = dot(jnp.concatenate(vectors, axis=1), jnp.concatenate(kernels, axis=0))
-            here = pl.multiple_of(t * M, M)
-            out_ref[:, pl.ds(here, M)] = AMPLITUDE * total[0:16, 0:M]
-            out_ref[:, pl.ds(here + M, M)] = AMPLITUDE * total[16:32, M : 2 * M]
+        kernels, vectors = [], []
+        for c in range(3):
+            src = layers[c]
+            for b in steps:
+                for a in range(3):
+                    slot = 9 * c + 3 * b + a
+                    u = t + (b - 1) * ROW + a - 1
+                    flags = jnp.where(near_ref[t, slot] < 0, 1, 0) + jnp.where(
+                        near_ref[t + 1, slot] < 0, 2, 0
+                    )
+                    factor = factor_ref[slot] + dead_ref[flags]
+                    left = yp_ref[c, u + 1] * jnp.concatenate([factor] * 8, axis=0)
+                    kernels.append(jnp.exp2(dot(left, w)).astype(jnp.bfloat16))
+                    vectors.append(jnp.concatenate([src[0:16, at(u)], src[0:16, at(u + 1)]], axis=0))
+        total = dot(jnp.concatenate(vectors, axis=1), jnp.concatenate(kernels, axis=0))
+        out_ref[:, at(t)] = AMPLITUDE * total[0:16, 0:M]
+        out_ref[:, at(t + 1)] = AMPLITUDE * total[16:32, M : 2 * M]
+
+    rows = B // ROW
+    for first, last, steps in ((0, 1, (1, 2)), (1, rows - 1, (0, 1, 2)), (rows - 1, rows, (0, 1))):
+
+        def step(q, carry, first=first, steps=steps):
+            t = first * ROW + 4 * q
+            pair(t, steps)
+            pair(t + 2, steps)
             return carry
 
-        lax.fori_loop(0, ROW // 2, pair, 0)
-
-
-def near_field(near_src, x_tiles, low, own, high):
-    sel = np.zeros((32, 128), np.float32)
-    for half in range(2):
-        for k in range(3):
-            for r, source in enumerate((2 * k, 2 * k + 1, 2 * k, 2 * k + 1, 9, 9, 9)):
-                sel[16 * half + source, 64 * half + 16 * k + r] = 1
-        for r, source in enumerate((9, 6, 7, 8)):
-            sel[16 * half + source, 64 * half + 48 + r] = 1
-    mask = np.zeros((2, 16, 128), np.float32)
-    mask[:, 1:4] = 1
-    mask[0, 0] = DEAD
+        lax.fori_loop(0, (last - first) * ROW // 4, step, 0)
+
+
+def near_field(near_src, low, own, high):
     return pl.pallas_call(
         near_kernel,
         name="near_field",
         out_shape=jax.ShapeDtypeStruct((N, B * M), jnp.float32),
-        in_specs=[pl.BlockSpec(memory_space=pltpu.SMEM)] + [vmem()] * 6,
+        in_specs=[pl.BlockSpec(memory_space=pltpu.SMEM)] + [vmem()] * 7,
         out_specs=vmem(),
         scratch_shapes=[pltpu.VMEM((3, B + 1, M, M), jnp.bfloat16)],
         compiler_params=pltpu.CompilerParams(vmem_limit_bytes=40 << 20),
         cost_estimate=pl.CostEstimate(
             flops=20_000_000_000, bytes_accessed=5_000_000, transcendentals=28_000_000
         ),
-    )(
-        near_src,
-        x_tiles,
-        low,
-        own,
-        high,
-        jnp.asarray(sel, jnp.bfloat16),
-        jnp.asarray(mask, jnp.bfloat16),
-    )
+    )(near_src, low, own, high, *near_tables())
+
+
+def relay_kernel(transfer_ref, coupling_ref, links_ref, coupling_t_ref, flat_ref, pair_ref):
+    lower = lax.broadcasted_iota(jnp.int32, (K // 2, 2 * K), 1) < K
+
+    def unpack(ref):
+        for i in range(K // 2):
+            flat_ref[pl.ds(i, ref.shape[0], stride=K // 2), :] = ref[
+                :, 2 * K * i : 2 * K * (i + 1)
+            ].astype(jnp.float32)
+
+    def join(left, right):
+        one = flat_ref[left * (K // 2) : (left + 1) * (K // 2), :]
+        two = flat_ref[right * (K // 2) : (right + 1) * (K // 2), :]
+        pair_ref[pl.ds(0, K // 2, stride=2), :] = jnp.where(lower, one, pltpu.roll(two, K, 1))
+        pair_ref[pl.ds(1, K // 2, stride=2), :] = jnp.where(lower, pltpu.roll(one, K, 1), two)
+        return pair_ref[...]
+
+    unpack(transfer_ref)
+    for p in range(PAIRS - 1):
+        links_ref[p] = join(2 * p + 1, 2 * p + 2).astype(jnp.bfloat16)
+    links_ref[PAIRS - 1] = join(0, 0).astype(jnp.bfloat16)
+    unpack(coupling_ref)
+    for p in range(coupling_ref.shape[0] // 2):
+        both = jnp.transpose(join(2 * p, 2 * p + 1)).astype(jnp.bfloat16)
+        coupling_t_ref[2 * p] = both[0:K]
+        coupling_t_ref[2 * p + 1] = both[K : 2 * K]
+
+
+def relay(transfer, coupling):
+    return pl.pallas_call(
+        relay_kernel,
+        name="relay",
+        out_shape=[
+            jax.ShapeDtypeStruct((PAIRS, K, 2 * K), jnp.bfloat16),
+            jax.ShapeDtypeStruct((coupling.shape[0], K, K), jnp.bfloat16),
+        ],
+        in_specs=[vmem()] * 2,
+        out_specs=[vmem()] * 2,
+        scratch_shapes=[
+            pltpu.VMEM(((TB + 1) * K // 2, 2 * K), jnp.float32),
+            pltpu.VMEM((K, 2 * K), jnp.float32),
+        ],
+        compiler_params=pltpu.CompilerParams(vmem_limit_bytes=16 << 20),
+        cost_estimate=pl.CostEstimate(flops=1000, bytes_accessed=100_000, transcendentals=0),
+    )(transfer, coupling)
 
 
 def counts_kernel(col_ref, cls_ref, a_ref):
@@ -176,7 +254,7 @@
         out_specs=vmem(),
         compiler_params=pltpu.CompilerParams(vmem_limit_bytes=20 << 20),
         cost_estimate=pl.CostEstimate(
-            flops=2_000_000_000, bytes_accessed=1_600_000, transcendentals=0
+            flops=1000, bytes_accessed=100_000, transcendentals=0
         ),
     )(columns, classes)
 
@@ -186,19 +264,12 @@
 RIM_ROWS = 32
 
 
-def children_of(matrix_ref, slot):
-    return jnp.concatenate([matrix_ref[2 * slot + 1], matrix_ref[2 * slot + 2]], axis=1)
-
-
-def links_of(matrix_ref, pair_index):
-    return jnp.concatenate(
-        [children_of(matrix_ref, 2 * pair_index + 1), children_of(matrix_ref, 2 * pair_index + 2)],
-        axis=0,
-    )
+def links_of(links_ref, pair_index):
+    return jnp.concatenate([links_ref[2 * pair_index + 1], links_ref[2 * pair_index + 2]], axis=0)
 
 
 def up_kernel(
-    values_ref, basis_ref, matrix_ref, out_ref, first_ref, last_ref, root_ref, cs_ref, fs_ref, ls_ref
+    values_ref, basis_ref, links_ref, out_ref, first_ref, last_ref, root_ref, cs_ref, fs_ref, ls_ref
 ):
     lower = lax.broadcasted_iota(jnp.int32, (N, 2 * K), 1) < K
 
@@ -222,13 +293,14 @@
         keep(B // 2 - 1 + i, tiles[B // 2 - 1 + i].astype(jnp.float32))
     for j in reversed(range(B // 2 - 1)):
         stacked = jnp.concatenate([tiles[2 * j + 1], tiles[2 * j + 2]], axis=0)
-        tiles[j] = lift(stacked, links_of(matrix_ref, j))
+        tiles[j] = lift(stacked, links_of(links_ref, j))
         keep(j, tiles[j].astype(jnp.float32))
-    root = dot(tiles[0], children_of(matrix_ref, 0), NT).astype(jnp.bfloat16)
-    up = dot(root, matrix_ref[0], NT)
+    root = dot(tiles[0], links_ref[0], NT).astype(jnp.bfloat16)
+    up = dot(root, links_ref[PAIRS - 1][:, 0:K], NT)
     last = jnp.concatenate([root.astype(jnp.float32), up], axis=1)
     keep(PAIRS - 1, last)
-    root_ref[...] = last.astype(jnp.bfloat16)
+    root_ref[0] = last.astype(jnp.bfloat16)
+    root_ref[1:] = jnp.zeros((N - 1, N, 2 * K), jnp.bfloat16)
     for n in range(N):
         out_ref[n] = cs_ref[n * PAIRS : (n + 1) * PAIRS, :].astype(jnp.bfloat16)
         for source, target in ((fs_ref, first_ref), (ls_ref, last_ref)):
@@ -237,7 +309,7 @@
             target[n] = source[base : base + RIM_ROWS, :].astype(jnp.bfloat16)
 
 
-def upward(values, basis, matrices):
+def upward(values, basis, links):
     return pl.pallas_call(
         up_kernel,
         name="upward",
@@ -245,7 +317,7 @@
             jax.ShapeDtypeStruct((N, PAIRS, 2 * K), jnp.bfloat16),
             jax.ShapeDtypeStruct((N, RIM_ROWS, 2 * K), jnp.bfloat16),
             jax.ShapeDtypeStruct((N, RIM_ROWS, 2 * K), jnp.bfloat16),
-            jax.ShapeDtypeStruct((N, 2 * K), jnp.bfloat16),
+            jax.ShapeDtypeStruct((N, N, 2 * K), jnp.bfloat16),
         ],
         in_specs=[vmem()] * 3,
         out_specs=[vmem()] * 4,
@@ -258,7 +330,7 @@
         cost_estimate=pl.CostEstimate(
             flops=300_000_000, bytes_accessed=3_000_000, transcendentals=0
         ),
-    )(values, basis, matrices)
+    )(values, basis, links)
 
 
 def down_kernel(
@@ -268,7 +340,7 @@
     tops_ref,
     a_ref,
     coupling_ref,
-    matrix_ref,
+    links_ref,
     basis_ref,
     near_ref,
     out_ref,
@@ -294,8 +366,8 @@
         if used < height:
             cf_ref[base + used : base + height, :] = jnp.zeros((height - used, 2 * K), jnp.float32)
     for q in range(subtrees // 2):
-        even = tops_ref[2 * q].astype(jnp.float32)
-        odd = tops_ref[2 * q + 1].astype(jnp.float32)
+        even = tops_ref[2 * q, 0].astype(jnp.float32)
+        odd = tops_ref[2 * q + 1, 0].astype(jnp.float32)
         at = PAIRS + 2 * RIM + 2 * q
         cf_ref[pl.ds(at, N, stride=height), :] = jnp.where(lower, even, even + odd)
         cf_ref[pl.ds(at + 1, N, stride=height), :] = odd
@@ -349,10 +421,10 @@
 
     last = field_of(PAIRS - 1)
     top = last[:, K : 2 * K].astype(jnp.bfloat16)
-    root = (last[:, 0:K] + dot(top, matrix_ref[0])).astype(jnp.bfloat16)
-    tiles = {0: field_of(0) + dot(root, children_of(matrix_ref, 0))}
+    root = (last[:, 0:K] + dot(top, links_ref[PAIRS - 1][:, 0:K])).astype(jnp.bfloat16)
+    tiles = {0: field_of(0) + dot(root, links_ref[0])}
     for j in range(B // 2 - 1):
-        both = push(tiles[j], links_of(matrix_ref, j))
+        both = push(tiles[j], links_of(links_ref, j))
         tiles[2 * j + 1] = field_of(2 * j + 1) + both[:N]
         tiles[2 * j + 2] = field_of(2 * j + 2) + both[N:]
     for i in range(B // 2):
@@ -362,7 +434,7 @@
             out_ref[:, lanes] = (near_ref[:, lanes] + both[h * N : (h + 1) * N]).astype(jnp.bfloat16)
 
 
-def downward(low, own, high, tops, counts, coupling, matrices, basis, near):
+def downward(low, own, high, tops, counts, coupling, links, basis, near):
     classes = counts.shape[0]
     height = counts.shape[2] // 2
     return pl.pallas_call(
@@ -382,7 +454,7 @@
         cost_estimate=pl.CostEstimate(
             flops=4_000_000_000, bytes_accessed=6_000_000, transcendentals=0
         ),
-    )(low, own, high, tops, counts, coupling, matrices, basis, near)
+    )(low, own, high, tops, counts, coupling, links, basis, near)
 
 
 def source_columns(far_src, top_src, position, subtrees, height):
@@ -434,7 +506,6 @@
     centre = jnp.stack(
         [box % ROW, box // ROW, jnp.full((B,), 0, jnp.int32) + position]
     ).astype(jnp.float32) + 0.5
-    local = coords.reshape(3, B, M) - centre[:, :, None]
     flat = coords - jnp.repeat(centre, M, axis=1)
     coarse = rounded(flat)
     rest = rounded(flat - coarse)
@@ -447,36 +518,13 @@
     for k in range(3):
         rows += [coarse[k], rest[k]]
     rows += [size_a, size_b, size_c, jnp.ones_like(size)]
-    rows += [jnp.zeros_like(size)] * 6
+    doubled = 2 * SCALE * flat
+    doubled_a = rounded(doubled)
+    doubled_b = rounded(doubled - doubled_a)
+    for k in range(3):
+        rows += [doubled_a[k], doubled_b[k]]
     packed = jnp.concatenate([values, jnp.stack(rows).astype(jnp.bfloat16)], axis=0)
-    forward = [(i, i + 1) for i in range(subtrees - 1)]
-    backward = [(i + 1, i) for i in range(subtrees - 1)]
-    from_low = lax.ppermute(packed, "leaf", forward)
-    from_high = lax.ppermute(packed, "leaf", backward)
-
-    moved = (
-        jnp.transpose(local, (1, 0, 2))[:, :, None, None, :]
-        - jnp.arange(-1, 2, dtype=jnp.float32)[None, None, :, None, None]
-    )
-    row = jnp.arange(16, dtype=jnp.int32)[None, None, None, :, None]
-    term = jnp.where(
-        row < 4,
-        2 * SCALE * moved,
-        -SCALE * moved * moved,
-    )
-    term_a = rounded(term)
-    term_b = rounded(term - term_a)
-    term_c = term - term_a - term_b
-    x_tiles = jnp.where(
-        (row < 2) | (row == 4),
-        term_a,
-        jnp.where((row < 4) | (row == 5), term_b, jnp.where(row == 6, term_c, 0.0)),
-    )
-    x_tiles = x_tiles.astype(jnp.bfloat16).reshape(B, 9, 16, M)
-
-    matrices = transfer.reshape(TB, K, K)
-    coupling_t = jnp.transpose(coupling.reshape(class_count, K, K), (0, 2, 1))
-
+    links, coupling_t = relay(transfer, coupling)
     columns = source_columns(far_src, top_src, position, subtrees, height)
     classes = by_parity(
         far_cls,
@@ -485,14 +533,19 @@
     )
     counts = class_counts(columns, classes, class_count, 2 * height)
 
-    whole_basis, counts, x_tiles = lax.optimization_barrier((whole_basis, counts, x_tiles))
+    packed, counts, links = lax.optimization_barrier((packed, counts, links))
+    forward = [(i, i + 1) for i in range(subtrees - 1)]
+    backward = [(i + 1, i) for i in range(subtrees - 1)]
+    from_low = lax.ppermute(packed, "leaf", forward)
+    from_high = lax.ppermute(packed, "leaf", backward)
+    whole_basis, counts, links = lax.optimization_barrier((whole_basis, counts, links))
     basis_pairs = whole_basis.reshape(B // 2, 2 * K, M)
-    coefs, first, last, root = upward(values, basis_pairs, matrices)
+    coefs, first, last, root = upward(values, basis_pairs, links)
     tops = lax.all_gather(root, "leaf", axis=0)
     low = lax.ppermute(last, "leaf", forward)
     high = lax.ppermute(first, "leaf", backward)
-    near = near_field(near_src, x_tiles, from_low, packed, from_high)
-    return downward(low, coefs, high, tops, counts, coupling_t, matrices, basis_pairs, near)
+    near = near_field(near_src, from_low, packed, from_high)
+    return downward(low, coefs, high, tops, counts, coupling_t, links, basis_pairs, near)
 
 
 def solution(mesh):

time: 136 us -> 159 us (1.17)
  waiting for transfers between devices: 0.03 us -> 19.5 us
  Pallas kernels: 52.9 us -> 60.1 us
  other arithmetic: 6.83 us -> 2.81 us
  local copies, waits for them, and re-layouts: 16.5 us -> 14.7 us
  blocking collectives: 33 us -> 34.8 us
    ppermute x1, waiting for transfers between devices: 0.01 us -> 19.5 us  [per_device(): from_low = lax.ppermute(packed, 'leaf', forward)]
    reshape x3 -> x0, local copies, waits for them, and re-layouts: 6.57 us -> none  [the longest x1 4.24 us: per_device(): matrices = transfer.reshape(TB, K, K)]
    pallas_call x1, Pallas kernels: 37.8 us -> 43 us  [near_field(): pl.pallas_call(near_kernel, name='near_field', out_shape=jax.ShapeDtypeSt...]
    convert_element_type x1 -> x0, other arithmetic: 4.1 us -> none  [per_device(): x_tiles = x_tiles.astype(jnp.bfloat16).reshape(B, 9, 16, M)]
    pallas_call x0 -> x1, Pallas kernels: none -> 2.13 us  [relay(): pl.pallas_call(relay_kernel, name='relay', out_shape=[jax.ShapeDtypeStruc...]
    mul x2 -> x0, local copies, waits for them, and re-layouts: 2.06 us -> none  [per_device(): term = jnp.where(row < 4, 2 * SCALE * moved, -SCALE * moved * moved)]
    unnamed x30 -> x34, local copies, waits for them, and re-layouts: 4.24 us -> 6.17 us
    all_gather x1, blocking collectives: 33 us -> 34.8 us  [per_device(): tops = lax.all_gather(root, 'leaf', axis=0)]
  transfers between devices with their start and end apart: 5 -> 5, of which waited for: 0 -> 1; matrix products, arithmetic and copies ran while one was open for 13% -> 1% of each run, Pallas kernels for 31% -> 27%
where the time goes in v3:
time: 159 us; the launch traced here: 158 us
  Pallas kernels  60.1 us (38%)
  blocking collectives  34.8 us (22%)
  waiting for transfers between devices  19.5 us (12%)
  local copies, waits for them, and re-layouts  14.7 us (9%)
  between operations  13.7 us (9%)
  starting transfers between devices  12.7 us (8%)
  other arithmetic  2.81 us (2%)
    pallas_call x1, Pallas kernels, near_field(): pl.pallas_call(near_kernel, name='near_field', out_shape=jax.ShapeDtypeSt...  43 us
    all_gather x1, blocking collectives, per_device(): tops = lax.all_gather(root, 'leaf', axis=0)  34.8 us
    ppermute x1, waiting for transfers between devices, per_device(): from_low = lax.ppermute(packed, 'leaf', forward)  19.5 us
    pallas_call x1, Pallas kernels, downward(): pl.pallas_call(down_kernel, name='downward', out_shape=jax.ShapeDtypeStru...  10.4 us
    unnamed x34, local copies, waits for them, and re-layouts  6.17 us
    ppermute x1, starting transfers between devices, per_device(): from_low = lax.ppermute(packed, 'leaf', forward)  5.67 us
    ppermute x1, starting transfers between devices, per_device(): low = lax.ppermute(last, 'leaf', forward)  4.45 us
  transfers between devices with their start and end apart: 5, of which 1 were waited for; matrix products, arithmetic and copies ran while one was open for 1% of the time, Pallas kernels for 27%

profile of v3, /device:TPU:0, one launch (start us, length us, event | category | flops | bytes accessed | tf_op | source)
XLA Modules:
  0.0 158.2 jit_solution(17814949135477520207)
XLA Ops:
  6.5 0.0 all-gather.3.cloned.1.call-start
  6.6 0.8 constant_dynamic-slice_fusion.1
  7.3 0.1 copy.50
  7.4 0.1 copy.49
  7.5 0.8 add_select_fusion.5
  8.3 0.8 fusion.13
  9.1 0.1 copy.36
  9.3 0.1 fusion.29
  9.3 0.1 copy.37
  9.4 0.1 copy.39
  9.5 0.1 pad_add_fusion
  9.6 0.1 copy.46.col_ref
  9.7 0.1 copy.51
  9.7 0.1 copy.52
  9.8 0.8 slice.93
  10.6 0.1 copy.41
  10.8 0.1 fusion.28
  10.8 0.1 copy.42
  10.9 0.1 copy.44
  11.0 0.1 pad_add_fusion.1
  11.1 0.1 copy.47.cls_ref
  11.2 0.1 pad.10.clone
  11.2 0.1 fusion.22
  11.3 0.1 broadcast_bitcast_fusion
  11.4 0.0 copy-done.13
  11.4 0.1 fusion.3
  11.6 0.0 copy-start.1
  11.6 0.0 copy-start.4
  11.6 0.1 reduce-precision_convert_fusion
  11.7 0.1 fusion.4
  11.8 0.7 fusion.25
  12.5 0.7 fusion.26
  13.2 0.7 fusion.27
  13.9 0.7 fusion.24
  14.6 0.7 reduce-precision_convert_fusion.2
  15.3 2.6 %class_counts.1.a_ref = bf16[24,128,256]{2,1,0:T(8,128)(2,1)S(1)} custom-call(s32[128,24]{1,0:T(8,128)S(1)} %copy.46.col_ref, s32[128,24]{1,0:T(8,128)S(1)} %copy.47.cls_ref), custom_call_target="tpu_custom_call" | custom-call | flops 1000 | bytes 100000 | tf_op jit(solution)/shard_map/class_counts/pallas_call | solution.py:249
  17.9 0.0 copy-done.1
  17.9 0.0 copy-done.4
  17.9 0.0 copy-start.7
  17.9 2.1 %relay.1 = (bf16[64,64,128]{2,1,0:T(8,128)(2,1)S(1)}, bf16[24,64,64]{2,1,0:T(8,128)(2,1)S(1)}) custom-call(bf16[127,4096]{1,0:T(8,128)(2,1)S(1)} %copy-done.1, bf16[24,4096]{1,0:T(8,128)(2,1)S(1)} %copy-done.4), custom_call_target="tpu_custom_call" | custom-call | flops 1000 | bytes 100000 | tf_op jit(solution)/shard_map/relay/pallas_call | solution.py:195
  20.1 0.8 copy-done.5
  20.8 0.6 stack_broadcast_in_dim.3
  21.5 2.5 %concatenate.10.own_ref = bf16[32,8192]{1,0:T(8,128)(2,1)S(1)} concatenate(bf16[16,8192]{1,0:T(8,128)(2,1)S(1)} %copy-done, bf16[1,8192]{1,0:T(2,128)(2,1)} %get-tuple-element.50, bf16[1,8192]{1,0:T(2,128)(2,1)} %get-tuple-element.47, bf16[1,8192]{1,0:T(2,128)(2,1)} %get-tuple-element.49, bf16[1,8192]{1,0:T(2,128)(2,1)} %get-tuple-element.46, bf16[1,8192]{1,0:T(2,128)(2,1)} %get-tuple-element.48, ...), dimensions={0} | concatenate | bytes 1048576 | tf_op jit(solution)/shard_map/concatenate | solution.py:526
  24.0 5.7 %collective-permute-start.2 = (bf16[32,8192]{1,0:T(8,128)(2,1)S(1)}, bf16[32,8192]{1,0:T(8,128)(2,1)}, u32[]{:S(2)}, u32[]{:S(2)}) collective-permute-start(bf16[32,8192]{1,0:T(8,128)(2,1)S(1)} %concatenate.10.own_ref), channel_id=1, source_target_pairs={{0,4},{4,8},{8,12},{12,16},{16,20},{20,24},{24,28},{1,5},{5,9},{9,... | collective-permute-start | bytes 1572872 | tf_op jit(solution)/shard_map/ppermute | solution.py:539
  29.7 1.3 collective-permute-start.3
  31.0 0.0 all-gather.3.cloned.1.call-update
  31.0 0.8 copy.48.near_ref
  31.8 19.5 %collective-permute-done.2.low_ref = bf16[32,8192]{1,0:T(8,128)(2,1)} collective-permute-done((bf16[32,8192]{1,0:T(8,128)(2,1)S(1)}, bf16[32,8192]{1,0:T(8,128)(2,1)}, u32[]{:S(2)}, u32[]{:S(2)}) %collective-permute-start.2) | collective-permute-done | bytes 524320 | tf_op jit(solution)/shard_map/ppermute | solution.py:539
  51.3 0.0 collective-permute-done.3.high_ref
  51.3 0.7 copy-done.8
  52.0 0.7 copy-done.9
  52.7 0.7 copy-done.10
  53.4 43.0 %near_field.1.near_ref = f32[16,8192]{1,0:T(8,128)S(1)} custom-call(s32[64,27]{1,0:T(8,128)S(1)} %copy.48.near_ref, bf16[32,8192]{1,0:T(8,128)(2,1)} %collective-permute-done.2.low_ref, bf16[32,8192]{1,0:T(8,128)(2,1)S(1)} %concatenate.10.own_ref, bf16[32,8192]{1,0:T(8,128)(2,1)} %collective-permute-done.3.high_ref, bf16[32,128]{1,0:T(8,128)(2,1)S(1)} %copy-done.10, ...), custom_call_target="tpu_custom_call" | custom-call | flops 20000000000 | bytes 5000000 | tf_op jit(solution)/shard_map/near_field/pallas_call | solution.py:153
  96.4 0.8 copy-done.11
  97.2 1.2 copy-done.2
  98.4 2.0 %upward.1 = (bf16[16,64,128]{2,1,0:T(8,128)(2,1)S(1)}, bf16[16,32,128]{2,1,0:T(8,128)(2,1)S(1)}, bf16[16,32,128]{2,1,0:T(8,128)(2,1)S(1)}, bf16[16,16,128]{2,1,0:T(8,128)(2,1)S(1)}) custom-call(bf16[16,8192]{1,0:T(8,128)(2,1)S(1)} %copy-done, bf16[32,128,128]{2,1,0:T(8,128)(2,1)S(1)} %bitcast.12, bf16[64,64,128]{2,1,0:T(8,128)(2,1)S(1)} %get-tuple-element.21.links_ref), custom_call_target="tpu_custom_call" | custom-call | flops 300000000 | bytes 3000000 | tf_op jit(solution)/shard_map/upward/pallas_call | solution.py:313
  100.5 4.4 %collective-permute-start = (bf16[16,32,128]{2,1,0:T(8,128)(2,1)S(1)}, bf16[16,32,128]{2,1,0:T(8,128)(2,1)S(1)}, u32[]{:S(2)}, u32[]{:S(2)}) collective-permute-start(bf16[16,32,128]{2,1,0:T(8,128)(2,1)S(1)} %get-tuple-element.22), channel_id=1, source_target_pairs={{0,4},{4,8},{8,12},{12,16},{16,20},{20,24},{24,28},{1,5},{5,9},{9,... | collective-permute-start | bytes 393224 | tf_op jit(solution)/shard_map/ppermute | solution.py:545
  104.9 1.3 collective-permute-start.1
  106.2 34.8 %all-gather = bf16[128,16,128]{2,1,0:T(8,128)(2,1)S(1)} all-gather(bf16[16,16,128]{2,1,0:T(8,128)(2,1)S(1)} %get-tuple-element.25), channel_id=2, replica_groups=mesh['leaf'=8,'vec'=4] {'leaf'}, dimensions={0}, use_global_device_ids=true | all-gather | bytes 589824 | tf_op jit(solution)/shard_map/all_gather | solution.py:544
  141.0 0.0 collective-permute-done.low_ref
  141.0 0.0 collective-permute-done.1.high_ref
  141.0 0.0 copy-done.6
  141.0 0.0 copy-done.12
  141.0 10.4 %downward.1 = bf16[16,8192]{1,0:T(8,128)(2,1)} custom-call(bf16[16,32,128]{2,1,0:T(8,128)(2,1)S(1)} %collective-permute-done.low_ref, bf16[16,64,128]{2,1,0:T(8,128)(2,1)S(1)} %get-tuple-element.23.own_ref, bf16[16,32,128]{2,1,0:T(8,128)(2,1)S(1)} %collective-permute-done.1.high_ref, bf16[8,16,16,128]{3,2,1,0:T(8,128)(2,1)S(1)} %bitcast.14, ...), custom_call_target="tpu_custom_call" | custom-call | flops 4000000000 | bytes 6000000 | tf_op jit(solution)/shard_map/downward/pallas_call | solution.py:440
  (20 shorter events, 0.1 us)
Async XLA Ops:
  6.5 4.9 %copy-start.13 = (f32[3,8192]{1,0:T(4,128)S(1)}, f32[3,8192]{1,0:T(4,128)}, u32[]{:S(2)}) copy-start(f32[3,8192]{1,0:T(4,128)} %param.15) | copy-start | bytes 294916
  6.5 90.7 %all-gather.3.cloned.1.call-start = ((), (), s32[]{:S(2)}) async-start(), calls=%async_computation | async-start | bytes 1310720 | tf_op jit(solution)/shard_map/all_gather | solution.py:503
  11.6 6.4 %copy-start.1 = (bf16[127,4096]{1,0:T(8,128)(2,1)S(1)}, bf16[127,4096]{1,0:T(8,128)(2,1)}, u32[]{:S(2)}) copy-start(bf16[127,4096]{1,0:T(8,128)(2,1)} %transfer_ref.1) | copy-start | bytes 3121156
  11.6 6.4 %copy-start.4 = (bf16[24,4096]{1,0:T(8,128)(2,1)S(1)}, bf16[24,4096]{1,0:T(8,128)(2,1)}, u32[]{:S(2)}) copy-start(bf16[24,4096]{1,0:T(8,128)(2,1)} %coupling_ref.1) | copy-start | bytes 589828
  14.6 6.9 %copy-start = (bf16[16,8192]{1,0:T(8,128)(2,1)S(1)}, bf16[16,8192]{1,0:T(8,128)(2,1)}, u32[]{:S(2)}) copy-start(bf16[16,8192]{1,0:T(8,128)(2,1)} %values_ref.1) | copy-start | bytes 786436
  17.9 33.4 %copy-start.7 = (bf16[27,16,128]{2,1,0:T(8,128)(2,1)S(1)}, bf16[27,16,128]{2,1,0:T(8,128)(2,1)}, u32[]{:S(2)}) copy-start(bf16[27,16,128]{2,1,0:T(8,128)(2,1)} %constant.159.clone.factor_ref) | copy-start | bytes 331780
  20.1 0.8 copy-start.5
  24.0 27.3 %collective-permute-start.2 = (bf16[32,8192]{1,0:T(8,128)(2,1)S(1)}, bf16[32,8192]{1,0:T(8,128)(2,1)}, u32[]{:S(2)}, u32[]{:S(2)}) collective-permute-start(bf16[32,8192]{1,0:T(8,128)(2,1)S(1)} %concatenate.10.own_ref), channel_id=1, source_target_pairs={{0,4},{4,8},{8,12},{12,16},{16,20},{20,24},{24,28},{1,5},{5,9},{9,... | collective-permute-start | bytes 1572872 | tf_op jit(solution)/shard_map/ppermute | solution.py:539
  29.7 21.6 %collective-permute-start.3 = (bf16[32,8192]{1,0:T(8,128)(2,1)S(1)}, bf16[32,8192]{1,0:T(8,128)(2,1)}, u32[]{:S(2)}, u32[]{:S(2)}) collective-permute-start(bf16[32,8192]{1,0:T(8,128)(2,1)S(1)} %concatenate.10.own_ref), channel_id=1, source_target_pairs={{4,0},{8,4},{12,8},{16,12},{20,16},{24,20},{28,24},{5,1},{9,5},{13... | collective-permute-start | bytes 1572872 | tf_op jit(solution)/shard_map/ppermute | solution.py:540
  51.3 0.7 copy-start.8
  52.0 0.7 copy-start.9
  52.7 0.7 copy-start.10
  96.4 0.8 copy-start.11
  97.2 1.2 copy-start.2
  98.4 42.6 %copy-start.3 = (bf16[64,64,128]{2,1,0:T(8,128)(2,1)S(1)}, bf16[64,64,128]{2,1,0:T(8,128)(2,1)}, u32[]{:S(2)}) copy-start(bf16[64,64,128]{2,1,0:T(8,128)(2,1)} %all-gather.3.cloned.1.call-done) | copy-start | bytes 3145732
  98.4 42.6 %copy-start.6 = (bf16[24,64,64]{2,1,0:T(8,128)(2,1)S(1)}, bf16[24,64,64]{2,1,0:T(8,128)(2,1)}, u32[]{:S(2)}) copy-start(bf16[24,64,64]{2,1,0:T(8,128)(2,1)} %copy-done.5) | copy-start | bytes 589828
  98.4 42.6 %copy-start.12 = (f32[16,8192]{1,0:T(8,128)S(1)}, f32[16,8192]{1,0:T(8,128)}, u32[]{:S(2)}) copy-start(f32[16,8192]{1,0:T(8,128)} %copy-done.11) | copy-start | bytes 1572868
  100.5 40.5 %collective-permute-start = (bf16[16,32,128]{2,1,0:T(8,128)(2,1)S(1)}, bf16[16,32,128]{2,1,0:T(8,128)(2,1)S(1)}, u32[]{:S(2)}, u32[]{:S(2)}) collective-permute-start(bf16[16,32,128]{2,1,0:T(8,128)(2,1)S(1)} %get-tuple-element.22), channel_id=1, source_target_pairs={{0,4},{4,8},{8,12},{12,16},{16,20},{20,24},{24,28},{1,5},{5,9},{9,... | collective-permute-start | bytes 393224 | tf_op jit(solution)/shard_map/ppermute | solution.py:545
  104.9 36.1 %collective-permute-start.1 = (bf16[16,32,128]{2,1,0:T(8,128)(2,1)S(1)}, bf16[16,32,128]{2,1,0:T(8,128)(2,1)S(1)}, u32[]{:S(2)}, u32[]{:S(2)}) collective-permute-start(bf16[16,32,128]{2,1,0:T(8,128)(2,1)S(1)} %get-tuple-element.24), channel_id=1, source_target_pairs={{4,0},{8,4},{12,8},{16,12},{20,16},{24,20},{28,24},{5,1},{9,5},{13... | collective-permute-start | bytes 393224 | tf_op jit(solution)/shard_map/ppermute | solution.py:546
Sparse Core Ops, SparseCore 0:
  31.1 19.1 all-gather.2

commit v4 on v3

--- a/solution.py
+++ b/solution.py
@@ -1,5 +1,3 @@
-import math
-
 import jax
 import jax.numpy as jnp
 import numpy as np
@@ -18,7 +16,6 @@
 PAIRS = 64
 RIM = 28
 
-SCALE = math.log2(math.e) / 0.2
 AMPLITUDE = 0.3
 DEAD = -1000.0
 
@@ -40,110 +37,103 @@
 
 
 def near_tables():
-    def split(value, parts):
-        out = []
-        for _ in range(parts):
-            part = float(np.float32(np.asarray(value).astype(jnp.bfloat16)))
-            out.append(part)
-            value -= part
-        return out
-
-    one = 9
-    lanes = []
+    one = 8
+    source = np.zeros((32, 128), np.float32)
+    target = np.zeros((11 * 16, 32), np.float32)
+
+    def lane(at, y):
+        for half in range(2):
+            source[(8 * half + y) if y < one else 16, 64 * half + at] = 1
+
+    def row(tile, at, x, factor):
+        target[16 * tile + at, x if x < one else 16] = factor
+
     for k in range(3):
-        high, rest = 2 * k, 2 * k + 1
-        x_high, x_rest = 10 + 2 * k, 11 + 2 * k
-        for y in (high, rest):
-            for x in (x_high, x_rest):
-                lanes.append((y, None, x, 1.0))
-            for part in split(-2 * SCALE, 2):
-                lanes.append((y, k, one, part))
-        for x in (x_high, x_rest):
-            lanes.append((one, k, x, 1.0))
-    for row in (6, 7, 8):
-        lanes.append((one, None, row, 1.0))
-        lanes.append((row, None, one, 1.0))
-    for part in split(-SCALE, 3):
-        lanes.append((one, 3, one, part))
-    lanes.append((one, 4, one, DEAD))
-    source = np.zeros((32, 128), np.float32)
-    target = np.zeros((64, 16), np.float32)
-    factor = np.zeros((27, 16, 128), np.float32)
-    dead = np.zeros((4, 16, 128), np.float32)
-    for lane, (y, kind, x, part) in enumerate(lanes):
-        target[lane, x] = part
-        for half in range(2):
-            at = 64 * half + lane
-            source[16 * half + y, at] = 1
-            for slot in range(27):
-                step = (slot % 3 - 1, slot // 3 % 3 - 1, slot // 9 - 1)
-                if kind is None:
-                    factor[slot, :, at] = 1
-                elif kind < 3:
-                    factor[slot, :, at] = step[kind]
-                elif kind == 3:
-                    factor[slot, :, at] = sum(d * d for d in step)
-            if kind == 4:
-                for flags in range(4):
-                    dead[flags, :, at] = flags >> half & 1
-    return [jnp.asarray(x, jnp.bfloat16) for x in (source, target, factor, dead)]
+        parts = [(x, p) for x in (2 * k, 2 * k + 1) for p in (8, 2)]
+        terms = [(y, x, p, None) for y in (2 * k, 2 * k + 1) for x, p in parts]
+        terms += [(y, one, -10, 1) for y in (2 * k, 2 * k + 1)]
+        terms += [(one, x, p, 1) for x, p in parts]
+        terms += [(one, one, -5, 2)]
+        for at, (y, x, factor, power) in enumerate(terms):
+            lane(16 * k + at, y)
+            for step in range(3):
+                scale = 1 if power is None else (step - 1) ** power
+                row(3 * k + step, at, x, factor * scale)
+    for at, (y, x) in enumerate(((6, one), (7, one), (one, 6), (one, 7))):
+        lane(48 + at, y)
+        for tile in (9, 10):
+            row(tile, at, x, 1)
+    lane(52, one)
+    row(10, 4, one, DEAD)
+    return [jnp.asarray(x, jnp.bfloat16) for x in (source, target)]
 
 
 def near_kernel(
-    near_ref, low_ref, own_ref, high_ref, source_ref, target_ref, factor_ref, dead_ref, out_ref, yp_ref
+    near_ref, low_ref, own_ref, high_ref, source_ref, target_ref, out_ref, yp_ref, x_ref
 ):
     layers = (low_ref, own_ref, high_ref)
+    ones = jnp.ones((16, M), jnp.float32)
 
     def at(u):
         return pl.ds(pl.multiple_of(jnp.clip(u, 0, B - 1) * M, M), M)
 
+    def points(ref, first, second):
+        two = [ref[:, at(u)].astype(jnp.float32)[16:24] for u in (first, second)]
+        return jnp.concatenate(two + [ones], axis=0).astype(jnp.bfloat16)
+
     for l, src in enumerate(layers):
 
         def features(u, carry, l=l, src=src):
-            both = jnp.concatenate([src[16:32, at(u - 1)], src[16:32, at(u)]], axis=0)
-            yp_ref[l, u] = dot(both, source_ref[...], TN).astype(jnp.bfloat16)
+            yp_ref[l, u] = dot(points(src, u - 1, u), source_ref[...], TN).astype(jnp.bfloat16)
             return carry
 
-        lax.fori_loop(0, B + 1, features, 0, unroll=5)
+        lax.fori_loop(0, B + 1, features, 0, unroll=13)
+
+    def targets(t, carry):
+        x_ref[t] = dot(target_ref[...], points(own_ref, t, t)).astype(jnp.bfloat16)
+        return carry
+
+    lax.fori_loop(0, B, targets, 0, unroll=8)
 
     zero = jnp.zeros((64, M), jnp.bfloat16)
 
-    def target(t):
-        return dot(target_ref[...], own_ref[16:32, at(t)]).astype(jnp.bfloat16)
-
-    def pair(t, steps):
+    def weights(t, a, b, c, slot):
+        last = jnp.where(near_ref[t, slot] >= 0, 9, 10) * 16
+        tiles = [x_ref[t, 16 * i : 16 * (i + 1), :] for i in (a, 3 + b, 6 + c)]
+        return jnp.concatenate(tiles + [x_ref[t, pl.ds(pl.multiple_of(last, 16), 16), :]], axis=0)
+
+    def kernel(t, a, b, c):
+        slot = 9 * c + 3 * b + a
+        u = t + (b - 1) * ROW + a - 1
         w = jnp.concatenate(
             [
-                jnp.concatenate([target(t), zero], axis=1),
-                jnp.concatenate([zero, target(t + 1)], axis=1),
+                jnp.concatenate([weights(t, a, b, c, slot), zero], axis=1),
+                jnp.concatenate([zero, weights(t + 1, a, b, c, slot)], axis=1),
             ],
             axis=0,
         )
-        kernels, vectors = [], []
-        for c in range(3):
-            src = layers[c]
-            for b in steps:
-                for a in range(3):
-                    slot = 9 * c + 3 * b + a
-                    u = t + (b - 1) * ROW + a - 1
-                    flags = jnp.where(near_ref[t, slot] < 0, 1, 0) + jnp.where(
-                        near_ref[t + 1, slot] < 0, 2, 0
-                    )
-                    factor = factor_ref[slot] + dead_ref[flags]
-                    left = yp_ref[c, u + 1] * jnp.concatenate([factor] * 8, axis=0)
-                    kernels.append(jnp.exp2(dot(left, w)).astype(jnp.bfloat16))
-                    vectors.append(jnp.concatenate([src[0:16, at(u)], src[0:16, at(u + 1)]], axis=0))
-        total = dot(jnp.concatenate(vectors, axis=1), jnp.concatenate(kernels, axis=0))
-        out_ref[:, at(t)] = AMPLITUDE * total[0:16, 0:M]
-        out_ref[:, at(t + 1)] = AMPLITUDE * total[16:32, M : 2 * M]
+        src = layers[c]
+        vectors = jnp.concatenate([src[0:16, at(u)], src[0:16, at(u + 1)]], axis=0)
+        return vectors, jnp.exp(dot(yp_ref[c, u + 1], w)).astype(jnp.bfloat16)
 
     rows = B // ROW
     for first, last, steps in ((0, 1, (1, 2)), (1, rows - 1, (0, 1, 2)), (rows - 1, rows, (0, 1))):
-
-        def step(q, carry, first=first, steps=steps):
-            t = first * ROW + 4 * q
-            pair(t, steps)
-            pair(t + 2, steps)
+        slots = [(a, b, c) for c in range(3) for b in steps for a in range(3)]
+        groups = [slots[i : i + 2] for i in range(0, len(slots), 2)]
+
+        def step(q, carry, first=first, groups=groups):
+            pairs = [first * ROW + 4 * q, first * ROW + 4 * q + 2]
+            totals = [jnp.zeros((32, 2 * M), jnp.float32) for _ in pairs]
+            for group in groups:
+                for p, t in enumerate(pairs):
+                    both = [kernel(t, *slot) for slot in group]
+                    totals[p] += dot(
+                        jnp.concatenate([v for v, _ in both], axis=1),
+                        jnp.concatenate([k for _, k in both], axis=0),
+                    )
+            for p, t in enumerate(pairs):
+                out_ref[:, at(t)] = AMPLITUDE * totals[p][0:16, 0:M]
+                out_ref[:, at(t + 1)] = AMPLITUDE * totals[p][16:32, M : 2 * M]
             return carry
 
         lax.fori_loop(0, (last - first) * ROW // 4, step, 0)
@@ -154,9 +144,12 @@
         near_kernel,
         name="near_field",
         out_shape=jax.ShapeDtypeStruct((N, B * M), jnp.float32),
-        in_specs=[pl.BlockSpec(memory_space=pltpu.SMEM)] + [vmem()] * 7,
+        in_specs=[pl.BlockSpec(memory_space=pltpu.SMEM)] + [vmem()] * 5,
         out_specs=vmem(),
-        scratch_shapes=[pltpu.VMEM((3, B + 1, M, M), jnp.bfloat16)],
+        scratch_shapes=[
+            pltpu.VMEM((3, B + 1, M, M), jnp.bfloat16),
+            pltpu.VMEM((B, 11 * 16, M), jnp.bfloat16),
+        ],
         compiler_params=pltpu.CompilerParams(vmem_limit_bytes=40 << 20),
         cost_estimate=pl.CostEstimate(
             flops=20_000_000_000, bytes_accessed=5_000_000, transcendentals=28_000_000
@@ -300,7 +293,7 @@
     last = jnp.concatenate([root.astype(jnp.float32), up], axis=1)
     keep(PAIRS - 1, last)
     root_ref[0] = last.astype(jnp.bfloat16)
-    root_ref[1:] = jnp.zeros((N - 1, N, 2 * K), jnp.bfloat16)
+    root_ref[1:] = jnp.zeros((2 * N - 1, N, 2 * K), jnp.bfloat16)
     for n in range(N):
         out_ref[n] = cs_ref[n * PAIRS : (n + 1) * PAIRS, :].astype(jnp.bfloat16)
         for source, target in ((fs_ref, first_ref), (ls_ref, last_ref)):
@@ -317,7 +310,7 @@
             jax.ShapeDtypeStruct((N, PAIRS, 2 * K), jnp.bfloat16),
             jax.ShapeDtypeStruct((N, RIM_ROWS, 2 * K), jnp.bfloat16),
             jax.ShapeDtypeStruct((N, RIM_ROWS, 2 * K), jnp.bfloat16),
-            jax.ShapeDtypeStruct((N, N, 2 * K), jnp.bfloat16),
+            jax.ShapeDtypeStruct((2 * N, N, 2 * K), jnp.bfloat16),
         ],
         in_specs=[vmem()] * 3,
         out_specs=[vmem()] * 4,
@@ -510,19 +503,13 @@
     coarse = rounded(flat)
     rest = rounded(flat - coarse)
     held = coarse + rest
-    size = -SCALE * (held[0] ** 2 + held[1] ** 2 + held[2] ** 2)
+    size = -5.0 * (held[0] ** 2 + held[1] ** 2 + held[2] ** 2)
     size_a = rounded(size)
-    size_b = rounded(size - size_a)
-    size_c = size - size_a - size_b
+    size_b = size - size_a
     rows = []
     for k in range(3):
         rows += [coarse[k], rest[k]]
-    rows += [size_a, size_b, size_c, jnp.ones_like(size)]
-    doubled = 2 * SCALE * flat
-    doubled_a = rounded(doubled)
-    doubled_b = rounded(doubled - doubled_a)
-    for k in range(3):
-        rows += [doubled_a[k], doubled_b[k]]
+    rows += [size_a, size_b]
     packed = jnp.concatenate([values, jnp.stack(rows).astype(jnp.bfloat16)], axis=0)
     links, coupling_t = relay(transfer, coupling)
     columns = source_columns(far_src, top_src, position, subtrees, height)
@@ -533,18 +520,18 @@
     )
     counts = class_counts(columns, classes, class_count, 2 * height)
 
-    packed, counts, links = lax.optimization_barrier((packed, counts, links))
     forward = [(i, i + 1) for i in range(subtrees - 1)]
     backward = [(i + 1, i) for i in range(subtrees - 1)]
     from_low = lax.ppermute(packed, "leaf", forward)
     from_high = lax.ppermute(packed, "leaf", backward)
-    whole_basis, counts, links = lax.optimization_barrier((whole_basis, counts, links))
     basis_pairs = whole_basis.reshape(B // 2, 2 * K, M)
     coefs, first, last, root = upward(values, basis_pairs, links)
     tops = lax.all_gather(root, "leaf", axis=0)
     low = lax.ppermute(last, "leaf", forward)
     high = lax.ppermute(first, "leaf", backward)
+    near_src, coefs = lax.optimization_barrier((near_src, coefs))
     near = near_field(near_src, from_low, packed, from_high)
+    tops = lax.slice_in_dim(tops, 0, 1, axis=1)
     return downward(low, coefs, high, tops, counts, coupling_t, links, basis_pairs, near)
 
 

time: 159 us -> 126 us (0.79)
  blocking collectives: 34.8 us -> 0 us
  Pallas kernels: 60.1 us -> 73.2 us
  waiting for transfers between devices: 19.5 us -> 11.3 us
    all_gather x1 -> x0, blocking collectives: 34.8 us -> none  [per_device(): tops = lax.all_gather(root, 'leaf', axis=0)]
    ppermute x1, waiting for transfers between devices: 19.5 us -> 0.01 us  [per_device(): from_low = lax.ppermute(packed, 'leaf', forward)]
    pallas_call x1, Pallas kernels: 43 us -> 54.3 us  [near_field(): pl.pallas_call(near_kernel, name='near_field', out_shape=jax.ShapeDtypeSt...]
    all_gather x1, waiting for transfers between devices: 0.01 us -> 11.3 us  [per_device(): whole_basis = lax.all_gather(basis, 'vec', axis=0, tiled=True)]
    unnamed x34 -> x39, local copies, waits for them, and re-layouts: 6.17 us -> 8.66 us
  transfers between devices with their start and end apart: 5 -> 6, of which waited for: 1 -> 1; matrix products, arithmetic and copies ran while one was open for 1% -> 3% of each run, Pallas kernels for 27% -> 49%
where the time goes in v4:
time: 126 us; the launch traced here: 125 us
  Pallas kernels  73.2 us (58%)
  local copies, waits for them, and re-layouts  13.7 us (11%)
  between operations  13.7 us (11%)
  starting transfers between devices  11.9 us (9%)
  waiting for transfers between devices  11.3 us (9%)
  other arithmetic  1.58 us (1%)
    pallas_call x1, Pallas kernels, near_field(): pl.pallas_call(near_kernel, name='near_field', out_shape=jax.ShapeDtypeSt...  54.3 us
    pallas_call x1, Pallas kernels, downward(): pl.pallas_call(down_kernel, name='downward', out_shape=jax.ShapeDtypeStru...  11.4 us
    all_gather x1, waiting for transfers between devices, per_device(): whole_basis = lax.all_gather(basis, 'vec', axis=0, tiled=True)  11.3 us
    unnamed x39, local copies, waits for them, and re-layouts  8.66 us
    ppermute x1, starting transfers between devices, per_device(): from_low = lax.ppermute(packed, 'leaf', forward)  5.62 us
    ppermute x1, starting transfers between devices, per_device(): low = lax.ppermute(last, 'leaf', forward)  3.52 us
    pallas_call x1, Pallas kernels, upward(): pl.pallas_call(up_kernel, name='upward', out_shape=[jax.ShapeDtypeStruct(...  2.69 us
    pallas_call x1, Pallas kernels, class_counts(): pl.pallas_call(counts_kernel, name='class_counts', out_shape=jax.ShapeDty...  2.64 us
  transfers between devices with their start and end apart: 6, of which 1 were waited for; matrix products, arithmetic and copies ran while one was open for 3% of the time, Pallas kernels for 49%

profile of v4, /device:TPU:0, one launch (start us, length us, event | category | flops | bytes accessed | tf_op | source)
XLA Modules:
  0.0 125.4 jit_solution(13002605128448192112)
XLA Ops:
  6.5 0.0 all-gather.4.cloned.1.call-start
  6.6 0.1 pad.2.clone
  6.6 0.1 fusion.20
  6.7 0.1 broadcast_bitcast_fusion
  6.8 0.0 copy-start.16
  6.8 1.0 reduce-precision_add_fusion
  7.8 0.1 fusion.22
  7.9 0.0 copy-start.1
  7.9 0.0 copy-start.6
  7.9 0.1 fusion.23
  8.0 0.1 fusion.2
  8.2 1.5 %concatenate.12.own_ref = bf16[24,8192]{1,0:T(8,128)(2,1)S(1)} concatenate(bf16[16,8192]{1,0:T(8,128)(2,1)} %values_ref.1, bf16[1,8192]{1,0:T(2,128)(2,1)S(1)} %get-tuple-element.33, bf16[1,8192]{1,0:T(2,128)(2,1)S(1)} %get-tuple-element.30, bf16[1,8192]{1,0:T(2,128)(2,1)S(1)} %get-tuple-element.32, bf16[1,8192]{1,0:T(2,128)(2,1)S(1)} %get-tuple-element.29, ...), dimensions={0} | concatenate | bytes 786432 | tf_op jit(solution)/shard_map/concatenate | solution.py:513
  9.7 5.6 %collective-permute-start.2 = (bf16[24,8192]{1,0:T(8,128)(2,1)S(1)}, bf16[24,8192]{1,0:T(8,128)(2,1)}, u32[]{:S(2)}, u32[]{:S(2)}) collective-permute-start(bf16[24,8192]{1,0:T(8,128)(2,1)S(1)} %concatenate.12.own_ref), channel_id=1, source_target_pairs={{0,4},{4,8},{8,12},{12,16},{16,20},{20,24},{24,28},{1,5},{5,9},{9,... | collective-permute-start | bytes 1179656 | tf_op jit(solution)/shard_map/ppermute | solution.py:525
  15.3 1.3 %collective-permute-start.3 = (bf16[24,8192]{1,0:T(8,128)(2,1)S(1)}, bf16[24,8192]{1,0:T(8,128)(2,1)}, u32[]{:S(2)}, u32[]{:S(2)}) collective-permute-start(bf16[24,8192]{1,0:T(8,128)(2,1)S(1)} %concatenate.12.own_ref), channel_id=1, source_target_pairs={{4,0},{8,4},{12,8},{16,12},{20,16},{24,20},{28,24},{5,1},{9,5},{13... | collective-permute-start | bytes 1179656 | tf_op jit(solution)/shard_map/ppermute | solution.py:526
  16.6 0.0 all-gather.4.cloned.1.call-update
  16.6 0.0 all-gather.6.cloned.1.call-start
  16.7 0.8 constant_dynamic-slice_fusion.1
  17.4 0.1 copy.48
  17.5 0.1 copy.47
  17.6 0.1 add_select_fusion.5
  17.6 0.1 fusion.11
  17.8 0.1 copy.34
  17.9 0.1 fusion.25
  18.0 0.1 copy.35
  18.0 0.1 copy.37
  18.1 0.1 pad_add_fusion
  18.2 0.1 copy.44.col_ref
  18.3 0.1 copy.49
  18.4 0.1 copy.50
  18.5 0.1 slice.58
  18.6 0.1 copy.39
  18.7 0.1 fusion.24
  18.8 0.1 copy.40
  18.9 0.1 copy.42
  18.9 0.1 pad_add_fusion.1
  19.0 0.1 copy.45.cls_ref
  19.1 0.0 copy-done.6
  19.2 2.1 %relay.1 = (bf16[64,64,128]{2,1,0:T(8,128)(2,1)S(1)}, bf16[24,64,64]{2,1,0:T(8,128)(2,1)S(1)}) custom-call(bf16[127,4096]{1,0:T(8,128)(2,1)S(1)} %copy-done.1, bf16[24,4096]{1,0:T(8,128)(2,1)S(1)} %copy-done.6), custom_call_target="tpu_custom_call" | custom-call | flops 1000 | bytes 100000 | tf_op jit(solution)/shard_map/relay/pallas_call | solution.py:188
  21.3 0.7 copy-done.7
  22.0 2.6 %class_counts.1.a_ref = bf16[24,128,256]{2,1,0:T(8,128)(2,1)S(1)} custom-call(s32[128,24]{1,0:T(8,128)S(1)} %copy.44.col_ref, s32[128,24]{1,0:T(8,128)S(1)} %copy.45.cls_ref), custom_call_target="tpu_custom_call" | custom-call | flops 1000 | bytes 100000 | tf_op jit(solution)/shard_map/class_counts/pallas_call | solution.py:242
  24.7 11.3 %all-gather.4.cloned.1.call-done = bf16[64,64,128]{2,1,0:T(8,128)(2,1)} async-done(((bf16[16,64,128]{2,1,0:T(8,128)(2,1)}), bf16[64,64,128]{2,1,0:T(8,128)(2,1)}) %all-gather.4.cloned.1.call-update) | async-done | bytes 1048592 | tf_op jit(solution)/shard_map/all_gather | solution.py:496
  36.0 0.0 copy-done
  36.0 1.2 copy-done.2
  37.2 2.7 %upward.1 = (bf16[16,64,128]{2,1,0:T(8,128)(2,1)S(1)}, bf16[16,32,128]{2,1,0:T(8,128)(2,1)S(1)}, bf16[16,32,128]{2,1,0:T(8,128)(2,1)S(1)}, bf16[32,16,128]{2,1,0:T(8,128)(2,1)}) custom-call(bf16[16,8192]{1,0:T(8,128)(2,1)S(1)} %copy-done, bf16[32,128,128]{2,1,0:T(8,128)(2,1)S(1)} %bitcast.17, bf16[64,64,128]{2,1,0:T(8,128)(2,1)S(1)} %get-tuple-element.13.links_ref), custom_call_target="tpu_custom_call" | custom-call | flops 300000000 | bytes 3000000 | tf_op jit(solution)/shard_map/upward/pallas_call | solution.py:306
  39.9 0.7 copy-done.9
  40.6 0.7 copy-done.10
  41.2 0.8 copy.46.near_ref
  42.0 3.5 %collective-permute-start = (bf16[16,32,128]{2,1,0:T(8,128)(2,1)}, bf16[16,32,128]{2,1,0:T(8,128)(2,1)S(1)}, u32[]{:S(2)}, u32[]{:S(2)}) collective-permute-start(bf16[16,32,128]{2,1,0:T(8,128)(2,1)} %copy-done.10), channel_id=1, source_target_pairs={{0,4},{4,8},{8,12},{12,16},{16,20},{20,24},{24,28},{1,5},{5,9},{9,... | collective-permute-start | bytes 393224 | tf_op jit(solution)/shard_map/ppermute | solution.py:530
  45.5 1.5 %collective-permute-start.1 = (bf16[16,32,128]{2,1,0:T(8,128)(2,1)}, bf16[16,32,128]{2,1,0:T(8,128)(2,1)}, u32[]{:S(2)}, u32[]{:S(2)}) collective-permute-start(bf16[16,32,128]{2,1,0:T(8,128)(2,1)} %copy-done.9), channel_id=1, source_target_pairs={{4,0},{8,4},{12,8},{16,12},{20,16},{24,20},{28,24},{5,1},{9,5},{13... | collective-permute-start | bytes 393224 | tf_op jit(solution)/shard_map/ppermute | solution.py:531
  47.0 0.0 all-gather.6.cloned.1.call-update
  47.0 0.0 copy-start.3
  47.1 0.0 collective-permute-done.2.low_ref
  47.1 0.0 collective-permute-done.3.high_ref
  47.1 0.0 copy-start.11
  47.1 0.9 copy-done.11
  48.0 54.3 %near_field.1.near_ref = f32[16,8192]{1,0:T(8,128)S(1)} custom-call(s32[64,27]{1,0:T(8,128)S(1)} %copy.46.near_ref, bf16[24,8192]{1,0:T(8,128)(2,1)} %collective-permute-done.2.low_ref, bf16[24,8192]{1,0:T(8,128)(2,1)S(1)} %concatenate.12.own_ref, bf16[24,8192]{1,0:T(8,128)(2,1)} %collective-permute-done.3.high_ref, bf16[32,128]{1,0:T(8,128)(2,1)S(1)} %copy-done.12, ...), custom_call_target="tpu_custom_call" | custom-call | flops 20000000000 | bytes 5000000 | tf_op jit(solution)/shard_map/near_field/pallas_call | solution.py:143
  102.3 0.8 copy-done.13
  103.1 0.8 slice.70.tops_ref
  103.9 0.0 collective-permute-done.low_ref
  103.9 0.0 collective-permute-done.1.high_ref
  103.9 1.2 copy-done.5
  105.1 1.0 copy-done.8
  106.1 1.0 copy-done.14
  107.1 11.4 %downward.1 = bf16[16,8192]{1,0:T(8,128)(2,1)} custom-call(bf16[16,32,128]{2,1,0:T(8,128)(2,1)S(1)} %collective-permute-done.low_ref, bf16[16,64,128]{2,1,0:T(8,128)(2,1)S(1)} %get-tuple-element.16.own_ref, bf16[16,32,128]{2,1,0:T(8,128)(2,1)} %collective-permute-done.1.high_ref, bf16[8,1,16,128]{3,2,1,0:T(8,128)(2,1)S(1)} %slice.70.tops_ref, ...), custom_call_target="tpu_custom_call" | custom-call | flops 4000000000 | bytes 6000000 | tf_op jit(solution)/shard_map/downward/pallas_call | solution.py:433
  (25 shorter events, 0.2 us)
Async XLA Ops:
  6.5 11.1 %copy-start.15 = (s32[127,24]{0,1:T(8,128)S(1)}, s32[127,24]{0,1:T(8,128)}, u32[]{:S(2)}) copy-start(s32[127,24]{0,1:T(8,128)} %param.18) | copy-start | bytes 36580
  6.5 29.4 %all-gather.4.cloned.1.call-start = ((), (), s32[]{:S(2)}) async-start(), calls=%async_computation | async-start | bytes 1310720 | tf_op jit(solution)/shard_map/all_gather | solution.py:496
  6.8 11.7 %copy-start.16 = (s32[127,24]{0,1:T(8,128)S(1)}, s32[127,24]{0,1:T(8,128)}, u32[]{:S(2)}) copy-start(s32[127,24]{0,1:T(8,128)} %param.19) | copy-start | bytes 36580
  7.9 11.2 %copy-start.1 = (bf16[127,4096]{1,0:T(8,128)(2,1)S(1)}, bf16[127,4096]{1,0:T(8,128)(2,1)}, u32[]{:S(2)}) copy-start(bf16[127,4096]{1,0:T(8,128)(2,1)} %transfer_ref.1) | copy-start | bytes 3121156
  7.9 11.2 %copy-start.6 = (bf16[24,4096]{1,0:T(8,128)(2,1)S(1)}, bf16[24,4096]{1,0:T(8,128)(2,1)}, u32[]{:S(2)}) copy-start(bf16[24,4096]{1,0:T(8,128)(2,1)} %coupling_ref.1) | copy-start | bytes 589828
  9.7 37.4 %collective-permute-start.2 = (bf16[24,8192]{1,0:T(8,128)(2,1)S(1)}, bf16[24,8192]{1,0:T(8,128)(2,1)}, u32[]{:S(2)}, u32[]{:S(2)}) collective-permute-start(bf16[24,8192]{1,0:T(8,128)(2,1)S(1)} %concatenate.12.own_ref), channel_id=1, source_target_pairs={{0,4},{4,8},{8,12},{12,16},{16,20},{20,24},{24,28},{1,5},{5,9},{9,... | collective-permute-start | bytes 1179656 | tf_op jit(solution)/shard_map/ppermute | solution.py:525
  15.3 31.8 %collective-permute-start.3 = (bf16[24,8192]{1,0:T(8,128)(2,1)S(1)}, bf16[24,8192]{1,0:T(8,128)(2,1)}, u32[]{:S(2)}, u32[]{:S(2)}) collective-permute-start(bf16[24,8192]{1,0:T(8,128)(2,1)S(1)} %concatenate.12.own_ref), channel_id=1, source_target_pairs={{4,0},{8,4},{12,8},{16,12},{20,16},{24,20},{28,24},{5,1},{9,5},{13... | collective-permute-start | bytes 1179656 | tf_op jit(solution)/shard_map/ppermute | solution.py:526
  16.6 86.5 %all-gather.6.cloned.1.call-start = ((), (), s32[]{:S(2)}) async-start(), calls=%async_computation.1 | async-start | bytes 1179648 | tf_op jit(solution)/shard_map/all_gather | solution.py:529
  18.9 17.1 %copy-start = (bf16[16,8192]{1,0:T(8,128)(2,1)S(1)}, bf16[16,8192]{1,0:T(8,128)(2,1)}, u32[]{:S(2)}) copy-start(bf16[16,8192]{1,0:T(8,128)(2,1)} %values_ref.1) | copy-start | bytes 786436
  21.3 0.7 copy-start.7
  22.0 17.9 %copy-start.4 = (bf16[64,64,128]{2,1,0:T(8,128)(2,1)}, bf16[64,64,128]{2,1,0:T(8,128)(2,1)S(1)}, u32[]{:S(2)}) copy-start(bf16[64,64,128]{2,1,0:T(8,128)(2,1)S(1)} %get-tuple-element.13.links_ref) | copy-start | bytes 3145732
  22.0 25.0 %copy-start.12 = (bf16[32,128]{1,0:T(8,128)(2,1)S(1)}, bf16[32,128]{1,0:T(8,128)(2,1)}, u32[]{:S(2)}) copy-start(bf16[32,128]{1,0:T(8,128)(2,1)} %constant.148.clone.source_ref) | copy-start | bytes 24580
  36.0 1.2 copy-start.2
  39.9 0.7 copy-start.9
  40.6 0.7 copy-start.10
  42.0 61.9 %collective-permute-start = (bf16[16,32,128]{2,1,0:T(8,128)(2,1)}, bf16[16,32,128]{2,1,0:T(8,128)(2,1)S(1)}, u32[]{:S(2)}, u32[]{:S(2)}) collective-permute-start(bf16[16,32,128]{2,1,0:T(8,128)(2,1)} %copy-done.10), channel_id=1, source_target_pairs={{0,4},{4,8},{8,12},{12,16},{16,20},{20,24},{24,28},{1,5},{5,9},{9,... | collective-permute-start | bytes 393224 | tf_op jit(solution)/shard_map/ppermute | solution.py:530
  45.5 58.3 %collective-permute-start.1 = (bf16[16,32,128]{2,1,0:T(8,128)(2,1)}, bf16[16,32,128]{2,1,0:T(8,128)(2,1)}, u32[]{:S(2)}, u32[]{:S(2)}) collective-permute-start(bf16[16,32,128]{2,1,0:T(8,128)(2,1)} %copy-done.9), channel_id=1, source_target_pairs={{4,0},{8,4},{12,8},{16,12},{20,16},{24,20},{28,24},{5,1},{9,5},{13... | collective-permute-start | bytes 393224 | tf_op jit(solution)/shard_map/ppermute | solution.py:531
  47.0 56.8 %copy-start.3 = (bf16[64,64,128]{2,1,0:T(8,128)(2,1)S(1)}, bf16[64,64,128]{2,1,0:T(8,128)(2,1)}, u32[]{:S(2)}) copy-start(bf16[64,64,128]{2,1,0:T(8,128)(2,1)} %all-gather.4.cloned.1.call-done) | copy-start | bytes 3145732
  47.1 0.9 copy-start.11
  102.3 0.8 copy-start.13
  103.9 1.2 copy-start.5
  105.1 1.0 copy-start.8
  106.1 1.0 copy-start.14
Sparse Core Ops, SparseCore 0:
  16.7 19.2 all-gather.3
  47.2 41.7 all-gather.5

commit v5 on v4

--- a/solution.py
+++ b/solution.py
@@ -1,3 +1,5 @@
+import math
+
 import jax
 import jax.numpy as jnp
 import numpy as np
@@ -16,8 +18,9 @@
 PAIRS = 64
 RIM = 28
 
+SCALE = math.log2(math.e) / 0.2
 AMPLITUDE = 0.3
-DEAD = -1000.0
+VMEM_BYTES = 60 << 20
 
 NN = (((1,), (0,)), ((), ()))
 NT = (((1,), (1,)), ((), ()))
@@ -32,129 +35,161 @@
     return pl.BlockSpec(memory_space=pltpu.VMEM)
 
 
-def rounded(x):
-    return lax.reduce_precision(x, 8, 7)
+ONE = 12
+POINT_ROWS = 16
+
+
+def parts_of(x):
+    out = []
+    for _ in range(3):
+        part = x.astype(jnp.bfloat16).astype(jnp.float32)
+        out.append(part)
+        x = x - part
+    return out
+
+
+def pack_kernel(centre_ref, values_ref, coords_ref, own_ref, up_ref, down_ref, target_ref):
+    box = lax.broadcasted_iota(jnp.int32, (8, M), 0)
+    for g in range(B // 8):
+        planes = []
+        for k in range(3):
+            rows = [coords_ref[k : k + 1, (8 * g + i) * M : (8 * g + i + 1) * M] for i in range(8)]
+            planes.append(jnp.concatenate(rows, axis=0) - centre_ref[k])
+        ones = jnp.ones((8, M), jnp.float32)
+        zeros = jnp.zeros((8, M), jnp.float32)
+
+        def write(ref, base, shift, scale):
+            moved = planes[:2] + [planes[2] + shift]
+            size = -SCALE * (moved[0] * moved[0] + moved[1] * moved[1] + moved[2] * moved[2])
+            rows = []
+            for x in moved:
+                rows += parts_of(scale * x)
+            rows += parts_of(size) + [ones, zeros, zeros, zeros]
+            for i in range(8):
+                tile = jnp.concatenate([x[i : i + 1] for x in rows], axis=0)
+                at = slice((8 * g + i) * M, (8 * g + i + 1) * M)
+                ref[base : base + POINT_ROWS, at] = tile.astype(jnp.bfloat16)
+
+        write(own_ref, N, 0.0, 1.0)
+        write(up_ref, N, -1.0, 1.0)
+        write(down_ref, N, 1.0, 1.0)
+        write(target_ref, 0, 0.0, 2 * SCALE)
+    for ref in (own_ref, up_ref, down_ref):
+        ref[0:N, :] = values_ref[...]
+
+
+def pack(centre, values, coords):
+    wide = jax.ShapeDtypeStruct((N + POINT_ROWS, B * M), jnp.bfloat16)
+    return pl.pallas_call(
+        pack_kernel,
+        name="pack",
+        out_shape=[wide, wide, wide, jax.ShapeDtypeStruct((POINT_ROWS, B * M), jnp.bfloat16)],
+        in_specs=[pl.BlockSpec(memory_space=pltpu.SMEM)] + [vmem()] * 2,
+        out_specs=[vmem()] * 4,
+        compiler_params=pltpu.CompilerParams(vmem_limit_bytes=VMEM_BYTES),
+        cost_estimate=pl.CostEstimate(flops=1000, bytes_accessed=100_000, transcendentals=0),
+    )(centre, values, coords)
 
 
 def near_tables():
-    one = 8
-    source = np.zeros((32, 128), np.float32)
-    target = np.zeros((11 * 16, 32), np.float32)
-
-    def lane(at, y):
-        for half in range(2):
-            source[(8 * half + y) if y < one else 16, 64 * half + at] = 1
-
-    def row(tile, at, x, factor):
-        target[16 * tile + at, x if x < one else 16] = factor
-
+    lanes = []
     for k in range(3):
-        parts = [(x, p) for x in (2 * k, 2 * k + 1) for p in (8, 2)]
-        terms = [(y, x, p, None) for y in (2 * k, 2 * k + 1) for x, p in parts]
-        terms += [(y, one, -10, 1) for y in (2 * k, 2 * k + 1)]
-        terms += [(one, x, p, 1) for x, p in parts]
-        terms += [(one, one, -5, 2)]
-        for at, (y, x, factor, power) in enumerate(terms):
-            lane(16 * k + at, y)
-            for step in range(3):
-                scale = 1 if power is None else (step - 1) ** power
-                row(3 * k + step, at, x, factor * scale)
-    for at, (y, x) in enumerate(((6, one), (7, one), (one, 6), (one, 7))):
-        lane(48 + at, y)
-        for tile in (9, 10):
-            row(tile, at, x, 1)
-    lane(52, one)
-    row(10, 4, one, DEAD)
+        for i, j in ((0, 0), (0, 1), (1, 0), (1, 1), (0, 2), (2, 0)):
+            lanes.append((3 * k + i, 3 * k + j))
+    for i in range(3):
+        lanes += [(9 + i, ONE), (ONE, 9 + i)]
+    source = np.zeros((3 * POINT_ROWS, 2 * M), np.float32)
+    target = np.zeros((64, POINT_ROWS), np.float32)
+    for lane, (y, x) in enumerate(lanes):
+        target[lane, x] = 1
+        for half, box in enumerate((0, 1, 1, 2)):
+            source[POINT_ROWS * box + y, 64 * half + lane] = 1
     return [jnp.asarray(x, jnp.bfloat16) for x in (source, target)]
 
 
 def near_kernel(
-    near_ref, low_ref, own_ref, high_ref, source_ref, target_ref, out_ref, yp_ref, x_ref
+    near_ref, low_ref, own_ref, high_ref, xs_ref, source_ref, target_ref, out_ref, yp_ref, w_ref
 ):
     layers = (low_ref, own_ref, high_ref)
-    ones = jnp.ones((16, M), jnp.float32)
 
     def at(u):
         return pl.ds(pl.multiple_of(jnp.clip(u, 0, B - 1) * M, M), M)
 
-    def points(ref, first, second):
-        two = [ref[:, at(u)].astype(jnp.float32)[16:24] for u in (first, second)]
-        return jnp.concatenate(two + [ones], axis=0).astype(jnp.bfloat16)
-
     for l, src in enumerate(layers):
 
-        def features(u, carry, l=l, src=src):
-            yp_ref[l, u] = dot(points(src, u - 1, u), source_ref[...], TN).astype(jnp.bfloat16)
+        def features(q, carry, l=l, src=src):
+            u = 2 * q
+            rows = jnp.concatenate([src[N:, at(u + i)] for i in (-1, 0, 1)], axis=0)
+            both = dot(rows, source_ref[...], TN).astype(jnp.bfloat16)
+            yp_ref[l, u] = both[:, 0:M]
+            yp_ref[l, u + 1] = both[:, M : 2 * M]
             return carry
 
-        lax.fori_loop(0, B + 1, features, 0, unroll=13)
-
-    def targets(t, carry):
-        x_ref[t] = dot(target_ref[...], points(own_ref, t, t)).astype(jnp.bfloat16)
+        lax.fori_loop(0, B // 2 + 1, features, 0, unroll=11)
+
+    zero = jnp.zeros((64, M), jnp.bfloat16)
+
+    def targets(q, carry):
+        one, two = [
+            dot(target_ref[...], xs_ref[:, at(2 * q + i)]).astype(jnp.bfloat16) for i in range(2)
+        ]
+        w_ref[q] = jnp.concatenate(
+            [jnp.concatenate([one, zero], axis=1), jnp.concatenate([zero, two], axis=1)], axis=0
+        )
         return carry
 
-    lax.fori_loop(0, B, targets, 0, unroll=8)
-
-    zero = jnp.zeros((64, M), jnp.bfloat16)
-
-    def weights(t, a, b, c, slot):
-        last = jnp.where(near_ref[t, slot] >= 0, 9, 10) * 16
-        tiles = [x_ref[t, 16 * i : 16 * (i + 1), :] for i in (a, 3 + b, 6 + c)]
-        return jnp.concatenate(tiles + [x_ref[t, pl.ds(pl.multiple_of(last, 16), 16), :]], axis=0)
-
-    def kernel(t, a, b, c):
-        slot = 9 * c + 3 * b + a
-        u = t + (b - 1) * ROW + a - 1
-        w = jnp.concatenate(
-            [
-                jnp.concatenate([weights(t, a, b, c, slot), zero], axis=1),
-                jnp.concatenate([zero, weights(t + 1, a, b, c, slot)], axis=1),
-            ],
-            axis=0,
-        )
-        src = layers[c]
-        vectors = jnp.concatenate([src[0:16, at(u)], src[0:16, at(u + 1)]], axis=0)
-        return vectors, jnp.exp(dot(yp_ref[c, u + 1], w)).astype(jnp.bfloat16)
-
+    lax.fori_loop(0, B // 2, targets, 0, unroll=8)
+
+    none = jnp.zeros((N, M), jnp.bfloat16)
     rows = B // ROW
     for first, last, steps in ((0, 1, (1, 2)), (1, rows - 1, (0, 1, 2)), (rows - 1, rows, (0, 1))):
-        slots = [(a, b, c) for c in range(3) for b in steps for a in range(3)]
-        groups = [slots[i : i + 2] for i in range(0, len(slots), 2)]
-
-        def step(q, carry, first=first, groups=groups):
-            pairs = [first * ROW + 4 * q, first * ROW + 4 * q + 2]
-            totals = [jnp.zeros((32, 2 * M), jnp.float32) for _ in pairs]
-            for group in groups:
-                for p, t in enumerate(pairs):
-                    both = [kernel(t, *slot) for slot in group]
-                    totals[p] += dot(
-                        jnp.concatenate([v for v, _ in both], axis=1),
-                        jnp.concatenate([k for _, k in both], axis=0),
-                    )
-            for p, t in enumerate(pairs):
-                out_ref[:, at(t)] = AMPLITUDE * totals[p][0:16, 0:M]
-                out_ref[:, at(t + 1)] = AMPLITUDE * totals[p][16:32, M : 2 * M]
+
+        def step(q, carry, first=first, steps=steps):
+            t = first * ROW + 2 * q
+            sources, vectors = [], []
+            for c in range(3):
+                for b in steps:
+                    for a in range(3):
+                        slot = 9 * c + 3 * b + a
+                        u = t + (b - 1) * ROW + a - 1
+                        sources.append(yp_ref[c, u + 1])
+                        vectors.append(
+                            jnp.concatenate(
+                                [
+                                    jnp.where(
+                                        near_ref[t + i, slot] >= 0, layers[c][0:N, at(u + i)], none
+                                    )
+                                    for i in range(2)
+                                ],
+                                axis=0,
+                            )
+                        )
+            e = dot(jnp.concatenate(sources, axis=0), w_ref[first * ROW // 2 + q])
+            kernel = jnp.exp2(e).astype(jnp.bfloat16)
+            total = dot(jnp.concatenate(vectors, axis=1), kernel)
+            out_ref[:, at(t)] = AMPLITUDE * total[0:N, 0:M]
+            out_ref[:, at(t + 1)] = AMPLITUDE * total[N : 2 * N, M : 2 * M]
             return carry
 
-        lax.fori_loop(0, (last - first) * ROW // 4, step, 0)
-
-
-def near_field(near_src, low, own, high):
+        lax.fori_loop(0, (last - first) * ROW // 2, step, 0)
+
+
+def near_field(near_src, low, own, high, targets):
     return pl.pallas_call(
         near_kernel,
         name="near_field",
         out_shape=jax.ShapeDtypeStruct((N, B * M), jnp.float32),
-        in_specs=[pl.BlockSpec(memory_space=pltpu.SMEM)] + [vmem()] * 5,
+        in_specs=[pl.BlockSpec(memory_space=pltpu.SMEM)] + [vmem()] * 6,
         out_specs=vmem(),
         scratch_shapes=[
-            pltpu.VMEM((3, B + 1, M, M), jnp.bfloat16),
-            pltpu.VMEM((B, 11 * 16, M), jnp.bfloat16),
+            pltpu.VMEM((3, B + 2, M, M), jnp.bfloat16),
+            pltpu.VMEM((B // 2, M, 2 * M), jnp.bfloat16),
         ],
-        compiler_params=pltpu.CompilerParams(vmem_limit_bytes=40 << 20),
+        compiler_params=pltpu.CompilerParams(vmem_limit_bytes=VMEM_BYTES),
         cost_estimate=pl.CostEstimate(
             flops=20_000_000_000, bytes_accessed=5_000_000, transcendentals=28_000_000
         ),
-    )(near_src, low, own, high, *near_tables())
+    )(near_src, low, own, high, targets, *near_tables())
 
 
 def relay_kernel(transfer_ref, coupling_ref, links_ref, coupling_t_ref, flat_ref, pair_ref):
@@ -198,7 +233,7 @@
             pltpu.VMEM(((TB + 1) * K // 2, 2 * K), jnp.float32),
             pltpu.VMEM((K, 2 * K), jnp.float32),
         ],
-        compiler_params=pltpu.CompilerParams(vmem_limit_bytes=16 << 20),
+        compiler_params=pltpu.CompilerParams(vmem_limit_bytes=VMEM_BYTES),
         cost_estimate=pl.CostEstimate(flops=1000, bytes_accessed=100_000, transcendentals=0),
     )(transfer, coupling)
 
@@ -245,7 +280,7 @@
         out_shape=jax.ShapeDtypeStruct((class_count, 2 * PAIRS, width), jnp.bfloat16),
         in_specs=[vmem()] * 2,
         out_specs=vmem(),
-        compiler_params=pltpu.CompilerParams(vmem_limit_bytes=20 << 20),
+        compiler_params=pltpu.CompilerParams(vmem_limit_bytes=VMEM_BYTES),
         cost_estimate=pl.CostEstimate(
             flops=1000, bytes_accessed=100_000, transcendentals=0
         ),
@@ -319,7 +354,7 @@
             pltpu.VMEM((N * RIM_ROWS, 2 * K), jnp.float32),
             pltpu.VMEM((N * RIM_ROWS, 2 * K), jnp.float32),
         ],
-        compiler_params=pltpu.CompilerParams(vmem_limit_bytes=20 << 20),
+        compiler_params=pltpu.CompilerParams(vmem_limit_bytes=VMEM_BYTES),
         cost_estimate=pl.CostEstimate(
             flops=300_000_000, bytes_accessed=3_000_000, transcendentals=0
         ),
@@ -443,7 +478,7 @@
             pltpu.VMEM((N // 2 * PAIRS, classes * 4 * K), jnp.bfloat16),
             pltpu.VMEM((N * PAIRS, 2 * K), jnp.float32),
         ],
-        compiler_params=pltpu.CompilerParams(vmem_limit_bytes=40 << 20),
+        compiler_params=pltpu.CompilerParams(vmem_limit_bytes=VMEM_BYTES),
         cost_estimate=pl.CostEstimate(
             flops=4_000_000_000, bytes_accessed=6_000_000, transcendentals=0
         ),
@@ -495,22 +530,10 @@
 
     whole_basis = lax.all_gather(basis, "vec", axis=0, tiled=True)
 
-    box = jnp.arange(B, dtype=jnp.int32)
-    centre = jnp.stack(
-        [box % ROW, box // ROW, jnp.full((B,), 0, jnp.int32) + position]
-    ).astype(jnp.float32) + 0.5
-    flat = coords - jnp.repeat(centre, M, axis=1)
-    coarse = rounded(flat)
-    rest = rounded(flat - coarse)
-    held = coarse + rest
-    size = -5.0 * (held[0] ** 2 + held[1] ** 2 + held[2] ** 2)
-    size_a = rounded(size)
-    size_b = size - size_a
-    rows = []
-    for k in range(3):
-        rows += [coarse[k], rest[k]]
-    rows += [size_a, size_b]
-    packed = jnp.concatenate([values, jnp.stack(rows).astype(jnp.bfloat16)], axis=0)
+    middle = (ROW / 2, B // ROW / 2, position.astype(jnp.float32) + 0.5)
+    centre = jnp.stack([jnp.asarray(x, jnp.float32) for x in middle])
+    packed, for_high, for_low, targets = pack(centre, values, coords)
+
     links, coupling_t = relay(transfer, coupling)
     columns = source_columns(far_src, top_src, position, subtrees, height)
     classes = by_parity(
@@ -522,15 +545,16 @@
 
     forward = [(i, i + 1) for i in range(subtrees - 1)]
     backward = [(i + 1, i) for i in range(subtrees - 1)]
-    from_low = lax.ppermute(packed, "leaf", forward)
-    from_high = lax.ppermute(packed, "leaf", backward)
+    for_high, for_low, counts, links = lax.optimization_barrier((for_high, for_low, counts, links))
+    from_low = lax.ppermute(for_high, "leaf", forward)
+    from_high = lax.ppermute(for_low, "leaf", backward)
     basis_pairs = whole_basis.reshape(B // 2, 2 * K, M)
     coefs, first, last, root = upward(values, basis_pairs, links)
     tops = lax.all_gather(root, "leaf", axis=0)
     low = lax.ppermute(last, "leaf", forward)
     high = lax.ppermute(first, "leaf", backward)
     near_src, coefs = lax.optimization_barrier((near_src, coefs))
-    near = near_field(near_src, from_low, packed, from_high)
+    near = near_field(near_src, from_low, packed, from_high, targets)
     tops = lax.slice_in_dim(tops, 0, 1, axis=1)
     return downward(low, coefs, high, tops, counts, coupling_t, links, basis_pairs, near)
 

time: 126 us -> 118 us (0.937)
  Pallas kernels: 73.2 us -> 65.8 us
  local copies, waits for them, and re-layouts: 13.7 us -> 7.74 us
  waiting for transfers between devices: 11.3 us -> 16.3 us
    pallas_call x1, Pallas kernels: 54.3 us -> 36.7 us  [near_field(): pl.pallas_call(near_kernel, name='near_field', out_shape=jax.ShapeDtypeSt...]
    ppermute x2, waiting for transfers between devices: 0.01 us -> 15.6 us  [the longest x1 15.6 us: per_device(): from_low = lax.ppermute(for_high, 'leaf', forward)]
    all_gather x1, waiting for transfers between devices: 11.3 us -> 0.02 us  [per_device(): whole_basis = lax.all_gather(basis, 'vec', axis=0, tiled=True)]
    unnamed x39 -> x14, local copies, waits for them, and re-layouts: 8.66 us -> 2.01 us
    pallas_call x0 -> x1, Pallas kernels: none -> 2.88 us  [pack(): pl.pallas_call(pack_kernel, name='pack', out_shape=[wide, wide, wide, jax...]
    pallas_call x1, Pallas kernels: 2.14 us -> 4.3 us  [relay(): pl.pallas_call(relay_kernel, name='relay', out_shape=[jax.ShapeDtypeStruc...]
    pallas_call x1, Pallas kernels: 2.64 us -> 4.69 us  [class_counts(): pl.pallas_call(counts_kernel, name='class_counts', out_shape=jax.ShapeDty...]
    pallas_call x1, Pallas kernels: 2.69 us -> 4.4 us  [upward(): pl.pallas_call(up_kernel, name='upward', out_shape=[jax.ShapeDtypeStruct(...]
  transfers between devices with their start and end apart: 6 -> 6, of which waited for: 1 -> 1; matrix products, arithmetic and copies ran while one was open for 3% -> 7% of each run, Pallas kernels for 49% -> 45%
where the time goes in v5:
time: 118 us
  Pallas kernels  65.8 us (56%)
  waiting for transfers between devices  16.3 us (14%)
  between operations  13.5 us (11%)
  starting transfers between devices  12.2 us (10%)
  local copies, waits for them, and re-layouts  7.74 us (7%)
  other arithmetic  2.32 us (2%)
    pallas_call x1, Pallas kernels, near_field(): pl.pallas_call(near_kernel, name='near_field', out_shape=jax.ShapeDtypeSt...  36.7 us
    ppermute x1, waiting for transfers between devices, per_device(): from_low = lax.ppermute(for_high, 'leaf', forward)  15.6 us
    pallas_call x1, Pallas kernels, downward(): pl.pallas_call(down_kernel, name='downward', out_shape=jax.ShapeDtypeStru...  12.8 us
    ppermute x1, starting transfers between devices, per_device(): from_low = lax.ppermute(for_high, 'leaf', forward)  4.85 us
    pallas_call x1, Pallas kernels, class_counts(): pl.pallas_call(counts_kernel, name='class_counts', out_shape=jax.ShapeDty...  4.69 us
    ppermute x1, starting transfers between devices, per_device(): low = lax.ppermute(last, 'leaf', forward)  4.54 us
    pallas_call x1, Pallas kernels, upward(): pl.pallas_call(up_kernel, name='upward', out_shape=[jax.ShapeDtypeStruct(...  4.4 us
    pallas_call x1, Pallas kernels, relay(): pl.pallas_call(relay_kernel, name='relay', out_shape=[jax.ShapeDtypeStruc...  4.3 us
  transfers between devices with their start and end apart: 6, of which 1 were waited for; matrix products, arithmetic and copies ran while one was open for 7% of the time, Pallas kernels for 45%

profile of v5, /device:TPU:0, one launch (start us, length us, event | category | flops | bytes accessed | tf_op | source)
XLA Modules:
  0.0 117.9 jit_solution(4824658522164669008)
XLA Ops:
  6.5 0.0 all-gather.4.cloned.1.call-start
  6.5 0.7 all-gather.4.cloned.1.call-update
  7.3 0.0 all-gather.6.cloned.1.call-start
  7.3 0.8 add_select_fusion.5
  8.1 0.8 fusion.5
  8.9 0.1 copy.34
  9.1 0.1 fusion.15
  9.1 0.8 constant_dynamic-slice_fusion.1
  9.9 0.1 copy.48
  10.0 0.1 copy.47
  10.0 0.1 copy.35
  10.1 0.1 copy.37
  10.2 0.1 pad_add_fusion
  10.3 0.7 copy.44.col_ref
  11.0 0.1 copy.49
  11.1 0.1 copy.50
  11.2 0.8 slice.24
  12.0 0.1 copy.39
  12.1 0.1 fusion.14
  12.2 0.1 copy.40
  12.3 0.1 copy.42
  12.3 0.1 pad_add_fusion.1
  12.4 0.7 copy.45.cls_ref
  13.1 4.7 %class_counts.1.a_ref = bf16[24,128,256]{2,1,0:T(8,128)(2,1)} custom-call(s32[128,24]{1,0:T(8,128)} %copy.44.col_ref, s32[128,24]{1,0:T(8,128)} %copy.45.cls_ref), custom_call_target="tpu_custom_call" | custom-call | flops 1000 | bytes 100000 | tf_op jit(solution)/shard_map/class_counts/pallas_call | solution.py:277
  17.8 4.3 %relay.1 = (bf16[64,64,128]{2,1,0:T(8,128)(2,1)}, bf16[24,64,64]{2,1,0:T(8,128)(2,1)}) custom-call(bf16[127,4096]{1,0:T(8,128)(2,1)} %transfer_ref.1, bf16[24,4096]{1,0:T(8,128)(2,1)} %coupling_ref.1), custom_call_target="tpu_custom_call" | custom-call | flops 1000 | bytes 100000 | tf_op jit(solution)/shard_map/relay/pallas_call | solution.py:223
  22.1 0.0 copy-start
  22.1 0.6 pad_maximum_fusion.centre_ref
  22.7 2.9 %pack.1 = (bf16[32,8192]{1,0:T(8,128)(2,1)}, bf16[32,8192]{1,0:T(8,128)(2,1)}, bf16[32,8192]{1,0:T(8,128)(2,1)}, bf16[16,8192]{1,0:T(8,128)(2,1)}) custom-call(f32[3]{0:T(128)} %pad_maximum_fusion.centre_ref, bf16[16,8192]{1,0:T(8,128)(2,1)} %values_ref.3, f32[3,8192]{1,0:T(4,128)} %coords_ref.1), custom_call_target="tpu_custom_call" | custom-call | flops 1000 | bytes 100000 | tf_op jit(solution)/shard_map/pack/pallas_call | solution.py:83
  25.6 4.9 %collective-permute-start.2 = (bf16[32,8192]{1,0:T(8,128)(2,1)}, bf16[32,8192]{1,0:T(8,128)(2,1)S(1)}, u32[]{:S(2)}, u32[]{:S(2)}) collective-permute-start(bf16[32,8192]{1,0:T(8,128)(2,1)} %get-tuple-element.33), channel_id=1, source_target_pairs={{0,4},{4,8},{8,12},{12,16},{16,20},{20,24},{24,28},{1,5},{5,9},{9,... | collective-permute-start | bytes 1572872 | tf_op jit(solution)/shard_map/ppermute | solution.py:549
  30.5 1.3 %collective-permute-start.3 = (bf16[32,8192]{1,0:T(8,128)(2,1)}, bf16[32,8192]{1,0:T(8,128)(2,1)S(1)}, u32[]{:S(2)}, u32[]{:S(2)}) collective-permute-start(bf16[32,8192]{1,0:T(8,128)(2,1)} %get-tuple-element.35), channel_id=1, source_target_pairs={{4,0},{8,4},{12,8},{16,12},{20,16},{24,20},{28,24},{5,1},{9,5},{13... | collective-permute-start | bytes 1572872 | tf_op jit(solution)/shard_map/ppermute | solution.py:550
  31.8 0.0 all-gather.4.cloned.1.call-done
  31.8 4.4 %upward.1 = (bf16[16,64,128]{2,1,0:T(8,128)(2,1)}, bf16[16,32,128]{2,1,0:T(8,128)(2,1)}, bf16[16,32,128]{2,1,0:T(8,128)(2,1)}, bf16[32,16,128]{2,1,0:T(8,128)(2,1)}) custom-call(bf16[16,8192]{1,0:T(8,128)(2,1)} %values_ref.3, bf16[32,128,128]{2,1,0:T(8,128)(2,1)} %bitcast.7, bf16[64,64,128]{2,1,0:T(8,128)(2,1)} %get-tuple-element.24.links_ref), custom_call_target="tpu_custom_call" | custom-call | flops 300000000 | bytes 3000000 | tf_op jit(solution)/shard_map/upward/pallas_call | solution.py:341
  36.2 0.0 copy-done
  36.2 0.7 copy.46.near_ref
  36.9 4.5 %collective-permute-start = (bf16[16,32,128]{2,1,0:T(8,128)(2,1)}, bf16[16,32,128]{2,1,0:T(8,128)(2,1)S(1)}, u32[]{:S(2)}, u32[]{:S(2)}) collective-permute-start(bf16[16,32,128]{2,1,0:T(8,128)(2,1)} %get-tuple-element.25), channel_id=1, source_target_pairs={{0,4},{4,8},{8,12},{12,16},{16,20},{20,24},{24,28},{1,5},{5,9},{9,... | collective-permute-start | bytes 393224 | tf_op jit(solution)/shard_map/ppermute | solution.py:554
  41.4 1.5 %collective-permute-start.1 = (bf16[16,32,128]{2,1,0:T(8,128)(2,1)}, bf16[16,32,128]{2,1,0:T(8,128)(2,1)S(1)}, u32[]{:S(2)}, u32[]{:S(2)}) collective-permute-start(bf16[16,32,128]{2,1,0:T(8,128)(2,1)} %get-tuple-element.28), channel_id=1, source_target_pairs={{4,0},{8,4},{12,8},{16,12},{20,16},{24,20},{28,24},{5,1},{9,5},{13... | collective-permute-start | bytes 393224 | tf_op jit(solution)/shard_map/ppermute | solution.py:555
  42.9 0.0 all-gather.6.cloned.1.call-update
  42.9 15.6 %collective-permute-done.2.low_ref = bf16[32,8192]{1,0:T(8,128)(2,1)S(1)} collective-permute-done((bf16[32,8192]{1,0:T(8,128)(2,1)}, bf16[32,8192]{1,0:T(8,128)(2,1)S(1)}, u32[]{:S(2)}, u32[]{:S(2)}) %collective-permute-start.2) | collective-permute-done | bytes 524320 | tf_op jit(solution)/shard_map/ppermute | solution.py:549
  58.5 0.0 copy-start.1
  58.5 0.0 collective-permute-done.3.high_ref
  58.5 0.0 copy-start.2
  58.5 0.8 copy-done.1
  59.3 0.2 copy-done.2
  59.5 36.7 %near_field.1.near_ref = f32[16,8192]{1,0:T(8,128)} custom-call(s32[64,27]{1,0:T(8,128)} %copy.46.near_ref, bf16[32,8192]{1,0:T(8,128)(2,1)} %copy-done.1, bf16[32,8192]{1,0:T(8,128)(2,1)} %get-tuple-element.34.own_ref, bf16[32,8192]{1,0:T(8,128)(2,1)} %copy-done.2, bf16[16,8192]{1,0:T(8,128)(2,1)} %get-tuple-element.36.xs_ref, ...), custom_call_target="tpu_custom_call" | custom-call | flops 20000000000 | bytes 5000000 | tf_op jit(solution)/shard_map/near_field/pallas_call | solution.py:178
  96.1 0.0 all-gather.6.cloned.1.call-done
  96.1 1.4 %slice.41.tops_ref = bf16[8,1,16,128]{3,2,1,0:T(8,128)(2,1)} slice(bf16[8,32,16,128]{3,2,1,0:T(8,128)(2,1)} %bitcast.13), slice={[0:8], [0:1], [0:16], [0:128]} | slice | bytes 65536 | tf_op jit(solution)/shard_map/slice | solution.py:558
  97.5 0.0 collective-permute-done.low_ref
  97.5 0.0 copy-start.3
  97.5 0.0 collective-permute-done.1.high_ref
  97.5 0.0 copy-start.4
  97.5 0.6 copy-done.3
  98.2 0.0 copy-done.4
  98.2 12.8 %downward.1 = bf16[16,8192]{1,0:T(8,128)(2,1)} custom-call(bf16[16,32,128]{2,1,0:T(8,128)(2,1)} %copy-done.3, bf16[16,64,128]{2,1,0:T(8,128)(2,1)} %get-tuple-element.27.own_ref, bf16[16,32,128]{2,1,0:T(8,128)(2,1)} %copy-done.4, bf16[8,1,16,128]{3,2,1,0:T(8,128)(2,1)} %slice.41.tops_ref, bf16[24,128,256]{2,1,0:T(8,128)(2,1)} %class_counts.1.a_ref, ...), custom_call_target="tpu_custom_call" | custom-call | flops 4000000000 | bytes 6000000 | tf_op jit(solution)/shard_map/downward/pallas_call | solution.py:468
  (4 shorter events, 0.1 us)
Async XLA Ops:
  6.5 25.2 %all-gather.4.cloned.1.call-start = ((), (), s32[]{:S(2)}) async-start(), calls=%async_computation | async-start | bytes 1310720 | tf_op jit(solution)/shard_map/all_gather | solution.py:531
  7.3 88.9 %all-gather.6.cloned.1.call-start = ((), (), s32[]{:S(2)}) async-start(), calls=%async_computation.1 | async-start | bytes 1179648 | tf_op jit(solution)/shard_map/all_gather | solution.py:553
  22.1 14.1 %copy-start = (s32[64,27]{0,1:T(8,128)S(1)}, s32[64,27]{0,1:T(8,128)}, u32[]{:S(2)}) copy-start(s32[64,27]{0,1:T(8,128)} %param.17) | copy-start | bytes 20740
  25.6 32.9 %collective-permute-start.2 = (bf16[32,8192]{1,0:T(8,128)(2,1)}, bf16[32,8192]{1,0:T(8,128)(2,1)S(1)}, u32[]{:S(2)}, u32[]{:S(2)}) collective-permute-start(bf16[32,8192]{1,0:T(8,128)(2,1)} %get-tuple-element.33), channel_id=1, source_target_pairs={{0,4},{4,8},{8,12},{12,16},{16,20},{20,24},{24,28},{1,5},{5,9},{9,... | collective-permute-start | bytes 1572872 | tf_op jit(solution)/shard_map/ppermute | solution.py:549
  30.5 28.0 %collective-permute-start.3 = (bf16[32,8192]{1,0:T(8,128)(2,1)}, bf16[32,8192]{1,0:T(8,128)(2,1)S(1)}, u32[]{:S(2)}, u32[]{:S(2)}) collective-permute-start(bf16[32,8192]{1,0:T(8,128)(2,1)} %get-tuple-element.35), channel_id=1, source_target_pairs={{4,0},{8,4},{12,8},{16,12},{20,16},{24,20},{28,24},{5,1},{9,5},{13... | collective-permute-start | bytes 1572872 | tf_op jit(solution)/shard_map/ppermute | solution.py:550
  36.9 60.6 %collective-permute-start = (bf16[16,32,128]{2,1,0:T(8,128)(2,1)}, bf16[16,32,128]{2,1,0:T(8,128)(2,1)S(1)}, u32[]{:S(2)}, u32[]{:S(2)}) collective-permute-start(bf16[16,32,128]{2,1,0:T(8,128)(2,1)} %get-tuple-element.25), channel_id=1, source_target_pairs={{0,4},{4,8},{8,12},{12,16},{16,20},{20,24},{24,28},{1,5},{5,9},{9,... | collective-permute-start | bytes 393224 | tf_op jit(solution)/shard_map/ppermute | solution.py:554
  41.4 56.1 %collective-permute-start.1 = (bf16[16,32,128]{2,1,0:T(8,128)(2,1)}, bf16[16,32,128]{2,1,0:T(8,128)(2,1)S(1)}, u32[]{:S(2)}, u32[]{:S(2)}) collective-permute-start(bf16[16,32,128]{2,1,0:T(8,128)(2,1)} %get-tuple-element.28), channel_id=1, source_target_pairs={{4,0},{8,4},{12,8},{16,12},{20,16},{24,20},{28,24},{5,1},{9,5},{13... | collective-permute-start | bytes 393224 | tf_op jit(solution)/shard_map/ppermute | solution.py:555
  58.5 0.8 copy-start.1
  58.5 1.0 copy-start.2
  97.5 0.7 copy-start.3
  97.5 0.7 copy-start.4
Sparse Core Ops, SparseCore 0:
  8.9 19.6 all-gather.3
  43.1 44.7 all-gather.5

commit v6 on v5

--- a/solution.py
+++ b/solution.py
@@ -1,3 +1,4 @@
+import functools
 import math
 
 import jax
@@ -20,7 +21,9 @@
 
 SCALE = math.log2(math.e) / 0.2
 AMPLITUDE = 0.3
-VMEM_BYTES = 60 << 20
+VMEM_BYTES = 32 << 20
+QUAD = 4
+LANES = 32
 
 NN = (((1,), (0,)), ((), ()))
 NT = (((1,), (1,)), ((), ()))
@@ -86,7 +89,7 @@
         out_shape=[wide, wide, wide, jax.ShapeDtypeStruct((POINT_ROWS, B * M), jnp.bfloat16)],
         in_specs=[pl.BlockSpec(memory_space=pltpu.SMEM)] + [vmem()] * 2,
         out_specs=[vmem()] * 4,
-        compiler_params=pltpu.CompilerParams(vmem_limit_bytes=VMEM_BYTES),
+        compiler_params=pltpu.CompilerParams(vmem_limit_bytes=16 << 20),
         cost_estimate=pl.CostEstimate(flops=1000, bytes_accessed=100_000, transcendentals=0),
     )(centre, values, coords)
 
@@ -98,98 +101,95 @@
             lanes.append((3 * k + i, 3 * k + j))
     for i in range(3):
         lanes += [(9 + i, ONE), (ONE, 9 + i)]
-    source = np.zeros((3 * POINT_ROWS, 2 * M), np.float32)
-    target = np.zeros((64, POINT_ROWS), np.float32)
+    source = np.zeros(((QUAD + 2) * POINT_ROWS, 3 * M), np.float32)
+    target = np.zeros((LANES, POINT_ROWS), np.float32)
     for lane, (y, x) in enumerate(lanes):
         target[lane, x] = 1
-        for half, box in enumerate((0, 1, 1, 2)):
-            source[POINT_ROWS * box + y, 64 * half + lane] = 1
+        for step in range(3):
+            for i in range(QUAD):
+                source[POINT_ROWS * (step + i) + y, M * step + LANES * i + lane] = 1
     return [jnp.asarray(x, jnp.bfloat16) for x in (source, target)]
 
 
-def near_kernel(
-    near_ref, low_ref, own_ref, high_ref, xs_ref, source_ref, target_ref, out_ref, yp_ref, w_ref
-):
-    layers = (low_ref, own_ref, high_ref)
+def near_kernel(layer, near_ref, src_ref, xs_ref, source_ref, target_ref, *rest):
+    before_ref = rest[0] if len(rest) == 4 else None
+    out_ref, yq_ref, w_ref = rest[-3:]
 
     def at(u):
         return pl.ds(pl.multiple_of(jnp.clip(u, 0, B - 1) * M, M), M)
 
-    for l, src in enumerate(layers):
-
-        def features(q, carry, l=l, src=src):
-            u = 2 * q
-            rows = jnp.concatenate([src[N:, at(u + i)] for i in (-1, 0, 1)], axis=0)
-            both = dot(rows, source_ref[...], TN).astype(jnp.bfloat16)
-            yp_ref[l, u] = both[:, 0:M]
-            yp_ref[l, u + 1] = both[:, M : 2 * M]
-            return carry
-
-        lax.fori_loop(0, B // 2 + 1, features, 0, unroll=11)
-
-    zero = jnp.zeros((64, M), jnp.bfloat16)
-
-    def targets(q, carry):
-        one, two = [
-            dot(target_ref[...], xs_ref[:, at(2 * q + i)]).astype(jnp.bfloat16) for i in range(2)
-        ]
-        w_ref[q] = jnp.concatenate(
-            [jnp.concatenate([one, zero], axis=1), jnp.concatenate([zero, two], axis=1)], axis=0
-        )
+    def features(q, carry):
+        t = QUAD * q
+        rows = jnp.concatenate([src_ref[N:, at(t + i)] for i in range(-1, QUAD + 1)], axis=0)
+        wide = dot(rows, source_ref[...], TN).astype(jnp.bfloat16)
+        for step in range(3):
+            yq_ref[q, step * M : (step + 1) * M, :] = wide[:, step * M : (step + 1) * M]
+        tiles = [dot(target_ref[...], xs_ref[:, at(t + i)]).astype(jnp.bfloat16) for i in range(QUAD)]
+        zero = jnp.zeros((LANES, M), jnp.bfloat16)
+        for i in range(QUAD):
+            w_ref[q, LANES * i : LANES * (i + 1), :] = jnp.concatenate(
+                [tiles[i] if i == j else zero for j in range(QUAD)], axis=1
+            )
         return carry
 
-    lax.fori_loop(0, B // 2, targets, 0, unroll=8)
+    lax.fori_loop(0, B // QUAD, features, 0, unroll=8)
 
     none = jnp.zeros((N, M), jnp.bfloat16)
     rows = B // ROW
+    row_quads = ROW // QUAD
+
+    def quad(q, steps):
+        t = QUAD * q
+        sources, vectors = [], []
+        for b in steps:
+            sources.append(yq_ref[q + (b - 1) * row_quads])
+            for a in range(3):
+                slot = 9 * layer + 3 * b + a
+                u = t + (b - 1) * ROW + a - 1
+                vectors.append(
+                    jnp.concatenate(
+                        [
+                            jnp.where(near_ref[t + i, slot] >= 0, src_ref[0:N, at(u + i)], none)
+                            for i in range(QUAD)
+                        ],
+                        axis=0,
+                    )
+                )
+        e = dot(jnp.concatenate(sources, axis=0), w_ref[q])
+        total = dot(jnp.concatenate(vectors, axis=1), jnp.exp2(e).astype(jnp.bfloat16))
+        for i in range(QUAD):
+            tile = AMPLITUDE * total[N * i : N * (i + 1), M * i : M * (i + 1)]
+            if before_ref is not None:
+                tile = before_ref[:, at(t + i)] + tile
+            out_ref[:, at(t + i)] = tile
+
     for first, last, steps in ((0, 1, (1, 2)), (1, rows - 1, (0, 1, 2)), (rows - 1, rows, (0, 1))):
 
         def step(q, carry, first=first, steps=steps):
-            t = first * ROW + 2 * q
-            sources, vectors = [], []
-            for c in range(3):
-                for b in steps:
-                    for a in range(3):
-                        slot = 9 * c + 3 * b + a
-                        u = t + (b - 1) * ROW + a - 1
-                        sources.append(yp_ref[c, u + 1])
-                        vectors.append(
-                            jnp.concatenate(
-                                [
-                                    jnp.where(
-                                        near_ref[t + i, slot] >= 0, layers[c][0:N, at(u + i)], none
-                                    )
-                                    for i in range(2)
-                                ],
-                                axis=0,
-                            )
-                        )
-            e = dot(jnp.concatenate(sources, axis=0), w_ref[first * ROW // 2 + q])
-            kernel = jnp.exp2(e).astype(jnp.bfloat16)
-            total = dot(jnp.concatenate(vectors, axis=1), kernel)
-            out_ref[:, at(t)] = AMPLITUDE * total[0:N, 0:M]
-            out_ref[:, at(t + 1)] = AMPLITUDE * total[N : 2 * N, M : 2 * M]
+            for i in range(2):
+                quad(first * row_quads + 2 * q + i, steps)
             return carry
 
-        lax.fori_loop(0, (last - first) * ROW // 2, step, 0)
-
-
-def near_field(near_src, low, own, high, targets):
+        lax.fori_loop(0, (last - first) * row_quads // 2, step, 0)
+
+
+def near_field(layer, near_src, src, targets, before=None):
+    operands = [near_src, src, targets, *near_tables()] + ([] if before is None else [before])
     return pl.pallas_call(
-        near_kernel,
-        name="near_field",
+        functools.partial(near_kernel, layer),
+        name=("near_low", "near_own", "near_high")[layer],
         out_shape=jax.ShapeDtypeStruct((N, B * M), jnp.float32),
-        in_specs=[pl.BlockSpec(memory_space=pltpu.SMEM)] + [vmem()] * 6,
+        in_specs=[pl.BlockSpec(memory_space=pltpu.SMEM)] + [vmem()] * (len(operands) - 1),
         out_specs=vmem(),
         scratch_shapes=[
-            pltpu.VMEM((3, B + 2, M, M), jnp.bfloat16),
-            pltpu.VMEM((B // 2, M, 2 * M), jnp.bfloat16),
+            pltpu.VMEM((B // QUAD, 3 * M, M), jnp.bfloat16),
+            pltpu.VMEM((B // QUAD, M, QUAD * M), jnp.bfloat16),
         ],
         compiler_params=pltpu.CompilerParams(vmem_limit_bytes=VMEM_BYTES),
         cost_estimate=pl.CostEstimate(
-            flops=20_000_000_000, bytes_accessed=5_000_000, transcendentals=28_000_000
+            flops=7_000_000_000, bytes_accessed=2_000_000, transcendentals=9_000_000
         ),
-    )(near_src, low, own, high, targets, *near_tables())
+    )(*operands)
 
 
 def relay_kernel(transfer_ref, coupling_ref, links_ref, coupling_t_ref, flat_ref, pair_ref):
@@ -233,7 +233,7 @@
             pltpu.VMEM(((TB + 1) * K // 2, 2 * K), jnp.float32),
             pltpu.VMEM((K, 2 * K), jnp.float32),
         ],
-        compiler_params=pltpu.CompilerParams(vmem_limit_bytes=VMEM_BYTES),
+        compiler_params=pltpu.CompilerParams(vmem_limit_bytes=16 << 20),
         cost_estimate=pl.CostEstimate(flops=1000, bytes_accessed=100_000, transcendentals=0),
     )(transfer, coupling)
 
@@ -280,7 +280,7 @@
         out_shape=jax.ShapeDtypeStruct((class_count, 2 * PAIRS, width), jnp.bfloat16),
         in_specs=[vmem()] * 2,
         out_specs=vmem(),
-        compiler_params=pltpu.CompilerParams(vmem_limit_bytes=VMEM_BYTES),
+        compiler_params=pltpu.CompilerParams(vmem_limit_bytes=20 << 20),
         cost_estimate=pl.CostEstimate(
             flops=1000, bytes_accessed=100_000, transcendentals=0
         ),
@@ -327,8 +327,10 @@
     up = dot(root, links_ref[PAIRS - 1][:, 0:K], NT)
     last = jnp.concatenate([root.astype(jnp.float32), up], axis=1)
     keep(PAIRS - 1, last)
-    root_ref[0] = last.astype(jnp.bfloat16)
-    root_ref[1:] = jnp.zeros((2 * N - 1, N, 2 * K), jnp.bfloat16)
+    root_ref[...] = last.astype(jnp.bfloat16)
+    for ref in (first_ref, last_ref):
+        ref[N, 0:N, :] = last.astype(jnp.bfloat16)
+        ref[N, N:RIM_ROWS, :] = jnp.zeros((RIM_ROWS - N, 2 * K), jnp.bfloat16)
     for n in range(N):
         out_ref[n] = cs_ref[n * PAIRS : (n + 1) * PAIRS, :].astype(jnp.bfloat16)
         for source, target in ((fs_ref, first_ref), (ls_ref, last_ref)):
@@ -343,9 +345,9 @@
         name="upward",
         out_shape=[
             jax.ShapeDtypeStruct((N, PAIRS, 2 * K), jnp.bfloat16),
-            jax.ShapeDtypeStruct((N, RIM_ROWS, 2 * K), jnp.bfloat16),
-            jax.ShapeDtypeStruct((N, RIM_ROWS, 2 * K), jnp.bfloat16),
-            jax.ShapeDtypeStruct((2 * N, N, 2 * K), jnp.bfloat16),
+            jax.ShapeDtypeStruct((N + 1, RIM_ROWS, 2 * K), jnp.bfloat16),
+            jax.ShapeDtypeStruct((N + 1, RIM_ROWS, 2 * K), jnp.bfloat16),
+            jax.ShapeDtypeStruct((N, 2 * K), jnp.bfloat16),
         ],
         in_specs=[vmem()] * 3,
         out_specs=[vmem()] * 4,
@@ -354,7 +356,7 @@
             pltpu.VMEM((N * RIM_ROWS, 2 * K), jnp.float32),
             pltpu.VMEM((N * RIM_ROWS, 2 * K), jnp.float32),
         ],
-        compiler_params=pltpu.CompilerParams(vmem_limit_bytes=VMEM_BYTES),
+        compiler_params=pltpu.CompilerParams(vmem_limit_bytes=20 << 20),
         cost_estimate=pl.CostEstimate(
             flops=300_000_000, bytes_accessed=3_000_000, transcendentals=0
         ),
@@ -362,25 +364,21 @@
 
 
 def down_kernel(
+    place_ref,
     low_ref,
     own_ref,
     high_ref,
-    tops_ref,
     a_ref,
     coupling_ref,
     links_ref,
     basis_ref,
     near_ref,
-    out_ref,
-    cf_ref,
-    call_ref,
-    bd_ref,
-    lhs_ref,
-    fs_ref,
+    *rest,
 ):
+    tops_refs, (out_ref, cf_ref, call_ref, bd_ref, lhs_ref, fs_ref) = rest[:-6], rest[-6:]
     classes = a_ref.shape[0]
     height = a_ref.shape[2] // 2
-    subtrees = tops_ref.shape[0]
+    subtrees = sum(ref.shape[0] for ref in tops_refs)
     lower = lax.broadcasted_iota(jnp.int32, (N, 2 * K), 1) < K
 
     used = PAIRS + 2 * RIM + subtrees
@@ -393,10 +391,11 @@
         cf_ref[at : at + RIM, :] = high_ref[n].astype(jnp.float32)[:RIM]
         if used < height:
             cf_ref[base + used : base + height, :] = jnp.zeros((height - used, 2 * K), jnp.float32)
-    for q in range(subtrees // 2):
-        even = tops_ref[2 * q, 0].astype(jnp.float32)
-        odd = tops_ref[2 * q + 1, 0].astype(jnp.float32)
-        at = PAIRS + 2 * RIM + 2 * q
+    duos = [(ref, i) for ref in tops_refs for i in range(0, ref.shape[0], 2)]
+    for m, (ref, i) in enumerate(duos):
+        even = ref[i].astype(jnp.float32)
+        odd = ref[i + 1].astype(jnp.float32)
+        at = PAIRS + 2 * RIM + 2 * ((place_ref[0] // 2) ^ m)
         cf_ref[pl.ds(at, N, stride=height), :] = jnp.where(lower, even, even + odd)
         cf_ref[pl.ds(at + 1, N, stride=height), :] = odd
     wide_lower = lax.broadcasted_iota(jnp.int32, (height, 2 * K), 1) < K
@@ -462,14 +461,14 @@
             out_ref[:, lanes] = (near_ref[:, lanes] + both[h * N : (h + 1) * N]).astype(jnp.bfloat16)
 
 
-def downward(low, own, high, tops, counts, coupling, links, basis, near):
+def downward(place, low, own, high, counts, coupling, links, basis, near, tops):
     classes = counts.shape[0]
     height = counts.shape[2] // 2
     return pl.pallas_call(
         down_kernel,
         name="downward",
         out_shape=jax.ShapeDtypeStruct((N, B * M), jnp.bfloat16),
-        in_specs=[vmem()] * 9,
+        in_specs=[pl.BlockSpec(memory_space=pltpu.SMEM)] + [vmem()] * (8 + len(tops)),
         out_specs=vmem(),
         scratch_shapes=[
             pltpu.VMEM((N * height, 2 * K), jnp.float32),
@@ -478,11 +477,11 @@
             pltpu.VMEM((N // 2 * PAIRS, classes * 4 * K), jnp.bfloat16),
             pltpu.VMEM((N * PAIRS, 2 * K), jnp.float32),
         ],
-        compiler_params=pltpu.CompilerParams(vmem_limit_bytes=VMEM_BYTES),
+        compiler_params=pltpu.CompilerParams(vmem_limit_bytes=40 << 20),
         cost_estimate=pl.CostEstimate(
             flops=4_000_000_000, bytes_accessed=6_000_000, transcendentals=0
         ),
-    )(low, own, high, tops, counts, coupling, links, basis, near)
+    )(place, low, own, high, counts, coupling, links, basis, near, *tops)
 
 
 def source_columns(far_src, top_src, position, subtrees, height):
@@ -541,22 +540,40 @@
         lax.dynamic_slice_in_dim(top_cls, position, 1, 0),
         lax.dynamic_slice_in_dim(top_cls, subtrees + position // 2, 1, 0),
     )
-    counts = class_counts(columns, classes, class_count, 2 * height)
-
     forward = [(i, i + 1) for i in range(subtrees - 1)]
     backward = [(i + 1, i) for i in range(subtrees - 1)]
-    for_high, for_low, counts, links = lax.optimization_barrier((for_high, for_low, counts, links))
+    for_high, for_low, columns = lax.optimization_barrier((for_high, for_low, columns))
     from_low = lax.ppermute(for_high, "leaf", forward)
     from_high = lax.ppermute(for_low, "leaf", backward)
+    counts = class_counts(columns, classes, class_count, 2 * height)
+
     basis_pairs = whole_basis.reshape(B // 2, 2 * K, M)
     coefs, first, last, root = upward(values, basis_pairs, links)
-    tops = lax.all_gather(root, "leaf", axis=0)
     low = lax.ppermute(last, "leaf", forward)
     high = lax.ppermute(first, "leaf", backward)
     near_src, coefs = lax.optimization_barrier((near_src, coefs))
-    near = near_field(near_src, from_low, packed, from_high, targets)
-    tops = lax.slice_in_dim(tops, 0, 1, axis=1)
-    return downward(low, coefs, high, tops, counts, coupling_t, links, basis_pairs, near)
+    near = near_field(1, near_src, packed, targets)
+
+    is_even = position % 2 == 0
+    other = jnp.where(is_even, high[N, :N], low[N, :N])
+    duo = jnp.where(is_even, jnp.stack([root, other]), jnp.stack([other, root]))
+    tops = [duo]
+    layers = [(0, from_low), (2, from_high)]
+    step = 2
+    while step < subtrees:
+        known = jnp.concatenate(tops, axis=0) if len(tops) > 1 else duo
+        known, near = lax.optimization_barrier((known, near))
+        tops.append(lax.ppermute(known, "leaf", [(i, i ^ step) for i in range(subtrees)]))
+        if layers:
+            layer, source = layers.pop(0)
+            near = near_field(layer, near_src, source, targets, near)
+        step *= 2
+    for layer, source in layers:
+        near = near_field(layer, near_src, source, targets, near)
+    place = jnp.full((1,), 0, jnp.int32) + position
+    return downward(
+        place, low, coefs, high, counts, coupling_t, links, basis_pairs, near, tops
+    )
 
 
 def solution(mesh):

time: 118 us -> 98.5 us (0.83)
  Pallas kernels: 65.8 us -> 50.3 us
  waiting for transfers between devices: 16.3 us -> 1.06 us
  starting transfers between devices: 12.2 us -> 19.1 us
  local copies, waits for them, and re-layouts: 7.74 us -> 11.8 us
    ppermute x1, waiting for transfers between devices: 15.6 us -> 0.01 us  [per_device(): from_low = lax.ppermute(for_high, 'leaf', forward)]
    unnamed x14 -> x44, local copies, waits for them, and re-layouts: 2.01 us -> 9.26 us
    ppermute x0 -> x2, starting transfers between devices: none -> 6.42 us  [per_device(): lax.ppermute(known, 'leaf', [(i, i ^ step) for i in range(subtrees)])]
    pallas_call x1 -> x3, Pallas kernels: 36.7 us -> 30.6 us  [near_field(): pl.pallas_call(functools.partial(near_kernel, layer), name=('near_low', '...]
    pallas_call x1, Pallas kernels: 12.8 us -> 10.6 us  [downward(): pl.pallas_call(down_kernel, name='downward', out_shape=jax.ShapeDtypeStru...]
    pallas_call x1, Pallas kernels: 4.3 us -> 2.13 us  [relay(): pl.pallas_call(relay_kernel, name='relay', out_shape=[jax.ShapeDtypeStruc...]
    pallas_call x1, Pallas kernels: 4.69 us -> 2.64 us  [class_counts(): pl.pallas_call(counts_kernel, name='class_counts', out_shape=jax.ShapeDty...]
    pallas_call x1, Pallas kernels: 4.4 us -> 2.74 us  [upward(): pl.pallas_call(up_kernel, name='upward', out_shape=[jax.ShapeDtypeStruct(...]
  transfers between devices with their start and end apart: 6 -> 7, of which waited for: 1 -> 1; matrix products, arithmetic and copies ran while one was open for 7% -> 5% of each run, Pallas kernels for 45% -> 41%
where the time goes in v6:
time: 98.5 us; the launch traced here: 97.8 us
  Pallas kernels  50.3 us (51%)
  starting transfers between devices  19.1 us (19%)
  between operations  13.7 us (14%)
  local copies, waits for them, and re-layouts  11.8 us (12%)
  other arithmetic  1.83 us (2%)
  waiting for transfers between devices  1.06 us (1%)
    pallas_call x3, Pallas kernels, near_field(): pl.pallas_call(functools.partial(near_kernel, layer), name=('near_low', '...  30.6 us
    pallas_call x1, Pallas kernels, downward(): pl.pallas_call(down_kernel, name='downward', out_shape=jax.ShapeDtypeStru...  10.6 us
    unnamed x44, local copies, waits for them, and re-layouts  9.26 us
    ppermute x2, starting transfers between devices, per_device(): lax.ppermute(known, 'leaf', [(i, i ^ step) for i in range(subtrees)])  6.42 us
    ppermute x1, starting transfers between devices, per_device(): from_low = lax.ppermute(for_high, 'leaf', forward)  5.68 us
    ppermute x1, starting transfers between devices, per_device(): low = lax.ppermute(last, 'leaf', forward)  4.25 us
    pallas_call x1, Pallas kernels, upward(): pl.pallas_call(up_kernel, name='upward', out_shape=[jax.ShapeDtypeStruct(...  2.74 us
    pallas_call x1, Pallas kernels, class_counts(): pl.pallas_call(counts_kernel, name='class_counts', out_shape=jax.ShapeDty...  2.64 us
  transfers between devices with their start and end apart: 7, of which 1 were waited for; matrix products, arithmetic and copies ran while one was open for 5% of the time, Pallas kernels for 41%

profile of v6, /device:TPU:0, one launch (start us, length us, event | category | flops | bytes accessed | tf_op | source)
XLA Modules:
  0.0 97.8 jit_solution(6213046790429843310)
XLA Ops:
  6.5 0.0 all-gather.2.cloned.1.call-start
  6.5 0.7 all-gather.2.cloned.1.call-update
  7.3 0.7 constant_dynamic-slice_fusion.1
  8.0 0.1 copy.60
  8.1 0.1 copy.59
  8.2 0.1 pad_maximum_fusion.1.centre_ref
  8.3 0.9 copy-done
  9.2 0.9 copy-done.6
  10.1 1.6 %pack.1 = (bf16[32,8192]{1,0:T(8,128)(2,1)S(1)}, bf16[32,8192]{1,0:T(8,128)(2,1)}, bf16[32,8192]{1,0:T(8,128)(2,1)S(1)}, bf16[16,8192]{1,0:T(8,128)(2,1)S(1)}) custom-call(f32[3]{0:T(128)S(1)} %pad_maximum_fusion.1.centre_ref, bf16[16,8192]{1,0:T(8,128)(2,1)S(1)} %copy-done, f32[3,8192]{1,0:T(4,128)S(1)} %copy-done.6), custom_call_target="tpu_custom_call" | custom-call | flops 1000 | bytes 100000 | tf_op jit(solution)/shard_map/pack/pallas_call | solution.py:86
  11.8 0.8 copy-done.7
  12.6 0.8 add_select_fusion.5
  13.3 0.8 fusion.5
  14.1 0.1 copy.44
  14.3 0.1 fusion.15
  14.4 0.1 copy.45
  14.4 0.1 copy.47
  14.5 0.1 pad_add_fusion
  14.6 5.7 %collective-permute-start.4 = (bf16[32,8192]{1,0:T(8,128)(2,1)}, bf16[32,8192]{1,0:T(8,128)(2,1)}, u32[]{:S(2)}, u32[]{:S(2)}) collective-permute-start(bf16[32,8192]{1,0:T(8,128)(2,1)} %get-tuple-element.39), channel_id=1, source_target_pairs={{0,4},{4,8},{8,12},{12,16},{16,20},{20,24},{24,28},{1,5},{5,9},{9,... | collective-permute-start | bytes 1572872 | tf_op jit(solution)/shard_map/ppermute | solution.py:546
  20.3 1.3 %collective-permute-start.2 = (bf16[32,8192]{1,0:T(8,128)(2,1)S(1)}, bf16[32,8192]{1,0:T(8,128)(2,1)}, u32[]{:S(2)}, u32[]{:S(2)}) collective-permute-start(bf16[32,8192]{1,0:T(8,128)(2,1)S(1)} %get-tuple-element.34), channel_id=1, source_target_pairs={{4,0},{8,4},{12,8},{16,12},{20,16},{24,20},{28,24},{5,1},{9,5},{13... | collective-permute-start | bytes 1572872 | tf_op jit(solution)/shard_map/ppermute | solution.py:547
  21.6 0.1 copy.54.col_ref
  21.7 0.1 copy.61
  21.8 0.1 copy.62
  21.8 0.0 copy-done.19
  21.8 0.1 slice.27
  21.9 0.1 copy.49
  22.1 0.1 fusion.14
  22.1 0.1 copy.50
  22.2 0.1 copy.52
  22.3 0.1 pad_add_fusion.1
  22.4 0.1 copy.55.cls_ref
  22.5 0.0 copy-done.11
  22.5 0.0 copy-done.5
  22.5 0.0 copy-done.2
  22.5 2.1 %relay.1 = (bf16[64,64,128]{2,1,0:T(8,128)(2,1)S(1)}, bf16[24,64,64]{2,1,0:T(8,128)(2,1)S(1)}) custom-call(bf16[127,4096]{1,0:T(8,128)(2,1)S(1)} %copy-done.2, bf16[24,4096]{1,0:T(8,128)(2,1)S(1)} %copy-done.5), custom_call_target="tpu_custom_call" | custom-call | flops 1000 | bytes 100000 | tf_op jit(solution)/shard_map/relay/pallas_call | solution.py:223
  24.6 0.0 copy-start.9
  24.7 0.7 copy-done.9
  25.4 2.6 %class_counts.1.a_ref = bf16[24,128,256]{2,1,0:T(8,128)(2,1)S(1)} custom-call(s32[128,24]{1,0:T(8,128)S(1)} %copy.54.col_ref, s32[128,24]{1,0:T(8,128)S(1)} %copy.55.cls_ref), custom_call_target="tpu_custom_call" | custom-call | flops 1000 | bytes 100000 | tf_op jit(solution)/shard_map/class_counts/pallas_call | solution.py:277
  28.1 0.3 all-gather.2.cloned.1.call-done
  28.4 0.0 copy-done.1
  28.4 1.2 %copy-done.3 = bf16[64,64,128]{2,1,0:T(8,128)(2,1)S(1)} copy-done((bf16[64,64,128]{2,1,0:T(8,128)(2,1)S(1)}, bf16[64,64,128]{2,1,0:T(8,128)(2,1)}, u32[]{:S(2)}) %copy-start.3) | copy-done | bytes 1048600
  29.6 2.7 %upward.1 = (bf16[16,64,128]{2,1,0:T(8,128)(2,1)S(1)}, bf16[17,32,128]{2,1,0:T(8,128)(2,1)}, bf16[17,32,128]{2,1,0:T(8,128)(2,1)}, bf16[16,128]{1,0:T(8,128)(2,1)S(1)}) custom-call(bf16[16,8192]{1,0:T(8,128)(2,1)S(1)} %copy-done.1, bf16[32,128,128]{2,1,0:T(8,128)(2,1)S(1)} %bitcast.8, bf16[64,64,128]{2,1,0:T(8,128)(2,1)S(1)} %get-tuple-element.24.links_ref), custom_call_target="tpu_custom_call" | custom-call | flops 300000000 | bytes 3000000 | tf_op jit(solution)/shard_map/upward/pallas_call | solution.py:343
  32.4 0.7 copy-done.14
  33.1 4.2 %collective-permute-start = (bf16[17,32,128]{2,1,0:T(8,128)(2,1)}, bf16[17,32,128]{2,1,0:T(8,128)(2,1)S(1)}, u32[]{:S(2)}, u32[]{:S(2)}) collective-permute-start(bf16[17,32,128]{2,1,0:T(8,128)(2,1)} %get-tuple-element.25), channel_id=1, source_target_pairs={{0,4},{4,8},{8,12},{12,16},{16,20},{20,24},{24,28},{1,5},{5,9},{9,... | collective-permute-start | bytes 417800 | tf_op jit(solution)/shard_map/ppermute | solution.py:552
  37.3 1.5 %collective-permute-start.1 = (bf16[17,32,128]{2,1,0:T(8,128)(2,1)}, bf16[17,32,128]{2,1,0:T(8,128)(2,1)S(1)}, u32[]{:S(2)}, u32[]{:S(2)}) collective-permute-start(bf16[17,32,128]{2,1,0:T(8,128)(2,1)} %get-tuple-element.28), channel_id=1, source_target_pairs={{4,0},{8,4},{12,8},{16,12},{20,16},{24,20},{28,24},{5,1},{9,5},{13... | collective-permute-start | bytes 417800 | tf_op jit(solution)/shard_map/ppermute | solution.py:553
  38.8 0.8 copy.58.near_ref
  39.6 1.0 %copy-done.8 = bf16[32,8192]{1,0:T(8,128)(2,1)S(1)} copy-done((bf16[32,8192]{1,0:T(8,128)(2,1)S(1)}, bf16[32,8192]{1,0:T(8,128)(2,1)}, u32[]{:S(2)}) %copy-start.8) | copy-done | bytes 524312
  40.7 0.9 copy-done.12
  41.6 0.9 copy-done.16
  42.5 0.7 copy-done.17
  43.2 10.2 %near_own.1.rest_0_ = f32[16,8192]{1,0:T(8,128)S(1)} custom-call(s32[64,27]{1,0:T(8,128)S(1)} %copy.58.near_ref, bf16[32,8192]{1,0:T(8,128)(2,1)S(1)} %copy-done.8, bf16[16,8192]{1,0:T(8,128)(2,1)S(1)} %copy-done.12, bf16[96,384]{1,0:T(8,128)(2,1)S(1)} %copy-done.16, bf16[32,16]{1,0:T(8,128)(2,1)S(1)} %copy-done.17), custom_call_target="tpu_custom_call" | custom-call | flops 7000000000 | bytes 2000000 | tf_op jit(solution)/shard_map/near_own/pallas_call | solution.py:178
  53.4 0.0 collective-permute-done.low_ref
  53.4 0.0 collective-permute-done.1.high_ref
  53.4 3.8 %collective-permute-start.3 = (bf16[2,16,128]{2,1,0:T(8,128)(2,1)S(1)}, bf16[2,16,128]{2,1,0:T(8,128)(2,1)S(1)}, u32[]{:S(2)}, u32[]{:S(2)}) collective-permute-start(bf16[2,16,128]{2,1,0:T(8,128)(2,1)S(1)} %maximum_select_fusion.rest_0_), channel_id=1, source_target_pairs={{0,8},{4,12},{8,0},{12,4},{16,24},{20,28},{24,16},{28,20},{1,9},{5... | collective-permute-start | bytes 24584 | tf_op jit(solution)/shard_map/ppermute | solution.py:566
  57.2 0.0 collective-permute-done.4.src_ref
  57.2 0.0 copy-done.13
  57.2 0.0 copy-done.18
  57.2 10.2 %near_low.1.rest_0_ = f32[16,8192]{1,0:T(8,128)S(1)} custom-call(s32[64,27]{1,0:T(8,128)S(1)} %copy.58.near_ref, bf16[32,8192]{1,0:T(8,128)(2,1)} %collective-permute-done.4.src_ref, bf16[16,8192]{1,0:T(8,128)(2,1)S(1)} %copy-done.13, bf16[96,384]{1,0:T(8,128)(2,1)S(1)} %copy-done.16, bf16[32,16]{1,0:T(8,128)(2,1)S(1)} %copy-done.18, ...), custom_call_target="tpu_custom_call" | custom-call | flops 7000000000 | bytes 2000000 | tf_op jit(solution)/shard_map/near_low/pallas_call | solution.py:178
  67.4 0.0 collective-permute-done.3.rest_1_
  67.5 0.0 copy-start.15
  67.5 2.7 %collective-permute-start.5 = (bf16[4,16,128]{2,1,0:T(8,128)(2,1)S(1)}, bf16[4,16,128]{2,1,0:T(8,128)(2,1)S(1)}, u32[]{:S(2)}, u32[]{:S(2)}) collective-permute-start(bf16[4,16,128]{2,1,0:T(8,128)(2,1)S(1)} %pad_maximum_fusion), channel_id=1, source_target_pairs={{0,16},{4,20},{8,24},{12,28},{16,0},{20,4},{24,8},{28,12},{1,17},{... | collective-permute-start | bytes 49160 | tf_op jit(solution)/shard_map/ppermute | solution.py:566
  70.1 0.0 collective-permute-done.2.src_ref
  70.1 10.2 %near_high.1.near_ref = f32[16,8192]{1,0:T(8,128)S(1)} custom-call(s32[64,27]{1,0:T(8,128)S(1)} %copy.58.near_ref, bf16[32,8192]{1,0:T(8,128)(2,1)} %collective-permute-done.2.src_ref, bf16[16,8192]{1,0:T(8,128)(2,1)S(1)} %copy-done.13, bf16[96,384]{1,0:T(8,128)(2,1)S(1)} %copy-done.16, bf16[32,16]{1,0:T(8,128)(2,1)S(1)} %copy-done.18, ...), custom_call_target="tpu_custom_call" | custom-call | flops 7000000000 | bytes 2000000 | tf_op jit(solution)/shard_map/near_high/pallas_call | solution.py:178
  80.3 0.0 collective-permute-done.5.rest_2_
  80.4 10.6 %downward.1 = bf16[16,8192]{1,0:T(8,128)(2,1)} custom-call(s32[1]{0:T(128)} %bitcast.place_ref, bf16[17,32,128]{2,1,0:T(8,128)(2,1)S(1)} %collective-permute-done.low_ref, bf16[16,64,128]{2,1,0:T(8,128)(2,1)S(1)} %copy-done.15, bf16[17,32,128]{2,1,0:T(8,128)(2,1)S(1)} %collective-permute-done.1.high_ref, bf16[24,128,256]{2,1,0:T(8,128)(2,1)S(1)} %class_counts.1.a_ref, ...), custom_call_target="tpu_custom_call" | custom-call | flops 4000000000 | bytes 6000000 | tf_op jit(solution)/shard_map/downward/pallas_call | solution.py:467
  (28 shorter events, 0.1 us)
Async XLA Ops:
  6.5 15.3 %copy-start.19 = (s32[127,24]{0,1:T(8,128)S(1)}, s32[127,24]{0,1:T(8,128)}, u32[]{:S(2)}) copy-start(s32[127,24]{0,1:T(8,128)} %param.23) | copy-start | bytes 36580
  6.5 16.0 %copy-start.5 = (bf16[24,4096]{1,0:T(8,128)(2,1)S(1)}, bf16[24,4096]{1,0:T(8,128)(2,1)}, u32[]{:S(2)}) copy-start(bf16[24,4096]{1,0:T(8,128)(2,1)} %coupling_ref.1) | copy-start | bytes 589828
  6.5 21.9 %all-gather.2.cloned.1.call-start = ((), (), s32[]{:S(2)}) async-start(), calls=%async_computation | async-start | bytes 1310720 | tf_op jit(solution)/shard_map/all_gather | solution.py:530
  8.3 1.0 copy-start
  9.2 0.9 copy-start.6
  10.1 12.4 %copy-start.2 = (bf16[127,4096]{1,0:T(8,128)(2,1)S(1)}, bf16[127,4096]{1,0:T(8,128)(2,1)}, u32[]{:S(2)}) copy-start(bf16[127,4096]{1,0:T(8,128)(2,1)} %transfer_ref.1) | copy-start | bytes 3121156
  11.8 0.8 copy-start.7
  12.6 9.9 %copy-start.11 = (bf16[16,8192]{1,0:T(8,128)(2,1)}, bf16[16,8192]{1,0:T(8,128)(2,1)S(1)}, u32[]{:S(2)}) copy-start(bf16[16,8192]{1,0:T(8,128)(2,1)S(1)} %get-tuple-element.35.xs_ref) | copy-start | bytes 786436
  14.6 42.6 %collective-permute-start.4 = (bf16[32,8192]{1,0:T(8,128)(2,1)}, bf16[32,8192]{1,0:T(8,128)(2,1)}, u32[]{:S(2)}, u32[]{:S(2)}) collective-permute-start(bf16[32,8192]{1,0:T(8,128)(2,1)} %get-tuple-element.39), channel_id=1, source_target_pairs={{0,4},{4,8},{8,12},{12,16},{16,20},{20,24},{24,28},{1,5},{5,9},{9,... | collective-permute-start | bytes 1572872 | tf_op jit(solution)/shard_map/ppermute | solution.py:546
  20.3 49.8 %collective-permute-start.2 = (bf16[32,8192]{1,0:T(8,128)(2,1)S(1)}, bf16[32,8192]{1,0:T(8,128)(2,1)}, u32[]{:S(2)}, u32[]{:S(2)}) collective-permute-start(bf16[32,8192]{1,0:T(8,128)(2,1)S(1)} %get-tuple-element.34), channel_id=1, source_target_pairs={{4,0},{8,4},{12,8},{16,12},{20,16},{24,20},{28,24},{5,1},{9,5},{13... | collective-permute-start | bytes 1572872 | tf_op jit(solution)/shard_map/ppermute | solution.py:547
  22.2 6.2 %copy-start.1 = (bf16[16,8192]{1,0:T(8,128)(2,1)S(1)}, bf16[16,8192]{1,0:T(8,128)(2,1)}, u32[]{:S(2)}) copy-start(bf16[16,8192]{1,0:T(8,128)(2,1)} %values_ref.3) | copy-start | bytes 786436
  24.6 0.8 copy-start.9
  28.4 1.2 %copy-start.3 = (bf16[64,64,128]{2,1,0:T(8,128)(2,1)S(1)}, bf16[64,64,128]{2,1,0:T(8,128)(2,1)}, u32[]{:S(2)}) copy-start(bf16[64,64,128]{2,1,0:T(8,128)(2,1)} %all-gather.2.cloned.1.call-done) | copy-start | bytes 3145732
  32.4 0.7 copy-start.14
  33.1 20.3 %collective-permute-start = (bf16[17,32,128]{2,1,0:T(8,128)(2,1)}, bf16[17,32,128]{2,1,0:T(8,128)(2,1)S(1)}, u32[]{:S(2)}, u32[]{:S(2)}) collective-permute-start(bf16[17,32,128]{2,1,0:T(8,128)(2,1)} %get-tuple-element.25), channel_id=1, source_target_pairs={{0,4},{4,8},{8,12},{12,16},{16,20},{20,24},{24,28},{1,5},{5,9},{9,... | collective-permute-start | bytes 417800 | tf_op jit(solution)/shard_map/ppermute | solution.py:552
  37.3 16.1 %collective-permute-start.1 = (bf16[17,32,128]{2,1,0:T(8,128)(2,1)}, bf16[17,32,128]{2,1,0:T(8,128)(2,1)S(1)}, u32[]{:S(2)}, u32[]{:S(2)}) collective-permute-start(bf16[17,32,128]{2,1,0:T(8,128)(2,1)} %get-tuple-element.28), channel_id=1, source_target_pairs={{4,0},{8,4},{12,8},{16,12},{20,16},{24,20},{28,24},{5,1},{9,5},{13... | collective-permute-start | bytes 417800 | tf_op jit(solution)/shard_map/ppermute | solution.py:553
  39.6 1.0 %copy-start.8 = (bf16[32,8192]{1,0:T(8,128)(2,1)S(1)}, bf16[32,8192]{1,0:T(8,128)(2,1)}, u32[]{:S(2)}) copy-start(bf16[32,8192]{1,0:T(8,128)(2,1)} %copy-done.7) | copy-start | bytes 1572868
  40.6 0.9 copy-start.12
  41.6 0.9 copy-start.16
  42.5 0.7 copy-start.17
  43.2 14.0 %copy-start.13 = (bf16[16,8192]{1,0:T(8,128)(2,1)S(1)}, bf16[16,8192]{1,0:T(8,128)(2,1)}, u32[]{:S(2)}) copy-start(bf16[16,8192]{1,0:T(8,128)(2,1)} %copy-done.11) | copy-start | bytes 786436
  43.2 14.0 %copy-start.18 = (bf16[32,16]{1,0:T(8,128)(2,1)S(1)}, bf16[32,16]{1,0:T(8,128)(2,1)}, u32[]{:S(2)}) copy-start(bf16[32,16]{1,0:T(8,128)(2,1)} %constant.132.clone.target_ref) | copy-start | bytes 3076
  53.4 14.0 %collective-permute-start.3 = (bf16[2,16,128]{2,1,0:T(8,128)(2,1)S(1)}, bf16[2,16,128]{2,1,0:T(8,128)(2,1)S(1)}, u32[]{:S(2)}, u32[]{:S(2)}) collective-permute-start(bf16[2,16,128]{2,1,0:T(8,128)(2,1)S(1)} %maximum_select_fusion.rest_0_), channel_id=1, source_target_pairs={{0,8},{4,12},{8,0},{12,4},{16,24},{20,28},{24,16},{28,20},{1,9},{5... | collective-permute-start | bytes 24584 | tf_op jit(solution)/shard_map/ppermute | solution.py:566
  67.4 12.9 %copy-start.4 = (bf16[64,64,128]{2,1,0:T(8,128)(2,1)S(1)}, bf16[64,64,128]{2,1,0:T(8,128)(2,1)}, u32[]{:S(2)}) copy-start(bf16[64,64,128]{2,1,0:T(8,128)(2,1)} %all-gather.2.cloned.1.call-done) | copy-start | bytes 3145732
  67.4 12.9 %copy-start.10 = (bf16[24,64,64]{2,1,0:T(8,128)(2,1)S(1)}, bf16[24,64,64]{2,1,0:T(8,128)(2,1)}, u32[]{:S(2)}) copy-start(bf16[24,64,64]{2,1,0:T(8,128)(2,1)} %copy-done.9) | copy-start | bytes 589828
  67.5 12.9 %copy-start.15 = (bf16[16,64,128]{2,1,0:T(8,128)(2,1)S(1)}, bf16[16,64,128]{2,1,0:T(8,128)(2,1)}, u32[]{:S(2)}) copy-start(bf16[16,64,128]{2,1,0:T(8,128)(2,1)} %copy-done.14) | copy-start | bytes 786436
  67.5 12.9 %collective-permute-start.5 = (bf16[4,16,128]{2,1,0:T(8,128)(2,1)S(1)}, bf16[4,16,128]{2,1,0:T(8,128)(2,1)S(1)}, u32[]{:S(2)}, u32[]{:S(2)}) collective-permute-start(bf16[4,16,128]{2,1,0:T(8,128)(2,1)S(1)} %pad_maximum_fusion), channel_id=1, source_target_pairs={{0,16},{4,20},{8,24},{12,28},{16,0},{20,4},{24,8},{28,12},{1,17},{... | collective-permute-start | bytes 49160 | tf_op jit(solution)/shard_map/ppermute | solution.py:566
Sparse Core Ops, SparseCore 0:
  8.9 19.4 all-gather.1

commit v7 on v6

--- a/solution.py
+++ b/solution.py
@@ -94,26 +94,35 @@
     )(centre, values, coords)
 
 
+def terms(lane):
+    k = (lane >= 6).astype(jnp.int32) + (lane >= 12).astype(jnp.int32)
+    r = lane - 6 * k
+    i = jnp.where((r == 2) | (r == 3), 1, jnp.where(r == 5, 2, 0))
+    j = jnp.where((r == 1) | (r == 3), 1, jnp.where(r == 4, 2, 0))
+    size = 9 + ((lane - 18) >> 1)
+    even = (lane & 1) == 0
+    y = jnp.where(lane < 18, 3 * k + i, jnp.where(even, size, ONE))
+    x = jnp.where(lane < 18, 3 * k + j, jnp.where(even, ONE, size))
+    return jnp.where(lane < 24, y, -1000), jnp.where(lane < 24, x, -1000)
+
+
 def near_tables():
-    lanes = []
-    for k in range(3):
-        for i, j in ((0, 0), (0, 1), (1, 0), (1, 1), (0, 2), (2, 0)):
-            lanes.append((3 * k + i, 3 * k + j))
-    for i in range(3):
-        lanes += [(9 + i, ONE), (ONE, 9 + i)]
-    source = np.zeros(((QUAD + 2) * POINT_ROWS, 3 * M), np.float32)
-    target = np.zeros((LANES, POINT_ROWS), np.float32)
-    for lane, (y, x) in enumerate(lanes):
-        target[lane, x] = 1
-        for step in range(3):
-            for i in range(QUAD):
-                source[POINT_ROWS * (step + i) + y, M * step + LANES * i + lane] = 1
-    return [jnp.asarray(x, jnp.bfloat16) for x in (source, target)]
-
-
-def near_kernel(layer, near_ref, src_ref, xs_ref, source_ref, target_ref, *rest):
+    shape = ((QUAD + 2) * POINT_ROWS, 3 * M)
+    row = lax.broadcasted_iota(jnp.int32, shape, 0)
+    column = lax.broadcasted_iota(jnp.int32, shape, 1)
+    box = (column >> 7) + ((column & (M - 1)) >> 5)
+    y, _ = terms(column & (LANES - 1))
+    source = jnp.where(row == POINT_ROWS * box + y, 1.0, 0.0).astype(jnp.bfloat16)
+    shape = (LANES, POINT_ROWS)
+    _, x = terms(lax.broadcasted_iota(jnp.int32, shape, 0))
+    target = jnp.where(lax.broadcasted_iota(jnp.int32, shape, 1) == x, 1.0, 0.0)
+    return source, target.astype(jnp.bfloat16)
+
+
+def near_kernel(layer, near_ref, src_ref, xs_ref, *rest):
     before_ref = rest[0] if len(rest) == 4 else None
     out_ref, yq_ref, w_ref = rest[-3:]
+    source, target = near_tables()
 
     def at(u):
         return pl.ds(pl.multiple_of(jnp.clip(u, 0, B - 1) * M, M), M)
@@ -121,10 +130,10 @@
     def features(q, carry):
         t = QUAD * q
         rows = jnp.concatenate([src_ref[N:, at(t + i)] for i in range(-1, QUAD + 1)], axis=0)
-        wide = dot(rows, source_ref[...], TN).astype(jnp.bfloat16)
+        wide = dot(rows, source, TN).astype(jnp.bfloat16)
         for step in range(3):
             yq_ref[q, step * M : (step + 1) * M, :] = wide[:, step * M : (step + 1) * M]
-        tiles = [dot(target_ref[...], xs_ref[:, at(t + i)]).astype(jnp.bfloat16) for i in range(QUAD)]
+        tiles = [dot(target, xs_ref[:, at(t + i)]).astype(jnp.bfloat16) for i in range(QUAD)]
         zero = jnp.zeros((LANES, M), jnp.bfloat16)
         for i in range(QUAD):
             w_ref[q, LANES * i : LANES * (i + 1), :] = jnp.concatenate(
@@ -174,7 +183,7 @@
 
 
 def near_field(layer, near_src, src, targets, before=None):
-    operands = [near_src, src, targets, *near_tables()] + ([] if before is None else [before])
+    operands = [near_src, src, targets] + ([] if before is None else [before])
     return pl.pallas_call(
         functools.partial(near_kernel, layer),
         name=("near_low", "near_own", "near_high")[layer],
@@ -238,9 +247,47 @@
     )(transfer, coupling)
 
 
-def counts_kernel(col_ref, cls_ref, a_ref):
+def counts_kernel(
+    place_ref, far_src_ref, far_cls_ref, top_src_ref, top_cls_ref, a_ref, col_ref, cls_ref
+):
     classes = a_ref.shape[0]
     width = a_ref.shape[2]
+    height = width // 2
+    place = place_ref[0]
+    subtrees = top_src_ref.shape[0] * 2 // 3
+
+    def column(source):
+        owner = jnp.floor((source.astype(jnp.float32) + 0.5) * (1.0 / TB)).astype(jnp.int32)
+        slot = source - TB * owner
+        count = jnp.ones_like(slot)
+        for bit in range(1, 7):
+            count = jnp.where(slot + 1 >= 2**bit, 2**bit, count)
+        pairs = count >> 1
+        first = pairs - 1
+        inside = (slot - (count - 1)) >> 1
+        rim_first = jnp.where(count <= 16, first, jnp.where(count == 32, 14, 21))
+        side = owner - place
+        low = PAIRS + rim_first + inside - (pairs - jnp.minimum(pairs, 7))
+        row = jnp.where(
+            side == 0, first + inside, jnp.where(side < 0, low, PAIRS + RIM + rim_first + inside)
+        )
+        return jnp.where(source >= 0, row + ((slot + 1) & 1) * height, -1)
+
+    base = PAIRS + 2 * RIM
+    last = PAIRS - 1
+    for parity in range(2):
+        rows = pl.ds(1 + parity, last, stride=2)
+        col_ref[parity * PAIRS : parity * PAIRS + last, :] = column(far_src_ref[rows, :])
+        cls_ref[parity * PAIRS : parity * PAIRS + last, :] = far_cls_ref[rows, :]
+    root, top = pl.ds(place, 1), pl.ds(subtrees + (place >> 1), 1)
+    roots, tops = top_src_ref[root, :], top_src_ref[top, :]
+    col_ref[last : last + 1, :] = jnp.where(roots >= 0, base + roots, -1)
+    col_ref[PAIRS + last : PAIRS + last + 1, :] = jnp.where(
+        tops >= 0, height + base + 2 * tops, -1
+    )
+    cls_ref[last : last + 1, :] = top_cls_ref[root, :]
+    cls_ref[PAIRS + last : PAIRS + last + 1, :] = top_cls_ref[top, :]
+
     slots = col_ref.shape[1]
     spread = slots * 8
     lane = lax.broadcasted_iota(jnp.int32, (slots, spread), 1)
@@ -273,18 +320,17 @@
     lax.fori_loop(0, 2 * PAIRS // 16, block, 0)
 
 
-def class_counts(columns, classes, class_count, width):
+def class_counts(place, far_src, far_cls, top_src, top_cls, class_count, width):
     return pl.pallas_call(
         counts_kernel,
         name="class_counts",
         out_shape=jax.ShapeDtypeStruct((class_count, 2 * PAIRS, width), jnp.bfloat16),
-        in_specs=[vmem()] * 2,
+        in_specs=[pl.BlockSpec(memory_space=pltpu.SMEM)] + [vmem()] * 4,
         out_specs=vmem(),
+        scratch_shapes=[pltpu.VMEM((2 * PAIRS, far_src.shape[1]), jnp.int32)] * 2,
         compiler_params=pltpu.CompilerParams(vmem_limit_bytes=20 << 20),
-        cost_estimate=pl.CostEstimate(
-            flops=1000, bytes_accessed=100_000, transcendentals=0
-        ),
-    )(columns, classes)
+        cost_estimate=pl.CostEstimate(flops=1000, bytes_accessed=100_000, transcendentals=0),
+    )(place, far_src, far_cls, top_src, top_cls)
 
 
 FIRST_ROWS = tuple(range(14)) + tuple(range(15, 22)) + tuple(range(31, 38))
@@ -423,18 +469,23 @@
 
     lax.fori_loop(0, classes, spread, 0)
 
-    for c in range(classes):
-        grouped = dot(a_ref[c], call_ref[...]).astype(jnp.bfloat16)
-        for m in range(N // 2):
+    counts = a_ref[...].reshape(classes * 2 * PAIRS, 2 * height)
+    wide = N * K // 2
+    for half in range(2):
+        grouped = dot(counts, call_ref[:, half * wide : (half + 1) * wide]).astype(jnp.bfloat16)
+        for c in range(classes):
             for parity in range(2):
-                lhs_ref[
-                    m * PAIRS : (m + 1) * PAIRS,
-                    (2 * c + parity) * 2 * K : (2 * c + parity + 1) * 2 * K,
-                ] = grouped[parity * PAIRS : (parity + 1) * PAIRS, m * 2 * K : (m + 1) * 2 * K]
+                row = (2 * c + parity) * PAIRS
+                for i in range(N // 4):
+                    m = half * (N // 4) + i
+                    lhs_ref[
+                        m * PAIRS : (m + 1) * PAIRS, (2 * c + parity) * 2 * K : (2 * c + parity + 1) * 2 * K
+                    ] = grouped[row : row + PAIRS, i * 2 * K : (i + 1) * 2 * K]
+    field = dot(lhs_ref[...], bd_ref[...])
     for m in range(N // 2):
-        field = dot(lhs_ref[m * PAIRS : (m + 1) * PAIRS, :], bd_ref[...])
-        fs_ref[2 * m * PAIRS : (2 * m + 1) * PAIRS, :] = field[:, 0 : 2 * K]
-        fs_ref[(2 * m + 1) * PAIRS : (2 * m + 2) * PAIRS, :] = field[:, 2 * K : 4 * K]
+        rows = slice(m * PAIRS, (m + 1) * PAIRS)
+        fs_ref[2 * m * PAIRS : (2 * m + 1) * PAIRS, :] = field[rows, 0 : 2 * K]
+        fs_ref[(2 * m + 1) * PAIRS : (2 * m + 2) * PAIRS, :] = field[rows, 2 * K : 4 * K]
 
     def field_of(pair_index):
         return fs_ref[pl.ds(pair_index, N, stride=PAIRS), :]
@@ -484,41 +535,6 @@
     )(place, low, own, high, counts, coupling, links, basis, near, *tops)
 
 
-def source_columns(far_src, top_src, position, subtrees, height):
-    owner = far_src // TB
-    slot = far_src % TB
-    count = jnp.ones_like(slot)
-    for bit in range(1, 7):
-        count = jnp.where(slot + 1 >= 2**bit, 2**bit, count)
-    first = (count - 2) // 2
-    inside = (slot - (count - 1)) // 2
-    pairs = count // 2
-    width = jnp.minimum(pairs, 7)
-    rim_first = jnp.where(count <= 16, first, jnp.where(count == 32, 14, 21))
-    side = owner - position
-    row = jnp.where(
-        side == 0,
-        first + inside,
-        jnp.where(
-            side < 0,
-            PAIRS + rim_first + inside - (pairs - width),
-            PAIRS + RIM + rim_first + inside,
-        ),
-    )
-    column = jnp.where(far_src >= 0, row + ((slot - 1) % 2) * height, -1)
-    base = PAIRS + 2 * RIM
-    roots = lax.dynamic_slice_in_dim(top_src, position, 1, 0)
-    tops = lax.dynamic_slice_in_dim(top_src, subtrees + position // 2, 1, 0)
-    roots = jnp.where(roots >= 0, base + roots, -1)
-    tops = jnp.where(tops >= 0, height + base + 2 * tops, -1)
-    return by_parity(column, roots, tops)
-
-
-def by_parity(rows, root, top):
-    paired = rows[1:].reshape(PAIRS - 1, 2, rows.shape[1])
-    return jnp.concatenate([paired[:, 0], root, paired[:, 1], top], axis=0)
-
-
 def per_device(
     values, coords, basis, transfer, coupling, near_src, far_src, far_cls, top_src, top_cls
 ):
@@ -529,29 +545,23 @@
 
     whole_basis = lax.all_gather(basis, "vec", axis=0, tiled=True)
 
+    place = jnp.full((1,), 0, jnp.int32) + position
     middle = (ROW / 2, B // ROW / 2, position.astype(jnp.float32) + 0.5)
     centre = jnp.stack([jnp.asarray(x, jnp.float32) for x in middle])
     packed, for_high, for_low, targets = pack(centre, values, coords)
 
     links, coupling_t = relay(transfer, coupling)
-    columns = source_columns(far_src, top_src, position, subtrees, height)
-    classes = by_parity(
-        far_cls,
-        lax.dynamic_slice_in_dim(top_cls, position, 1, 0),
-        lax.dynamic_slice_in_dim(top_cls, subtrees + position // 2, 1, 0),
-    )
     forward = [(i, i + 1) for i in range(subtrees - 1)]
     backward = [(i + 1, i) for i in range(subtrees - 1)]
-    for_high, for_low, columns = lax.optimization_barrier((for_high, for_low, columns))
     from_low = lax.ppermute(for_high, "leaf", forward)
     from_high = lax.ppermute(for_low, "leaf", backward)
-    counts = class_counts(columns, classes, class_count, 2 * height)
+    counts = class_counts(place, far_src, far_cls, top_src, top_cls, class_count, 2 * height)
 
     basis_pairs = whole_basis.reshape(B // 2, 2 * K, M)
     coefs, first, last, root = upward(values, basis_pairs, links)
     low = lax.ppermute(last, "leaf", forward)
     high = lax.ppermute(first, "leaf", backward)
-    near_src, coefs = lax.optimization_barrier((near_src, coefs))
+    packed, coefs = lax.optimization_barrier((packed, coefs))
     near = near_field(1, near_src, packed, targets)
 
     is_even = position % 2 == 0
@@ -570,7 +580,6 @@
         step *= 2
     for layer, source in layers:
         near = near_field(layer, near_src, source, targets, near)
-    place = jnp.full((1,), 0, jnp.int32) + position
     return downward(
         place, low, coefs, high, counts, coupling_t, links, basis_pairs, near, tops
     )

time: 98.5 us -> 92.6 us (0.940)
  local copies, waits for them, and re-layouts: 11.8 us -> 8.52 us
  other arithmetic: 1.83 us -> 0.1 us
    select_n x4 -> x0, other arithmetic: 1.57 us -> none  [the longest x1 0.81 us: source_columns(): column = jnp.where(far_src >= 0, row + (slot - 1) % 2 * height, -1)]
    unnamed x44 -> x37, local copies, waits for them, and re-layouts: 9.26 us -> 8.52 us
  transfers between devices with their start and end apart: 7 -> 7, of which waited for: 1 -> 1; matrix products, arithmetic and copies ran while one was open for 5% -> 1% of each run, Pallas kernels for 41% -> 43%
where the time goes in v7:
time: 92.6 us; the launch traced here: 92.1 us
  Pallas kernels  49.6 us (54%)
  starting transfers between devices  19.5 us (21%)
  between operations  13.6 us (15%)
  local copies, waits for them, and re-layouts  8.52 us (9%)
    pallas_call x3, Pallas kernels, near_field(): pl.pallas_call(functools.partial(near_kernel, layer), name=('near_low', '...  30.8 us
    pallas_call x1, Pallas kernels, downward(): pl.pallas_call(down_kernel, name='downward', out_shape=jax.ShapeDtypeStru...  10.2 us
    unnamed x37, local copies, waits for them, and re-layouts  8.52 us
    ppermute x2, starting transfers between devices, per_device(): lax.ppermute(known, 'leaf', [(i, i ^ step) for i in range(subtrees)])  6.44 us
    ppermute x1, starting transfers between devices, per_device(): from_low = lax.ppermute(for_high, 'leaf', forward)  5.68 us
    ppermute x1, starting transfers between devices, per_device(): low = lax.ppermute(last, 'leaf', forward)  4.48 us
    pallas_call x1, Pallas kernels, class_counts(): pl.pallas_call(counts_kernel, name='class_counts', out_shape=jax.ShapeDty...  2.77 us
    pallas_call x1, Pallas kernels, relay(): pl.pallas_call(relay_kernel, name='relay', out_shape=[jax.ShapeDtypeStruc...  2.13 us
  transfers between devices with their start and end apart: 7, of which 1 were waited for; matrix products, arithmetic and copies ran while one was open for 1% of the time, Pallas kernels for 43%

profile of v7, /device:TPU:0, one launch (start us, length us, event | category | flops | bytes accessed | tf_op | source)
XLA Modules:
  0.0 92.1 jit_solution(9409601770282376865)
XLA Ops:
  6.5 0.0 copy-start.15
  6.5 0.0 copy-start.16
  6.5 0.0 copy-start.7
  6.5 0.0 copy-start.8
  6.5 0.0 all-gather.2.cloned.1.call-start
  6.6 0.7 all-gather.2.cloned.1.call-update
  7.3 0.1 pad_maximum_fusion.1.centre_ref
  7.4 0.0 copy-start
  7.4 0.9 %copy-done = bf16[16,8192]{1,0:T(8,128)(2,1)S(1)} copy-done((bf16[16,8192]{1,0:T(8,128)(2,1)S(1)}, bf16[16,8192]{1,0:T(8,128)(2,1)}, u32[]{:S(2)}) %copy-start) | copy-done | bytes 262168
  8.3 0.0 copy-start.6
  8.3 0.9 copy-done.6
  9.2 1.6 %pack.1 = (bf16[32,8192]{1,0:T(8,128)(2,1)S(1)}, bf16[32,8192]{1,0:T(8,128)(2,1)}, bf16[32,8192]{1,0:T(8,128)(2,1)S(1)}, bf16[16,8192]{1,0:T(8,128)(2,1)S(1)}) custom-call(f32[3]{0:T(128)S(1)} %pad_maximum_fusion.1.centre_ref, bf16[16,8192]{1,0:T(8,128)(2,1)S(1)} %copy-done, f32[3,8192]{1,0:T(4,128)S(1)} %copy-done.6), custom_call_target="tpu_custom_call" | custom-call | flops 1000 | bytes 100000 | tf_op jit(solution)/shard_map/pack/pallas_call | solution.py:86
  10.9 0.0 copy-start.9
  10.9 0.8 copy-done.9
  11.7 0.0 copy-start.13
  11.7 0.7 copy-done.13
  12.4 5.7 %collective-permute-start.4 = (bf16[32,8192]{1,0:T(8,128)(2,1)}, bf16[32,8192]{1,0:T(8,128)(2,1)}, u32[]{:S(2)}, u32[]{:S(2)}) collective-permute-start(bf16[32,8192]{1,0:T(8,128)(2,1)} %get-tuple-element.33), channel_id=1, source_target_pairs={{0,4},{4,8},{8,12},{12,16},{16,20},{20,24},{24,28},{1,5},{5,9},{9,... | collective-permute-start | bytes 1572872 | tf_op jit(solution)/shard_map/ppermute | solution.py:556
  18.0 0.0 copy-start.1
  18.0 1.4 %collective-permute-start.2 = (bf16[32,8192]{1,0:T(8,128)(2,1)S(1)}, bf16[32,8192]{1,0:T(8,128)(2,1)}, u32[]{:S(2)}, u32[]{:S(2)}) collective-permute-start(bf16[32,8192]{1,0:T(8,128)(2,1)S(1)} %get-tuple-element.28), channel_id=1, source_target_pairs={{4,0},{8,4},{12,8},{16,12},{20,16},{24,20},{28,24},{5,1},{9,5},{13... | collective-permute-start | bytes 1572872 | tf_op jit(solution)/shard_map/ppermute | solution.py:557
  19.5 0.0 copy-start.2
  19.5 1.2 %copy-done.2 = bf16[127,4096]{1,0:T(8,128)(2,1)S(1)} copy-done((bf16[127,4096]{1,0:T(8,128)(2,1)S(1)}, bf16[127,4096]{1,0:T(8,128)(2,1)}, u32[]{:S(2)}) %copy-start.2) | copy-done | bytes 1040408
  20.7 0.0 copy-start.5
  20.7 0.9 %copy-done.5 = bf16[24,4096]{1,0:T(8,128)(2,1)S(1)} copy-done((bf16[24,4096]{1,0:T(8,128)(2,1)S(1)}, bf16[24,4096]{1,0:T(8,128)(2,1)}, u32[]{:S(2)}) %copy-start.5) | copy-done | bytes 196632
  21.6 2.1 %relay.1 = (bf16[64,64,128]{2,1,0:T(8,128)(2,1)S(1)}, bf16[24,64,64]{2,1,0:T(8,128)(2,1)S(1)}) custom-call(bf16[127,4096]{1,0:T(8,128)(2,1)S(1)} %copy-done.2, bf16[24,4096]{1,0:T(8,128)(2,1)S(1)} %copy-done.5), custom_call_target="tpu_custom_call" | custom-call | flops 1000 | bytes 100000 | tf_op jit(solution)/shard_map/relay/pallas_call | solution.py:232
  23.8 0.0 copy-start.11
  23.8 0.7 copy-done.11
  24.5 0.0 copy-done.15
  24.5 0.1 copy.16.far_src_ref
  24.6 0.0 copy-done.16
  24.6 0.1 copy.17.far_cls_ref
  24.7 0.0 copy-done.7
  24.7 0.0 copy-done.8
  24.7 2.8 %class_counts.1.a_ref = bf16[24,128,256]{2,1,0:T(8,128)(2,1)S(1)} custom-call(s32[1]{0:T(128)} %bitcast.place_ref, s32[127,24]{1,0:T(8,128)S(1)} %copy.16.far_src_ref, s32[127,24]{1,0:T(8,128)S(1)} %copy.17.far_cls_ref, s32[12,24]{1,0:T(8,128)S(1)} %copy-done.7, s32[12,24]{1,0:T(8,128)S(1)} %copy-done.8), custom_call_target="tpu_custom_call" | custom-call | flops 1000 | bytes 100000 | tf_op jit(solution)/shard_map/class_counts/pallas_call | solution.py:324
  27.5 0.8 copy.20.near_ref
  28.3 0.1 all-gather.2.cloned.1.call-done
  28.4 0.0 copy-done.1
  28.4 0.0 copy-start.3
  28.4 1.2 %copy-done.3 = bf16[64,64,128]{2,1,0:T(8,128)(2,1)S(1)} copy-done((bf16[64,64,128]{2,1,0:T(8,128)(2,1)S(1)}, bf16[64,64,128]{2,1,0:T(8,128)(2,1)}, u32[]{:S(2)}) %copy-start.3) | copy-done | bytes 1048600
  29.7 0.0 copy-start.10
  29.7 0.0 copy-start.14
  29.7 2.0 %upward.1 = (bf16[16,64,128]{2,1,0:T(8,128)(2,1)S(1)}, bf16[17,32,128]{2,1,0:T(8,128)(2,1)S(1)}, bf16[17,32,128]{2,1,0:T(8,128)(2,1)S(1)}, bf16[16,128]{1,0:T(8,128)(2,1)S(1)}) custom-call(bf16[16,8192]{1,0:T(8,128)(2,1)S(1)} %copy-done.1, bf16[32,128,128]{2,1,0:T(8,128)(2,1)S(1)} %bitcast.4, bf16[64,64,128]{2,1,0:T(8,128)(2,1)S(1)} %get-tuple-element.21.links_ref), custom_call_target="tpu_custom_call" | custom-call | flops 300000000 | bytes 3000000 | tf_op jit(solution)/shard_map/upward/pallas_call | solution.py:389
  31.7 4.5 %collective-permute-start = (bf16[17,32,128]{2,1,0:T(8,128)(2,1)S(1)}, bf16[17,32,128]{2,1,0:T(8,128)(2,1)S(1)}, u32[]{:S(2)}, u32[]{:S(2)}) collective-permute-start(bf16[17,32,128]{2,1,0:T(8,128)(2,1)S(1)} %get-tuple-element.22), channel_id=1, source_target_pairs={{0,4},{4,8},{8,12},{12,16},{16,20},{20,24},{24,28},{1,5},{5,9},{9,... | collective-permute-start | bytes 417800 | tf_op jit(solution)/shard_map/ppermute | solution.py:562
  36.2 1.5 %collective-permute-start.1 = (bf16[17,32,128]{2,1,0:T(8,128)(2,1)S(1)}, bf16[17,32,128]{2,1,0:T(8,128)(2,1)S(1)}, u32[]{:S(2)}, u32[]{:S(2)}) collective-permute-start(bf16[17,32,128]{2,1,0:T(8,128)(2,1)S(1)} %get-tuple-element.26), channel_id=1, source_target_pairs={{4,0},{8,4},{12,8},{16,12},{20,16},{24,20},{28,24},{5,1},{9,5},{13... | collective-permute-start | bytes 417800 | tf_op jit(solution)/shard_map/ppermute | solution.py:563
  37.7 0.0 copy-done.10
  37.7 0.0 copy-done.14
  37.7 10.3 %near_own.1.rest_0_ = f32[16,8192]{1,0:T(8,128)S(1)} custom-call(s32[64,27]{1,0:T(8,128)S(1)} %copy.20.near_ref, bf16[32,8192]{1,0:T(8,128)(2,1)S(1)} %copy-done.10, bf16[16,8192]{1,0:T(8,128)(2,1)S(1)} %copy-done.14), custom_call_target="tpu_custom_call" | custom-call | flops 7000000000 | bytes 2000000 | tf_op jit(solution)/shard_map/near_own/pallas_call | solution.py:187
  48.0 0.0 collective-permute-done.low_ref
  48.0 0.0 collective-permute-done.1.high_ref
  48.0 3.8 %collective-permute-start.3 = (bf16[2,16,128]{2,1,0:T(8,128)(2,1)S(1)}, bf16[2,16,128]{2,1,0:T(8,128)(2,1)S(1)}, u32[]{:S(2)}, u32[]{:S(2)}) collective-permute-start(bf16[2,16,128]{2,1,0:T(8,128)(2,1)S(1)} %maximum_select_fusion.rest_0_), channel_id=1, source_target_pairs={{0,8},{4,12},{8,0},{12,4},{16,24},{20,28},{24,16},{28,20},{1,9},{5... | collective-permute-start | bytes 24584 | tf_op jit(solution)/shard_map/ppermute | solution.py:576
  51.8 0.0 collective-permute-done.4.src_ref
  51.8 10.3 %near_low.1.rest_0_ = f32[16,8192]{1,0:T(8,128)S(1)} custom-call(s32[64,27]{1,0:T(8,128)S(1)} %copy.20.near_ref, bf16[32,8192]{1,0:T(8,128)(2,1)} %collective-permute-done.4.src_ref, bf16[16,8192]{1,0:T(8,128)(2,1)S(1)} %copy-done.14, f32[16,8192]{1,0:T(8,128)S(1)} %near_own.1.rest_0_), custom_call_target="tpu_custom_call" | custom-call | flops 7000000000 | bytes 2000000 | tf_op jit(solution)/shard_map/near_low/pallas_call | solution.py:187
  62.1 0.0 collective-permute-done.3.rest_1_
  62.1 0.0 copy-start.4
  62.1 0.0 copy-start.12
  62.1 2.7 %collective-permute-start.5 = (bf16[4,16,128]{2,1,0:T(8,128)(2,1)S(1)}, bf16[4,16,128]{2,1,0:T(8,128)(2,1)S(1)}, u32[]{:S(2)}, u32[]{:S(2)}) collective-permute-start(bf16[4,16,128]{2,1,0:T(8,128)(2,1)S(1)} %pad_maximum_fusion), channel_id=1, source_target_pairs={{0,16},{4,20},{8,24},{12,28},{16,0},{20,4},{24,8},{28,12},{1,17},{... | collective-permute-start | bytes 49160 | tf_op jit(solution)/shard_map/ppermute | solution.py:576
  64.8 0.0 collective-permute-done.2.src_ref
  64.8 10.3 %near_high.1.near_ref = f32[16,8192]{1,0:T(8,128)S(1)} custom-call(s32[64,27]{1,0:T(8,128)S(1)} %copy.20.near_ref, bf16[32,8192]{1,0:T(8,128)(2,1)} %collective-permute-done.2.src_ref, bf16[16,8192]{1,0:T(8,128)(2,1)S(1)} %copy-done.14, f32[16,8192]{1,0:T(8,128)S(1)} %near_low.1.rest_0_), custom_call_target="tpu_custom_call" | custom-call | flops 7000000000 | bytes 2000000 | tf_op jit(solution)/shard_map/near_high/pallas_call | solution.py:187
  75.1 0.0 collective-permute-done.5.rest_2_
  75.1 0.0 copy-done.4
  75.1 0.0 copy-done.12
  75.1 10.2 %downward.1 = bf16[16,8192]{1,0:T(8,128)(2,1)} custom-call(s32[1]{0:T(128)} %bitcast.place_ref, bf16[17,32,128]{2,1,0:T(8,128)(2,1)S(1)} %collective-permute-done.low_ref, bf16[16,64,128]{2,1,0:T(8,128)(2,1)S(1)} %get-tuple-element.25.own_ref, bf16[17,32,128]{2,1,0:T(8,128)(2,1)S(1)} %collective-permute-done.1.high_ref, ...), custom_call_target="tpu_custom_call" | custom-call | flops 4000000000 | bytes 6000000 | tf_op jit(solution)/shard_map/downward/pallas_call | solution.py:518
  (3 shorter events, 0.0 us)
Async XLA Ops:
  6.5 18.0 %copy-start.15 = (s32[127,24]{0,1:T(8,128)S(1)}, s32[127,24]{0,1:T(8,128)}, u32[]{:S(2)}) copy-start(s32[127,24]{0,1:T(8,128)} %param.16) | copy-start | bytes 36580
  6.5 18.1 %copy-start.16 = (s32[127,24]{0,1:T(8,128)S(1)}, s32[127,24]{0,1:T(8,128)}, u32[]{:S(2)}) copy-start(s32[127,24]{0,1:T(8,128)} %param.17) | copy-start | bytes 36580
  6.5 18.2 %copy-start.7 = (s32[12,24]{1,0:T(8,128)S(1)}, s32[12,24]{1,0:T(8,128)}, u32[]{:S(2)}) copy-start(s32[12,24]{1,0:T(8,128)} %top_src_ref.1) | copy-start | bytes 3460
  6.5 18.2 %copy-start.8 = (s32[12,24]{1,0:T(8,128)S(1)}, s32[12,24]{1,0:T(8,128)}, u32[]{:S(2)}) copy-start(s32[12,24]{1,0:T(8,128)} %top_cls_ref.1) | copy-start | bytes 3460
  6.5 21.9 %all-gather.2.cloned.1.call-start = ((), (), s32[]{:S(2)}) async-start(), calls=%async_computation | async-start | bytes 1310720 | tf_op jit(solution)/shard_map/all_gather | solution.py:546
  7.4 1.0 %copy-start = (bf16[16,8192]{1,0:T(8,128)(2,1)S(1)}, bf16[16,8192]{1,0:T(8,128)(2,1)}, u32[]{:S(2)}) copy-start(bf16[16,8192]{1,0:T(8,128)(2,1)} %values_ref.3) | copy-start | bytes 786436
  8.3 0.9 copy-start.6
  10.9 0.8 copy-start.9
  11.7 0.7 copy-start.13
  12.4 39.4 %collective-permute-start.4 = (bf16[32,8192]{1,0:T(8,128)(2,1)}, bf16[32,8192]{1,0:T(8,128)(2,1)}, u32[]{:S(2)}, u32[]{:S(2)}) collective-permute-start(bf16[32,8192]{1,0:T(8,128)(2,1)} %get-tuple-element.33), channel_id=1, source_target_pairs={{0,4},{4,8},{8,12},{12,16},{16,20},{20,24},{24,28},{1,5},{5,9},{9,... | collective-permute-start | bytes 1572872 | tf_op jit(solution)/shard_map/ppermute | solution.py:556
  18.0 10.4 %copy-start.1 = (bf16[16,8192]{1,0:T(8,128)(2,1)S(1)}, bf16[16,8192]{1,0:T(8,128)(2,1)}, u32[]{:S(2)}) copy-start(bf16[16,8192]{1,0:T(8,128)(2,1)} %values_ref.3) | copy-start | bytes 786436
  18.0 46.7 %collective-permute-start.2 = (bf16[32,8192]{1,0:T(8,128)(2,1)S(1)}, bf16[32,8192]{1,0:T(8,128)(2,1)}, u32[]{:S(2)}, u32[]{:S(2)}) collective-permute-start(bf16[32,8192]{1,0:T(8,128)(2,1)S(1)} %get-tuple-element.28), channel_id=1, source_target_pairs={{4,0},{8,4},{12,8},{16,12},{20,16},{24,20},{28,24},{5,1},{9,5},{13... | collective-permute-start | bytes 1572872 | tf_op jit(solution)/shard_map/ppermute | solution.py:557
  19.5 1.2 %copy-start.2 = (bf16[127,4096]{1,0:T(8,128)(2,1)S(1)}, bf16[127,4096]{1,0:T(8,128)(2,1)}, u32[]{:S(2)}) copy-start(bf16[127,4096]{1,0:T(8,128)(2,1)} %transfer_ref.1) | copy-start | bytes 3121156
  20.7 0.9 %copy-start.5 = (bf16[24,4096]{1,0:T(8,128)(2,1)S(1)}, bf16[24,4096]{1,0:T(8,128)(2,1)}, u32[]{:S(2)}) copy-start(bf16[24,4096]{1,0:T(8,128)(2,1)} %coupling_ref.1) | copy-start | bytes 589828
  23.8 0.7 copy-start.11
  28.4 1.2 %copy-start.3 = (bf16[64,64,128]{2,1,0:T(8,128)(2,1)S(1)}, bf16[64,64,128]{2,1,0:T(8,128)(2,1)}, u32[]{:S(2)}) copy-start(bf16[64,64,128]{2,1,0:T(8,128)(2,1)} %all-gather.2.cloned.1.call-done) | copy-start | bytes 3145732
  29.7 8.0 %copy-start.10 = (bf16[32,8192]{1,0:T(8,128)(2,1)S(1)}, bf16[32,8192]{1,0:T(8,128)(2,1)}, u32[]{:S(2)}) copy-start(bf16[32,8192]{1,0:T(8,128)(2,1)} %copy-done.9) | copy-start | bytes 1572868
  29.7 8.0 %copy-start.14 = (bf16[16,8192]{1,0:T(8,128)(2,1)S(1)}, bf16[16,8192]{1,0:T(8,128)(2,1)}, u32[]{:S(2)}) copy-start(bf16[16,8192]{1,0:T(8,128)(2,1)} %copy-done.13) | copy-start | bytes 786436
  31.7 16.3 %collective-permute-start = (bf16[17,32,128]{2,1,0:T(8,128)(2,1)S(1)}, bf16[17,32,128]{2,1,0:T(8,128)(2,1)S(1)}, u32[]{:S(2)}, u32[]{:S(2)}) collective-permute-start(bf16[17,32,128]{2,1,0:T(8,128)(2,1)S(1)} %get-tuple-element.22), channel_id=1, source_target_pairs={{0,4},{4,8},{8,12},{12,16},{16,20},{20,24},{24,28},{1,5},{5,9},{9,... | collective-permute-start | bytes 417800 | tf_op jit(solution)/shard_map/ppermute | solution.py:562
  36.2 11.8 %collective-permute-start.1 = (bf16[17,32,128]{2,1,0:T(8,128)(2,1)S(1)}, bf16[17,32,128]{2,1,0:T(8,128)(2,1)S(1)}, u32[]{:S(2)}, u32[]{:S(2)}) collective-permute-start(bf16[17,32,128]{2,1,0:T(8,128)(2,1)S(1)} %get-tuple-element.26), channel_id=1, source_target_pairs={{4,0},{8,4},{12,8},{16,12},{20,16},{24,20},{28,24},{5,1},{9,5},{13... | collective-permute-start | bytes 417800 | tf_op jit(solution)/shard_map/ppermute | solution.py:563
  48.0 14.1 %collective-permute-start.3 = (bf16[2,16,128]{2,1,0:T(8,128)(2,1)S(1)}, bf16[2,16,128]{2,1,0:T(8,128)(2,1)S(1)}, u32[]{:S(2)}, u32[]{:S(2)}) collective-permute-start(bf16[2,16,128]{2,1,0:T(8,128)(2,1)S(1)} %maximum_select_fusion.rest_0_), channel_id=1, source_target_pairs={{0,8},{4,12},{8,0},{12,4},{16,24},{20,28},{24,16},{28,20},{1,9},{5... | collective-permute-start | bytes 24584 | tf_op jit(solution)/shard_map/ppermute | solution.py:576
  62.1 13.0 %copy-start.4 = (bf16[64,64,128]{2,1,0:T(8,128)(2,1)S(1)}, bf16[64,64,128]{2,1,0:T(8,128)(2,1)}, u32[]{:S(2)}) copy-start(bf16[64,64,128]{2,1,0:T(8,128)(2,1)} %all-gather.2.cloned.1.call-done) | copy-start | bytes 3145732
  62.1 13.0 %copy-start.12 = (bf16[24,64,64]{2,1,0:T(8,128)(2,1)S(1)}, bf16[24,64,64]{2,1,0:T(8,128)(2,1)}, u32[]{:S(2)}) copy-start(bf16[24,64,64]{2,1,0:T(8,128)(2,1)} %copy-done.11) | copy-start | bytes 589828
  62.1 12.9 %collective-permute-start.5 = (bf16[4,16,128]{2,1,0:T(8,128)(2,1)S(1)}, bf16[4,16,128]{2,1,0:T(8,128)(2,1)S(1)}, u32[]{:S(2)}, u32[]{:S(2)}) collective-permute-start(bf16[4,16,128]{2,1,0:T(8,128)(2,1)S(1)} %pad_maximum_fusion), channel_id=1, source_target_pairs={{0,16},{4,20},{8,24},{12,28},{16,0},{20,4},{24,8},{28,12},{1,17},{... | collective-permute-start | bytes 49160 | tf_op jit(solution)/shard_map/ppermute | solution.py:576
Sparse Core Ops, SparseCore 0:
  8.9 19.4 all-gather.1

commit v8 on v7

--- a/solution.py
+++ b/solution.py
@@ -165,7 +165,7 @@
                     )
                 )
         e = dot(jnp.concatenate(sources, axis=0), w_ref[q])
-        total = dot(jnp.concatenate(vectors, axis=1), jnp.exp2(e).astype(jnp.bfloat16))
+        total = dot(jnp.concatenate(vectors, axis=1), jnp.exp2(e.astype(jnp.bfloat16)))
         for i in range(QUAD):
             tile = AMPLITUDE * total[N * i : N * (i + 1), M * i : M * (i + 1)]
             if before_ref is not None:

time: 92.6 us -> 95.2 us (1.028)
  Pallas kernels: 49.6 us -> 52.2 us
    pallas_call x3, Pallas kernels: 30.8 us -> 33.4 us  [near_field(): pl.pallas_call(functools.partial(near_kernel, layer), name=('near_low', '...]
  transfers between devices with their start and end apart: 7 -> 7, of which waited for: 1 -> 1; matrix products, arithmetic and copies ran while one was open for 1% -> 1% of each run, Pallas kernels for 43% -> 44%
where the time goes in v8:
time: 95.2 us; the launch traced here: 94.8 us
  Pallas kernels  52.2 us (55%)
  starting transfers between devices  19.5 us (20%)
  between operations  13.6 us (14%)
  local copies, waits for them, and re-layouts  8.52 us (9%)
    pallas_call x3, Pallas kernels, near_field(): pl.pallas_call(functools.partial(near_kernel, layer), name=('near_low', '...  33.4 us
    pallas_call x1, Pallas kernels, downward(): pl.pallas_call(down_kernel, name='downward', out_shape=jax.ShapeDtypeStru...  10.2 us
    unnamed x37, local copies, waits for them, and re-layouts  8.52 us
    ppermute x2, starting transfers between devices, per_device(): lax.ppermute(known, 'leaf', [(i, i ^ step) for i in range(subtrees)])  6.46 us
    ppermute x1, starting transfers between devices, per_device(): from_low = lax.ppermute(for_high, 'leaf', forward)  5.68 us
    ppermute x1, starting transfers between devices, per_device(): low = lax.ppermute(last, 'leaf', forward)  4.48 us
    pallas_call x1, Pallas kernels, class_counts(): pl.pallas_call(counts_kernel, name='class_counts', out_shape=jax.ShapeDty...  2.77 us
    pallas_call x1, Pallas kernels, relay(): pl.pallas_call(relay_kernel, name='relay', out_shape=[jax.ShapeDtypeStruc...  2.13 us
  transfers between devices with their start and end apart: 7, of which 1 were waited for; matrix products, arithmetic and copies ran while one was open for 1% of the time, Pallas kernels for 44%

profile of v8, /device:TPU:0, one launch (start us, length us, event | category | flops | bytes accessed | tf_op | source)
XLA Modules:
  0.0 94.8 jit_solution(831749193821793164)
XLA Ops:
  6.5 0.0 copy-start.15
  6.5 0.0 copy-start.16
  6.5 0.0 copy-start.7
  6.5 0.0 copy-start.8
  6.5 0.0 all-gather.2.cloned.1.call-start
  6.6 0.7 all-gather.2.cloned.1.call-update
  7.3 0.1 pad_maximum_fusion.1.centre_ref
  7.4 0.0 copy-start
  7.4 0.9 %copy-done = bf16[16,8192]{1,0:T(8,128)(2,1)S(1)} copy-done((bf16[16,8192]{1,0:T(8,128)(2,1)S(1)}, bf16[16,8192]{1,0:T(8,128)(2,1)}, u32[]{:S(2)}) %copy-start) | copy-done | bytes 262168
  8.3 0.0 copy-start.6
  8.3 0.9 copy-done.6
  9.2 1.6 %pack.1 = (bf16[32,8192]{1,0:T(8,128)(2,1)S(1)}, bf16[32,8192]{1,0:T(8,128)(2,1)}, bf16[32,8192]{1,0:T(8,128)(2,1)S(1)}, bf16[16,8192]{1,0:T(8,128)(2,1)S(1)}) custom-call(f32[3]{0:T(128)S(1)} %pad_maximum_fusion.1.centre_ref, bf16[16,8192]{1,0:T(8,128)(2,1)S(1)} %copy-done, f32[3,8192]{1,0:T(4,128)S(1)} %copy-done.6), custom_call_target="tpu_custom_call" | custom-call | flops 1000 | bytes 100000 | tf_op jit(solution)/shard_map/pack/pallas_call | solution.py:86
  10.9 0.0 copy-start.9
  10.9 0.8 copy-done.9
  11.7 0.0 copy-start.13
  11.7 0.7 copy-done.13
  12.4 5.7 %collective-permute-start.4 = (bf16[32,8192]{1,0:T(8,128)(2,1)}, bf16[32,8192]{1,0:T(8,128)(2,1)}, u32[]{:S(2)}, u32[]{:S(2)}) collective-permute-start(bf16[32,8192]{1,0:T(8,128)(2,1)} %get-tuple-element.33), channel_id=1, source_target_pairs={{0,4},{4,8},{8,12},{12,16},{16,20},{20,24},{24,28},{1,5},{5,9},{9,... | collective-permute-start | bytes 1572872 | tf_op jit(solution)/shard_map/ppermute | solution.py:556
  18.0 0.0 copy-start.1
  18.0 1.4 %collective-permute-start.2 = (bf16[32,8192]{1,0:T(8,128)(2,1)S(1)}, bf16[32,8192]{1,0:T(8,128)(2,1)}, u32[]{:S(2)}, u32[]{:S(2)}) collective-permute-start(bf16[32,8192]{1,0:T(8,128)(2,1)S(1)} %get-tuple-element.28), channel_id=1, source_target_pairs={{4,0},{8,4},{12,8},{16,12},{20,16},{24,20},{28,24},{5,1},{9,5},{13... | collective-permute-start | bytes 1572872 | tf_op jit(solution)/shard_map/ppermute | solution.py:557
  19.5 0.0 copy-start.2
  19.5 1.2 %copy-done.2 = bf16[127,4096]{1,0:T(8,128)(2,1)S(1)} copy-done((bf16[127,4096]{1,0:T(8,128)(2,1)S(1)}, bf16[127,4096]{1,0:T(8,128)(2,1)}, u32[]{:S(2)}) %copy-start.2) | copy-done | bytes 1040408
  20.7 0.0 copy-start.5
  20.7 0.9 copy-done.5
  21.6 2.1 %relay.1 = (bf16[64,64,128]{2,1,0:T(8,128)(2,1)S(1)}, bf16[24,64,64]{2,1,0:T(8,128)(2,1)S(1)}) custom-call(bf16[127,4096]{1,0:T(8,128)(2,1)S(1)} %copy-done.2, bf16[24,4096]{1,0:T(8,128)(2,1)S(1)} %copy-done.5), custom_call_target="tpu_custom_call" | custom-call | flops 1000 | bytes 100000 | tf_op jit(solution)/shard_map/relay/pallas_call | solution.py:232
  23.8 0.0 copy-start.11
  23.8 0.7 copy-done.11
  24.5 0.0 copy-done.15
  24.5 0.1 copy.16.far_src_ref
  24.6 0.0 copy-done.16
  24.6 0.1 copy.17.far_cls_ref
  24.7 0.0 copy-done.7
  24.7 0.0 copy-done.8
  24.7 2.8 %class_counts.1.a_ref = bf16[24,128,256]{2,1,0:T(8,128)(2,1)S(1)} custom-call(s32[1]{0:T(128)} %bitcast.place_ref, s32[127,24]{1,0:T(8,128)S(1)} %copy.16.far_src_ref, s32[127,24]{1,0:T(8,128)S(1)} %copy.17.far_cls_ref, s32[12,24]{1,0:T(8,128)S(1)} %copy-done.7, s32[12,24]{1,0:T(8,128)S(1)} %copy-done.8), custom_call_target="tpu_custom_call" | custom-call | flops 1000 | bytes 100000 | tf_op jit(solution)/shard_map/class_counts/pallas_call | solution.py:324
  27.5 0.8 copy.20.near_ref
  28.3 0.1 all-gather.2.cloned.1.call-done
  28.4 0.0 copy-done.1
  28.4 0.0 copy-start.3
  28.4 1.2 %copy-done.3 = bf16[64,64,128]{2,1,0:T(8,128)(2,1)S(1)} copy-done((bf16[64,64,128]{2,1,0:T(8,128)(2,1)S(1)}, bf16[64,64,128]{2,1,0:T(8,128)(2,1)}, u32[]{:S(2)}) %copy-start.3) | copy-done | bytes 1048600
  29.7 0.0 copy-start.10
  29.7 0.0 copy-start.14
  29.7 2.0 %upward.1 = (bf16[16,64,128]{2,1,0:T(8,128)(2,1)S(1)}, bf16[17,32,128]{2,1,0:T(8,128)(2,1)S(1)}, bf16[17,32,128]{2,1,0:T(8,128)(2,1)S(1)}, bf16[16,128]{1,0:T(8,128)(2,1)S(1)}) custom-call(bf16[16,8192]{1,0:T(8,128)(2,1)S(1)} %copy-done.1, bf16[32,128,128]{2,1,0:T(8,128)(2,1)S(1)} %bitcast.4, bf16[64,64,128]{2,1,0:T(8,128)(2,1)S(1)} %get-tuple-element.21.links_ref), custom_call_target="tpu_custom_call" | custom-call | flops 300000000 | bytes 3000000 | tf_op jit(solution)/shard_map/upward/pallas_call | solution.py:389
  31.7 4.5 %collective-permute-start = (bf16[17,32,128]{2,1,0:T(8,128)(2,1)S(1)}, bf16[17,32,128]{2,1,0:T(8,128)(2,1)S(1)}, u32[]{:S(2)}, u32[]{:S(2)}) collective-permute-start(bf16[17,32,128]{2,1,0:T(8,128)(2,1)S(1)} %get-tuple-element.22), channel_id=1, source_target_pairs={{0,4},{4,8},{8,12},{12,16},{16,20},{20,24},{24,28},{1,5},{5,9},{9,... | collective-permute-start | bytes 417800 | tf_op jit(solution)/shard_map/ppermute | solution.py:562
  36.2 1.5 %collective-permute-start.1 = (bf16[17,32,128]{2,1,0:T(8,128)(2,1)S(1)}, bf16[17,32,128]{2,1,0:T(8,128)(2,1)S(1)}, u32[]{:S(2)}, u32[]{:S(2)}) collective-permute-start(bf16[17,32,128]{2,1,0:T(8,128)(2,1)S(1)} %get-tuple-element.26), channel_id=1, source_target_pairs={{4,0},{8,4},{12,8},{16,12},{20,16},{24,20},{28,24},{5,1},{9,5},{13... | collective-permute-start | bytes 417800 | tf_op jit(solution)/shard_map/ppermute | solution.py:563
  37.7 0.0 copy-done.10
  37.7 0.0 copy-done.14
  37.7 11.0 %near_own.1.rest_0_ = f32[16,8192]{1,0:T(8,128)S(1)} custom-call(s32[64,27]{1,0:T(8,128)S(1)} %copy.20.near_ref, bf16[32,8192]{1,0:T(8,128)(2,1)S(1)} %copy-done.10, bf16[16,8192]{1,0:T(8,128)(2,1)S(1)} %copy-done.14), custom_call_target="tpu_custom_call" | custom-call | flops 7000000000 | bytes 2000000 | tf_op jit(solution)/shard_map/near_own/pallas_call | solution.py:187
  48.7 0.0 collective-permute-done.low_ref
  48.8 0.0 collective-permute-done.1.high_ref
  48.8 3.8 %collective-permute-start.3 = (bf16[2,16,128]{2,1,0:T(8,128)(2,1)S(1)}, bf16[2,16,128]{2,1,0:T(8,128)(2,1)S(1)}, u32[]{:S(2)}, u32[]{:S(2)}) collective-permute-start(bf16[2,16,128]{2,1,0:T(8,128)(2,1)S(1)} %maximum_select_fusion.rest_0_), channel_id=1, source_target_pairs={{0,8},{4,12},{8,0},{12,4},{16,24},{20,28},{24,16},{28,20},{1,9},{5... | collective-permute-start | bytes 24584 | tf_op jit(solution)/shard_map/ppermute | solution.py:576
  52.6 0.0 collective-permute-done.4.src_ref
  52.6 11.2 %near_low.1.rest_0_ = f32[16,8192]{1,0:T(8,128)S(1)} custom-call(s32[64,27]{1,0:T(8,128)S(1)} %copy.20.near_ref, bf16[32,8192]{1,0:T(8,128)(2,1)} %collective-permute-done.4.src_ref, bf16[16,8192]{1,0:T(8,128)(2,1)S(1)} %copy-done.14, f32[16,8192]{1,0:T(8,128)S(1)} %near_own.1.rest_0_), custom_call_target="tpu_custom_call" | custom-call | flops 7000000000 | bytes 2000000 | tf_op jit(solution)/shard_map/near_low/pallas_call | solution.py:187
  63.8 0.0 collective-permute-done.3.rest_1_
  63.8 0.0 copy-start.4
  63.8 0.0 copy-start.12
  63.8 2.7 %collective-permute-start.5 = (bf16[4,16,128]{2,1,0:T(8,128)(2,1)S(1)}, bf16[4,16,128]{2,1,0:T(8,128)(2,1)S(1)}, u32[]{:S(2)}, u32[]{:S(2)}) collective-permute-start(bf16[4,16,128]{2,1,0:T(8,128)(2,1)S(1)} %pad_maximum_fusion), channel_id=1, source_target_pairs={{0,16},{4,20},{8,24},{12,28},{16,0},{20,4},{24,8},{28,12},{1,17},{... | collective-permute-start | bytes 49160 | tf_op jit(solution)/shard_map/ppermute | solution.py:576
  66.5 0.0 collective-permute-done.2.src_ref
  66.5 11.2 %near_high.1.near_ref = f32[16,8192]{1,0:T(8,128)S(1)} custom-call(s32[64,27]{1,0:T(8,128)S(1)} %copy.20.near_ref, bf16[32,8192]{1,0:T(8,128)(2,1)} %collective-permute-done.2.src_ref, bf16[16,8192]{1,0:T(8,128)(2,1)S(1)} %copy-done.14, f32[16,8192]{1,0:T(8,128)S(1)} %near_low.1.rest_0_), custom_call_target="tpu_custom_call" | custom-call | flops 7000000000 | bytes 2000000 | tf_op jit(solution)/shard_map/near_high/pallas_call | solution.py:187
  77.7 0.0 collective-permute-done.5.rest_2_
  77.7 0.0 copy-done.4
  77.7 0.0 copy-done.12
  77.7 10.2 %downward.1 = bf16[16,8192]{1,0:T(8,128)(2,1)} custom-call(s32[1]{0:T(128)} %bitcast.place_ref, bf16[17,32,128]{2,1,0:T(8,128)(2,1)S(1)} %collective-permute-done.low_ref, bf16[16,64,128]{2,1,0:T(8,128)(2,1)S(1)} %get-tuple-element.25.own_ref, bf16[17,32,128]{2,1,0:T(8,128)(2,1)S(1)} %collective-permute-done.1.high_ref, ...), custom_call_target="tpu_custom_call" | custom-call | flops 4000000000 | bytes 6000000 | tf_op jit(solution)/shard_map/downward/pallas_call | solution.py:518
  (3 shorter events, 0.0 us)
Async XLA Ops:
  6.5 18.0 %copy-start.15 = (s32[127,24]{0,1:T(8,128)S(1)}, s32[127,24]{0,1:T(8,128)}, u32[]{:S(2)}) copy-start(s32[127,24]{0,1:T(8,128)} %param.16) | copy-start | bytes 36580
  6.5 18.1 %copy-start.16 = (s32[127,24]{0,1:T(8,128)S(1)}, s32[127,24]{0,1:T(8,128)}, u32[]{:S(2)}) copy-start(s32[127,24]{0,1:T(8,128)} %param.17) | copy-start | bytes 36580
  6.5 18.2 %copy-start.7 = (s32[12,24]{1,0:T(8,128)S(1)}, s32[12,24]{1,0:T(8,128)}, u32[]{:S(2)}) copy-start(s32[12,24]{1,0:T(8,128)} %top_src_ref.1) | copy-start | bytes 3460
  6.5 18.2 %copy-start.8 = (s32[12,24]{1,0:T(8,128)S(1)}, s32[12,24]{1,0:T(8,128)}, u32[]{:S(2)}) copy-start(s32[12,24]{1,0:T(8,128)} %top_cls_ref.1) | copy-start | bytes 3460
  6.5 21.9 %all-gather.2.cloned.1.call-start = ((), (), s32[]{:S(2)}) async-start(), calls=%async_computation | async-start | bytes 1310720 | tf_op jit(solution)/shard_map/all_gather | solution.py:546
  7.4 1.0 %copy-start = (bf16[16,8192]{1,0:T(8,128)(2,1)S(1)}, bf16[16,8192]{1,0:T(8,128)(2,1)}, u32[]{:S(2)}) copy-start(bf16[16,8192]{1,0:T(8,128)(2,1)} %values_ref.3) | copy-start | bytes 786436
  8.3 0.9 copy-start.6
  10.9 0.8 copy-start.9
  11.7 0.7 copy-start.13
  12.4 40.2 %collective-permute-start.4 = (bf16[32,8192]{1,0:T(8,128)(2,1)}, bf16[32,8192]{1,0:T(8,128)(2,1)}, u32[]{:S(2)}, u32[]{:S(2)}) collective-permute-start(bf16[32,8192]{1,0:T(8,128)(2,1)} %get-tuple-element.33), channel_id=1, source_target_pairs={{0,4},{4,8},{8,12},{12,16},{16,20},{20,24},{24,28},{1,5},{5,9},{9,... | collective-permute-start | bytes 1572872 | tf_op jit(solution)/shard_map/ppermute | solution.py:556
  18.0 10.4 %copy-start.1 = (bf16[16,8192]{1,0:T(8,128)(2,1)S(1)}, bf16[16,8192]{1,0:T(8,128)(2,1)}, u32[]{:S(2)}) copy-start(bf16[16,8192]{1,0:T(8,128)(2,1)} %values_ref.3) | copy-start | bytes 786436
  18.0 48.4 %collective-permute-start.2 = (bf16[32,8192]{1,0:T(8,128)(2,1)S(1)}, bf16[32,8192]{1,0:T(8,128)(2,1)}, u32[]{:S(2)}, u32[]{:S(2)}) collective-permute-start(bf16[32,8192]{1,0:T(8,128)(2,1)S(1)} %get-tuple-element.28), channel_id=1, source_target_pairs={{4,0},{8,4},{12,8},{16,12},{20,16},{24,20},{28,24},{5,1},{9,5},{13... | collective-permute-start | bytes 1572872 | tf_op jit(solution)/shard_map/ppermute | solution.py:557
  19.5 1.2 %copy-start.2 = (bf16[127,4096]{1,0:T(8,128)(2,1)S(1)}, bf16[127,4096]{1,0:T(8,128)(2,1)}, u32[]{:S(2)}) copy-start(bf16[127,4096]{1,0:T(8,128)(2,1)} %transfer_ref.1) | copy-start | bytes 3121156
  20.7 0.9 copy-start.5
  23.8 0.7 copy-start.11
  28.4 1.2 %copy-start.3 = (bf16[64,64,128]{2,1,0:T(8,128)(2,1)S(1)}, bf16[64,64,128]{2,1,0:T(8,128)(2,1)}, u32[]{:S(2)}) copy-start(bf16[64,64,128]{2,1,0:T(8,128)(2,1)} %all-gather.2.cloned.1.call-done) | copy-start | bytes 3145732
  29.7 8.0 %copy-start.10 = (bf16[32,8192]{1,0:T(8,128)(2,1)S(1)}, bf16[32,8192]{1,0:T(8,128)(2,1)}, u32[]{:S(2)}) copy-start(bf16[32,8192]{1,0:T(8,128)(2,1)} %copy-done.9) | copy-start | bytes 1572868
  29.7 8.0 %copy-start.14 = (bf16[16,8192]{1,0:T(8,128)(2,1)S(1)}, bf16[16,8192]{1,0:T(8,128)(2,1)}, u32[]{:S(2)}) copy-start(bf16[16,8192]{1,0:T(8,128)(2,1)} %copy-done.13) | copy-start | bytes 786436
  31.7 17.0 %collective-permute-start = (bf16[17,32,128]{2,1,0:T(8,128)(2,1)S(1)}, bf16[17,32,128]{2,1,0:T(8,128)(2,1)S(1)}, u32[]{:S(2)}, u32[]{:S(2)}) collective-permute-start(bf16[17,32,128]{2,1,0:T(8,128)(2,1)S(1)} %get-tuple-element.22), channel_id=1, source_target_pairs={{0,4},{4,8},{8,12},{12,16},{16,20},{20,24},{24,28},{1,5},{5,9},{9,... | collective-permute-start | bytes 417800 | tf_op jit(solution)/shard_map/ppermute | solution.py:562
  36.2 12.6 %collective-permute-start.1 = (bf16[17,32,128]{2,1,0:T(8,128)(2,1)S(1)}, bf16[17,32,128]{2,1,0:T(8,128)(2,1)S(1)}, u32[]{:S(2)}, u32[]{:S(2)}) collective-permute-start(bf16[17,32,128]{2,1,0:T(8,128)(2,1)S(1)} %get-tuple-element.26), channel_id=1, source_target_pairs={{4,0},{8,4},{12,8},{16,12},{20,16},{24,20},{28,24},{5,1},{9,5},{13... | collective-permute-start | bytes 417800 | tf_op jit(solution)/shard_map/ppermute | solution.py:563
  48.8 15.0 %collective-permute-start.3 = (bf16[2,16,128]{2,1,0:T(8,128)(2,1)S(1)}, bf16[2,16,128]{2,1,0:T(8,128)(2,1)S(1)}, u32[]{:S(2)}, u32[]{:S(2)}) collective-permute-start(bf16[2,16,128]{2,1,0:T(8,128)(2,1)S(1)} %maximum_select_fusion.rest_0_), channel_id=1, source_target_pairs={{0,8},{4,12},{8,0},{12,4},{16,24},{20,28},{24,16},{28,20},{1,9},{5... | collective-permute-start | bytes 24584 | tf_op jit(solution)/shard_map/ppermute | solution.py:576
  63.8 13.9 %copy-start.4 = (bf16[64,64,128]{2,1,0:T(8,128)(2,1)S(1)}, bf16[64,64,128]{2,1,0:T(8,128)(2,1)}, u32[]{:S(2)}) copy-start(bf16[64,64,128]{2,1,0:T(8,128)(2,1)} %all-gather.2.cloned.1.call-done) | copy-start | bytes 3145732
  63.8 13.9 %copy-start.12 = (bf16[24,64,64]{2,1,0:T(8,128)(2,1)S(1)}, bf16[24,64,64]{2,1,0:T(8,128)(2,1)}, u32[]{:S(2)}) copy-start(bf16[24,64,64]{2,1,0:T(8,128)(2,1)} %copy-done.11) | copy-start | bytes 589828
  63.8 13.9 %collective-permute-start.5 = (bf16[4,16,128]{2,1,0:T(8,128)(2,1)S(1)}, bf16[4,16,128]{2,1,0:T(8,128)(2,1)S(1)}, u32[]{:S(2)}, u32[]{:S(2)}) collective-permute-start(bf16[4,16,128]{2,1,0:T(8,128)(2,1)S(1)} %pad_maximum_fusion), channel_id=1, source_target_pairs={{0,16},{4,20},{8,24},{12,28},{16,0},{20,4},{24,8},{28,12},{1,17},{... | collective-permute-start | bytes 49160 | tf_op jit(solution)/shard_map/ppermute | solution.py:576
Sparse Core Ops, SparseCore 0:
  8.9 19.4 all-gather.1

commit v9 on v7

--- a/solution.py
+++ b/solution.py
@@ -469,23 +469,30 @@
 
     lax.fori_loop(0, classes, spread, 0)
 
-    counts = a_ref[...].reshape(classes * 2 * PAIRS, 2 * height)
-    wide = N * K // 2
-    for half in range(2):
-        grouped = dot(counts, call_ref[:, half * wide : (half + 1) * wide]).astype(jnp.bfloat16)
-        for c in range(classes):
-            for parity in range(2):
-                row = (2 * c + parity) * PAIRS
-                for i in range(N // 4):
-                    m = half * (N // 4) + i
-                    lhs_ref[
-                        m * PAIRS : (m + 1) * PAIRS, (2 * c + parity) * 2 * K : (2 * c + parity + 1) * 2 * K
-                    ] = grouped[row : row + PAIRS, i * 2 * K : (i + 1) * 2 * K]
-    field = dot(lhs_ref[...], bd_ref[...])
-    for m in range(N // 2):
-        rows = slice(m * PAIRS, (m + 1) * PAIRS)
-        fs_ref[2 * m * PAIRS : (2 * m + 1) * PAIRS, :] = field[rows, 0 : 2 * K]
-        fs_ref[(2 * m + 1) * PAIRS : (2 * m + 2) * PAIRS, :] = field[rows, 2 * K : 4 * K]
+    def group(c, carry):
+        grouped = dot(a_ref[c], call_ref[...]).astype(jnp.bfloat16)
+        for parity in range(2):
+            lanes = pl.ds(pl.multiple_of((2 * c + parity) * 2 * K, 2 * K), 2 * K)
+            for m in range(N // 2):
+                lhs_ref[m * PAIRS : (m + 1) * PAIRS, lanes] = grouped[
+                    parity * PAIRS : (parity + 1) * PAIRS, m * 2 * K : (m + 1) * 2 * K
+                ]
+        return carry
+
+    lax.fori_loop(0, classes, group, 0, unroll=2)
+
+    some = N // 4 * PAIRS
+
+    def couple(half, carry):
+        field = dot(lhs_ref[pl.ds(pl.multiple_of(half * some, some), some), :], bd_ref[...])
+        for i in range(N // 4):
+            at = pl.multiple_of(2 * half * some + 2 * i * PAIRS, PAIRS)
+            rows = slice(i * PAIRS, (i + 1) * PAIRS)
+            fs_ref[pl.ds(at, PAIRS), :] = field[rows, 0 : 2 * K]
+            fs_ref[pl.ds(at + PAIRS, PAIRS), :] = field[rows, 2 * K : 4 * K]
+        return carry
+
+    lax.fori_loop(0, 2, couple, 0)
 
     def field_of(pair_index):
         return fs_ref[pl.ds(pair_index, N, stride=PAIRS), :]

time: 92.6 us -> 92.5 us (level)
  no operation moved by 1% of the time
where the time goes in v9:
time: 92.5 us; the launch traced here: 92.1 us
  Pallas kernels  49.5 us (54%)
  starting transfers between devices  19.5 us (21%)
  between operations  13.6 us (15%)
  local copies, waits for them, and re-layouts  8.52 us (9%)
    pallas_call x3, Pallas kernels, near_field(): pl.pallas_call(functools.partial(near_kernel, layer), name=('near_low', '...  30.8 us
    pallas_call x1, Pallas kernels, downward(): pl.pallas_call(down_kernel, name='downward', out_shape=jax.ShapeDtypeStru...  10.1 us
    unnamed x37, local copies, waits for them, and re-layouts  8.52 us
    ppermute x2, starting transfers between devices, per_device(): lax.ppermute(known, 'leaf', [(i, i ^ step) for i in range(subtrees)])  6.44 us
    ppermute x1, starting transfers between devices, per_device(): from_low = lax.ppermute(for_high, 'leaf', forward)  5.68 us
    ppermute x1, starting transfers between devices, per_device(): low = lax.ppermute(last, 'leaf', forward)  4.48 us
    pallas_call x1, Pallas kernels, class_counts(): pl.pallas_call(counts_kernel, name='class_counts', out_shape=jax.ShapeDty...  2.77 us
    pallas_call x1, Pallas kernels, relay(): pl.pallas_call(relay_kernel, name='relay', out_shape=[jax.ShapeDtypeStruc...  2.13 us
  transfers between devices with their start and end apart: 7, of which 1 were waited for; matrix products, arithmetic and copies ran while one was open for 1% of the time, Pallas kernels for 43%

profile of v9, /device:TPU:0, one launch (start us, length us, event | category | flops | bytes accessed | tf_op | source)
XLA Modules:
  0.0 92.1 jit_solution(8698988462546864344)
XLA Ops:
  6.5 0.0 copy-start.15
  6.5 0.0 copy-start.16
  6.5 0.0 copy-start.7
  6.5 0.0 copy-start.8
  6.5 0.0 all-gather.2.cloned.1.call-start
  6.6 0.7 all-gather.2.cloned.1.call-update
  7.3 0.1 pad_maximum_fusion.1.centre_ref
  7.4 0.0 copy-start
  7.4 0.9 %copy-done = bf16[16,8192]{1,0:T(8,128)(2,1)S(1)} copy-done((bf16[16,8192]{1,0:T(8,128)(2,1)S(1)}, bf16[16,8192]{1,0:T(8,128)(2,1)}, u32[]{:S(2)}) %copy-start) | copy-done | bytes 262168
  8.3 0.0 copy-start.6
  8.3 0.9 copy-done.6
  9.2 1.6 %pack.1 = (bf16[32,8192]{1,0:T(8,128)(2,1)S(1)}, bf16[32,8192]{1,0:T(8,128)(2,1)}, bf16[32,8192]{1,0:T(8,128)(2,1)S(1)}, bf16[16,8192]{1,0:T(8,128)(2,1)S(1)}) custom-call(f32[3]{0:T(128)S(1)} %pad_maximum_fusion.1.centre_ref, bf16[16,8192]{1,0:T(8,128)(2,1)S(1)} %copy-done, f32[3,8192]{1,0:T(4,128)S(1)} %copy-done.6), custom_call_target="tpu_custom_call" | custom-call | flops 1000 | bytes 100000 | tf_op jit(solution)/shard_map/pack/pallas_call | solution.py:86
  10.9 0.0 copy-start.9
  10.9 0.8 copy-done.9
  11.7 0.0 copy-start.13
  11.7 0.7 copy-done.13
  12.4 5.7 %collective-permute-start.4 = (bf16[32,8192]{1,0:T(8,128)(2,1)}, bf16[32,8192]{1,0:T(8,128)(2,1)}, u32[]{:S(2)}, u32[]{:S(2)}) collective-permute-start(bf16[32,8192]{1,0:T(8,128)(2,1)} %get-tuple-element.33), channel_id=1, source_target_pairs={{0,4},{4,8},{8,12},{12,16},{16,20},{20,24},{24,28},{1,5},{5,9},{9,... | collective-permute-start | bytes 1572872 | tf_op jit(solution)/shard_map/ppermute | solution.py:563
  18.0 0.0 copy-start.1
  18.0 1.4 %collective-permute-start.2 = (bf16[32,8192]{1,0:T(8,128)(2,1)S(1)}, bf16[32,8192]{1,0:T(8,128)(2,1)}, u32[]{:S(2)}, u32[]{:S(2)}) collective-permute-start(bf16[32,8192]{1,0:T(8,128)(2,1)S(1)} %get-tuple-element.28), channel_id=1, source_target_pairs={{4,0},{8,4},{12,8},{16,12},{20,16},{24,20},{28,24},{5,1},{9,5},{13... | collective-permute-start | bytes 1572872 | tf_op jit(solution)/shard_map/ppermute | solution.py:564
  19.5 0.0 copy-start.2
  19.5 1.2 %copy-done.2 = bf16[127,4096]{1,0:T(8,128)(2,1)S(1)} copy-done((bf16[127,4096]{1,0:T(8,128)(2,1)S(1)}, bf16[127,4096]{1,0:T(8,128)(2,1)}, u32[]{:S(2)}) %copy-start.2) | copy-done | bytes 1040408
  20.7 0.0 copy-start.5
  20.7 0.9 %copy-done.5 = bf16[24,4096]{1,0:T(8,128)(2,1)S(1)} copy-done((bf16[24,4096]{1,0:T(8,128)(2,1)S(1)}, bf16[24,4096]{1,0:T(8,128)(2,1)}, u32[]{:S(2)}) %copy-start.5) | copy-done | bytes 196632
  21.6 2.1 %relay.1 = (bf16[64,64,128]{2,1,0:T(8,128)(2,1)S(1)}, bf16[24,64,64]{2,1,0:T(8,128)(2,1)S(1)}) custom-call(bf16[127,4096]{1,0:T(8,128)(2,1)S(1)} %copy-done.2, bf16[24,4096]{1,0:T(8,128)(2,1)S(1)} %copy-done.5), custom_call_target="tpu_custom_call" | custom-call | flops 1000 | bytes 100000 | tf_op jit(solution)/shard_map/relay/pallas_call | solution.py:232
  23.8 0.0 copy-start.11
  23.8 0.7 copy-done.11
  24.5 0.0 copy-done.15
  24.5 0.1 copy.16.far_src_ref
  24.6 0.0 copy-done.16
  24.6 0.1 copy.17.far_cls_ref
  24.7 0.0 copy-done.7
  24.7 0.0 copy-done.8
  24.7 2.8 %class_counts.1.a_ref = bf16[24,128,256]{2,1,0:T(8,128)(2,1)S(1)} custom-call(s32[1]{0:T(128)} %bitcast.place_ref, s32[127,24]{1,0:T(8,128)S(1)} %copy.16.far_src_ref, s32[127,24]{1,0:T(8,128)S(1)} %copy.17.far_cls_ref, s32[12,24]{1,0:T(8,128)S(1)} %copy-done.7, s32[12,24]{1,0:T(8,128)S(1)} %copy-done.8), custom_call_target="tpu_custom_call" | custom-call | flops 1000 | bytes 100000 | tf_op jit(solution)/shard_map/class_counts/pallas_call | solution.py:324
  27.5 0.8 copy.20.near_ref
  28.3 0.1 all-gather.2.cloned.1.call-done
  28.4 0.0 copy-done.1
  28.4 0.0 copy-start.3
  28.4 1.2 %copy-done.3 = bf16[64,64,128]{2,1,0:T(8,128)(2,1)S(1)} copy-done((bf16[64,64,128]{2,1,0:T(8,128)(2,1)S(1)}, bf16[64,64,128]{2,1,0:T(8,128)(2,1)}, u32[]{:S(2)}) %copy-start.3) | copy-done | bytes 1048600
  29.7 0.0 copy-start.10
  29.7 0.0 copy-start.14
  29.7 2.0 %upward.1 = (bf16[16,64,128]{2,1,0:T(8,128)(2,1)S(1)}, bf16[17,32,128]{2,1,0:T(8,128)(2,1)S(1)}, bf16[17,32,128]{2,1,0:T(8,128)(2,1)S(1)}, bf16[16,128]{1,0:T(8,128)(2,1)S(1)}) custom-call(bf16[16,8192]{1,0:T(8,128)(2,1)S(1)} %copy-done.1, bf16[32,128,128]{2,1,0:T(8,128)(2,1)S(1)} %bitcast.4, bf16[64,64,128]{2,1,0:T(8,128)(2,1)S(1)} %get-tuple-element.21.links_ref), custom_call_target="tpu_custom_call" | custom-call | flops 300000000 | bytes 3000000 | tf_op jit(solution)/shard_map/upward/pallas_call | solution.py:389
  31.7 4.5 %collective-permute-start = (bf16[17,32,128]{2,1,0:T(8,128)(2,1)S(1)}, bf16[17,32,128]{2,1,0:T(8,128)(2,1)S(1)}, u32[]{:S(2)}, u32[]{:S(2)}) collective-permute-start(bf16[17,32,128]{2,1,0:T(8,128)(2,1)S(1)} %get-tuple-element.22), channel_id=1, source_target_pairs={{0,4},{4,8},{8,12},{12,16},{16,20},{20,24},{24,28},{1,5},{5,9},{9,... | collective-permute-start | bytes 417800 | tf_op jit(solution)/shard_map/ppermute | solution.py:569
  36.2 1.5 %collective-permute-start.1 = (bf16[17,32,128]{2,1,0:T(8,128)(2,1)S(1)}, bf16[17,32,128]{2,1,0:T(8,128)(2,1)S(1)}, u32[]{:S(2)}, u32[]{:S(2)}) collective-permute-start(bf16[17,32,128]{2,1,0:T(8,128)(2,1)S(1)} %get-tuple-element.26), channel_id=1, source_target_pairs={{4,0},{8,4},{12,8},{16,12},{20,16},{24,20},{28,24},{5,1},{9,5},{13... | collective-permute-start | bytes 417800 | tf_op jit(solution)/shard_map/ppermute | solution.py:570
  37.7 0.0 copy-done.10
  37.7 0.0 copy-done.14
  37.7 10.3 %near_own.1.rest_0_ = f32[16,8192]{1,0:T(8,128)S(1)} custom-call(s32[64,27]{1,0:T(8,128)S(1)} %copy.20.near_ref, bf16[32,8192]{1,0:T(8,128)(2,1)S(1)} %copy-done.10, bf16[16,8192]{1,0:T(8,128)(2,1)S(1)} %copy-done.14), custom_call_target="tpu_custom_call" | custom-call | flops 7000000000 | bytes 2000000 | tf_op jit(solution)/shard_map/near_own/pallas_call | solution.py:187
  48.0 0.0 collective-permute-done.low_ref
  48.0 0.0 collective-permute-done.1.high_ref
  48.0 3.8 %collective-permute-start.3 = (bf16[2,16,128]{2,1,0:T(8,128)(2,1)S(1)}, bf16[2,16,128]{2,1,0:T(8,128)(2,1)S(1)}, u32[]{:S(2)}, u32[]{:S(2)}) collective-permute-start(bf16[2,16,128]{2,1,0:T(8,128)(2,1)S(1)} %maximum_select_fusion.rest_0_), channel_id=1, source_target_pairs={{0,8},{4,12},{8,0},{12,4},{16,24},{20,28},{24,16},{28,20},{1,9},{5... | collective-permute-start | bytes 24584 | tf_op jit(solution)/shard_map/ppermute | solution.py:583
  51.8 0.0 collective-permute-done.4.src_ref
  51.8 10.3 %near_low.1.rest_0_ = f32[16,8192]{1,0:T(8,128)S(1)} custom-call(s32[64,27]{1,0:T(8,128)S(1)} %copy.20.near_ref, bf16[32,8192]{1,0:T(8,128)(2,1)} %collective-permute-done.4.src_ref, bf16[16,8192]{1,0:T(8,128)(2,1)S(1)} %copy-done.14, f32[16,8192]{1,0:T(8,128)S(1)} %near_own.1.rest_0_), custom_call_target="tpu_custom_call" | custom-call | flops 7000000000 | bytes 2000000 | tf_op jit(solution)/shard_map/near_low/pallas_call | solution.py:187
  62.1 0.0 collective-permute-done.3.rest_1_
  62.1 0.0 copy-start.4
  62.1 0.0 copy-start.12
  62.1 2.7 %collective-permute-start.5 = (bf16[4,16,128]{2,1,0:T(8,128)(2,1)S(1)}, bf16[4,16,128]{2,1,0:T(8,128)(2,1)S(1)}, u32[]{:S(2)}, u32[]{:S(2)}) collective-permute-start(bf16[4,16,128]{2,1,0:T(8,128)(2,1)S(1)} %pad_maximum_fusion), channel_id=1, source_target_pairs={{0,16},{4,20},{8,24},{12,28},{16,0},{20,4},{24,8},{28,12},{1,17},{... | collective-permute-start | bytes 49160 | tf_op jit(solution)/shard_map/ppermute | solution.py:583
  64.8 0.0 collective-permute-done.2.src_ref
  64.8 10.3 %near_high.1.near_ref = f32[16,8192]{1,0:T(8,128)S(1)} custom-call(s32[64,27]{1,0:T(8,128)S(1)} %copy.20.near_ref, bf16[32,8192]{1,0:T(8,128)(2,1)} %collective-permute-done.2.src_ref, bf16[16,8192]{1,0:T(8,128)(2,1)S(1)} %copy-done.14, f32[16,8192]{1,0:T(8,128)S(1)} %near_low.1.rest_0_), custom_call_target="tpu_custom_call" | custom-call | flops 7000000000 | bytes 2000000 | tf_op jit(solution)/shard_map/near_high/pallas_call | solution.py:187
  75.1 0.0 collective-permute-done.5.rest_2_
  75.1 0.0 copy-done.4
  75.1 0.0 copy-done.12
  75.1 10.1 %downward.1 = bf16[16,8192]{1,0:T(8,128)(2,1)} custom-call(s32[1]{0:T(128)} %bitcast.place_ref, bf16[17,32,128]{2,1,0:T(8,128)(2,1)S(1)} %collective-permute-done.low_ref, bf16[16,64,128]{2,1,0:T(8,128)(2,1)S(1)} %get-tuple-element.25.own_ref, bf16[17,32,128]{2,1,0:T(8,128)(2,1)S(1)} %collective-permute-done.1.high_ref, ...), custom_call_target="tpu_custom_call" | custom-call | flops 4000000000 | bytes 6000000 | tf_op jit(solution)/shard_map/downward/pallas_call | solution.py:525
  (3 shorter events, 0.0 us)
Async XLA Ops:
  6.5 18.0 %copy-start.15 = (s32[127,24]{0,1:T(8,128)S(1)}, s32[127,24]{0,1:T(8,128)}, u32[]{:S(2)}) copy-start(s32[127,24]{0,1:T(8,128)} %param.16) | copy-start | bytes 36580
  6.5 18.1 %copy-start.16 = (s32[127,24]{0,1:T(8,128)S(1)}, s32[127,24]{0,1:T(8,128)}, u32[]{:S(2)}) copy-start(s32[127,24]{0,1:T(8,128)} %param.17) | copy-start | bytes 36580
  6.5 18.2 %copy-start.7 = (s32[12,24]{1,0:T(8,128)S(1)}, s32[12,24]{1,0:T(8,128)}, u32[]{:S(2)}) copy-start(s32[12,24]{1,0:T(8,128)} %top_src_ref.1) | copy-start | bytes 3460
  6.5 18.2 %copy-start.8 = (s32[12,24]{1,0:T(8,128)S(1)}, s32[12,24]{1,0:T(8,128)}, u32[]{:S(2)}) copy-start(s32[12,24]{1,0:T(8,128)} %top_cls_ref.1) | copy-start | bytes 3460
  6.5 21.9 %all-gather.2.cloned.1.call-start = ((), (), s32[]{:S(2)}) async-start(), calls=%async_computation | async-start | bytes 1310720 | tf_op jit(solution)/shard_map/all_gather | solution.py:553
  7.4 1.0 %copy-start = (bf16[16,8192]{1,0:T(8,128)(2,1)S(1)}, bf16[16,8192]{1,0:T(8,128)(2,1)}, u32[]{:S(2)}) copy-start(bf16[16,8192]{1,0:T(8,128)(2,1)} %values_ref.3) | copy-start | bytes 786436
  8.3 0.9 copy-start.6
  10.9 0.8 copy-start.9
  11.7 0.7 copy-start.13
  12.4 39.4 %collective-permute-start.4 = (bf16[32,8192]{1,0:T(8,128)(2,1)}, bf16[32,8192]{1,0:T(8,128)(2,1)}, u32[]{:S(2)}, u32[]{:S(2)}) collective-permute-start(bf16[32,8192]{1,0:T(8,128)(2,1)} %get-tuple-element.33), channel_id=1, source_target_pairs={{0,4},{4,8},{8,12},{12,16},{16,20},{20,24},{24,28},{1,5},{5,9},{9,... | collective-permute-start | bytes 1572872 | tf_op jit(solution)/shard_map/ppermute | solution.py:563
  18.0 10.4 %copy-start.1 = (bf16[16,8192]{1,0:T(8,128)(2,1)S(1)}, bf16[16,8192]{1,0:T(8,128)(2,1)}, u32[]{:S(2)}) copy-start(bf16[16,8192]{1,0:T(8,128)(2,1)} %values_ref.3) | copy-start | bytes 786436
  18.0 46.7 %collective-permute-start.2 = (bf16[32,8192]{1,0:T(8,128)(2,1)S(1)}, bf16[32,8192]{1,0:T(8,128)(2,1)}, u32[]{:S(2)}, u32[]{:S(2)}) collective-permute-start(bf16[32,8192]{1,0:T(8,128)(2,1)S(1)} %get-tuple-element.28), channel_id=1, source_target_pairs={{4,0},{8,4},{12,8},{16,12},{20,16},{24,20},{28,24},{5,1},{9,5},{13... | collective-permute-start | bytes 1572872 | tf_op jit(solution)/shard_map/ppermute | solution.py:564
  19.5 1.2 %copy-start.2 = (bf16[127,4096]{1,0:T(8,128)(2,1)S(1)}, bf16[127,4096]{1,0:T(8,128)(2,1)}, u32[]{:S(2)}) copy-start(bf16[127,4096]{1,0:T(8,128)(2,1)} %transfer_ref.1) | copy-start | bytes 3121156
  20.7 0.9 %copy-start.5 = (bf16[24,4096]{1,0:T(8,128)(2,1)S(1)}, bf16[24,4096]{1,0:T(8,128)(2,1)}, u32[]{:S(2)}) copy-start(bf16[24,4096]{1,0:T(8,128)(2,1)} %coupling_ref.1) | copy-start | bytes 589828
  23.8 0.7 copy-start.11
  28.4 1.2 %copy-start.3 = (bf16[64,64,128]{2,1,0:T(8,128)(2,1)S(1)}, bf16[64,64,128]{2,1,0:T(8,128)(2,1)}, u32[]{:S(2)}) copy-start(bf16[64,64,128]{2,1,0:T(8,128)(2,1)} %all-gather.2.cloned.1.call-done) | copy-start | bytes 3145732
  29.7 8.0 %copy-start.10 = (bf16[32,8192]{1,0:T(8,128)(2,1)S(1)}, bf16[32,8192]{1,0:T(8,128)(2,1)}, u32[]{:S(2)}) copy-start(bf16[32,8192]{1,0:T(8,128)(2,1)} %copy-done.9) | copy-start | bytes 1572868
  29.7 8.0 %copy-start.14 = (bf16[16,8192]{1,0:T(8,128)(2,1)S(1)}, bf16[16,8192]{1,0:T(8,128)(2,1)}, u32[]{:S(2)}) copy-start(bf16[16,8192]{1,0:T(8,128)(2,1)} %copy-done.13) | copy-start | bytes 786436
  31.7 16.3 %collective-permute-start = (bf16[17,32,128]{2,1,0:T(8,128)(2,1)S(1)}, bf16[17,32,128]{2,1,0:T(8,128)(2,1)S(1)}, u32[]{:S(2)}, u32[]{:S(2)}) collective-permute-start(bf16[17,32,128]{2,1,0:T(8,128)(2,1)S(1)} %get-tuple-element.22), channel_id=1, source_target_pairs={{0,4},{4,8},{8,12},{12,16},{16,20},{20,24},{24,28},{1,5},{5,9},{9,... | collective-permute-start | bytes 417800 | tf_op jit(solution)/shard_map/ppermute | solution.py:569
  36.2 11.8 %collective-permute-start.1 = (bf16[17,32,128]{2,1,0:T(8,128)(2,1)S(1)}, bf16[17,32,128]{2,1,0:T(8,128)(2,1)S(1)}, u32[]{:S(2)}, u32[]{:S(2)}) collective-permute-start(bf16[17,32,128]{2,1,0:T(8,128)(2,1)S(1)} %get-tuple-element.26), channel_id=1, source_target_pairs={{4,0},{8,4},{12,8},{16,12},{20,16},{24,20},{28,24},{5,1},{9,5},{13... | collective-permute-start | bytes 417800 | tf_op jit(solution)/shard_map/ppermute | solution.py:570
  48.0 14.1 %collective-permute-start.3 = (bf16[2,16,128]{2,1,0:T(8,128)(2,1)S(1)}, bf16[2,16,128]{2,1,0:T(8,128)(2,1)S(1)}, u32[]{:S(2)}, u32[]{:S(2)}) collective-permute-start(bf16[2,16,128]{2,1,0:T(8,128)(2,1)S(1)} %maximum_select_fusion.rest_0_), channel_id=1, source_target_pairs={{0,8},{4,12},{8,0},{12,4},{16,24},{20,28},{24,16},{28,20},{1,9},{5... | collective-permute-start | bytes 24584 | tf_op jit(solution)/shard_map/ppermute | solution.py:583
  62.1 13.0 %copy-start.4 = (bf16[64,64,128]{2,1,0:T(8,128)(2,1)S(1)}, bf16[64,64,128]{2,1,0:T(8,128)(2,1)}, u32[]{:S(2)}) copy-start(bf16[64,64,128]{2,1,0:T(8,128)(2,1)} %all-gather.2.cloned.1.call-done) | copy-start | bytes 3145732
  62.1 13.0 %copy-start.12 = (bf16[24,64,64]{2,1,0:T(8,128)(2,1)S(1)}, bf16[24,64,64]{2,1,0:T(8,128)(2,1)}, u32[]{:S(2)}) copy-start(bf16[24,64,64]{2,1,0:T(8,128)(2,1)} %copy-done.11) | copy-start | bytes 589828
  62.1 12.9 %collective-permute-start.5 = (bf16[4,16,128]{2,1,0:T(8,128)(2,1)S(1)}, bf16[4,16,128]{2,1,0:T(8,128)(2,1)S(1)}, u32[]{:S(2)}, u32[]{:S(2)}) collective-permute-start(bf16[4,16,128]{2,1,0:T(8,128)(2,1)S(1)} %pad_maximum_fusion), channel_id=1, source_target_pairs={{0,16},{4,20},{8,24},{12,28},{16,0},{20,4},{24,8},{28,12},{1,17},{... | collective-permute-start | bytes 49160 | tf_op jit(solution)/shard_map/ppermute | solution.py:583
Sparse Core Ops, SparseCore 0:
  8.9 19.4 all-gather.1
